TPU v7x, 32 devices: a whole 2x2x4 slice. The times are simulated.
32 devices in a mesh: grp: 1, gx: 16 (over z, y, x), gz: 2 (over core).
Axes of the slice: x: 2, y: 2, z: 4, core: 2. Of those that a mesh axis runs over, the one named last changes fastest.
Arguments:
- field: bfloat16 [20, 32, 32, 2048], P(None, ('grp', 'gx'), 'gz'), may hold values from -6 to 6
- cotangent: bfloat16 [20, 32, 32, 2048], P(None, ('grp', 'gx'), 'gz'), may hold values from -6 to 6
- spec_weight: bfloat16 [2, 20, 20, 192, 384], P(None, None, None, 'gx', 'gz'), may hold values from -9 to 9
- mix_weight: bfloat16 [20, 20], replicated, may hold values from -1.25 to 1.25
Outputs:
- field_grad: bfloat16 [20, 32, 32, 2048], P(None, ('grp', 'gx'), 'gz')
- spec_grad: float32 [2, 20, 20, 192, 384], P('grp', None, None, 'gx', 'gz')
- mix_grad: float32 [20, 20], P('grp')
All inputs are finite; a program needn't handle non-finite values.
Results may differ from a plain program's by a relative error of at most 0.018.
Values may be sent and summed in bfloat16 or wider, within the bound.
No kernel may reach another device: no remote copies, remote signals or barrier semaphores. Data moves between devices by JAX's collectives and lax.ppermute only.
A program may use at most 128 MiB of HBM per device.

v0:
```python
import functools
import math

import jax
import jax.numpy as jnp
import ml_dtypes
import numpy as np
from jax import lax
from jax.experimental import pallas as pl
from jax.experimental.pallas import tpu as pltpu
from jax.sharding import PartitionSpec as P

MX = 24
MY = 24
MZ = 16
MT = 8
NY = 128
NSTEP = 16
LANES = 128
MIX_ROWS = 4
BF = jnp.bfloat16
F32 = jnp.float32
VMEM_LIMIT = 40 * 1024 * 1024


def mode_angles(length, count, one_sided):
    cells = np.arange(length)
    ranks = np.arange(count)
    freqs = ranks if one_sided else np.where(ranks < count // 2, ranks, ranks - count)
    wrapped = np.mod(cells[:, None] * freqs[None, :], length)
    return wrapped.astype(np.float32) * np.float32(2.0 * math.pi / length)


def rounded(values):
    return np.asarray(values).astype(np.float32).astype(ml_dtypes.bfloat16).astype(np.float32)


def pair_table(angles, conjugate):
    cosine = rounded(np.cos(angles.astype(np.float64)))
    sine = rounded(np.sin(angles.astype(np.float64)))
    if conjugate:
        rows = [np.stack([cosine, sine], -1), np.stack([-sine, cosine], -1)]
    else:
        rows = [np.stack([cosine, -sine], -1), np.stack([sine, cosine], -1)]
    return np.stack(rows, 1)


def plane_rows():
    y_angle = mode_angles(NY, MY, False)
    t_angle = mode_angles(NSTEP, MT, True)
    total = (y_angle.T[:, None, :, None] + t_angle.T[None, :, None, :]).astype(np.float32)
    total = total.reshape(MY * MT, NY * NSTEP).astype(np.float64)
    return np.concatenate([np.cos(total), -np.sin(total)], 0)


class Plan:
    def __init__(self, field_shape, weight_shape, x_parts, z_parts):
        self.chans, self.xl, self.zl, self.plane = field_shape
        self.xp, self.zp = x_parts, z_parts
        self.x_len, self.z_len = self.xl * x_parts, self.zl * z_parts
        self.half = self.chans // 2
        self.s = weight_shape[3]
        self.modes = weight_shape[4]
        self.kxl = self.modes // MZ
        self.ms = self.s * x_parts
        self.xz = self.xl * self.zl
        self.rows = self.half * self.xz
        self.rows_pad = -(-self.rows // LANES) * LANES
        self.group = LANES // self.xz
        self.pairs = self.rows_pad // LANES
        self.width = self.xl * 2 * MZ
        self.blocks = self.half // 2
        self.used = self.blocks * self.s
        self.chunk = -(-(self.used + MIX_ROWS) // 16) * 16
        self.count = self.x_len * self.z_len * self.plane
        self.scale = 1.0 / self.count
        assert z_parts == 2 and 2 * self.width == LANES and self.group * self.xz == LANES
        assert self.zl == MZ

    def tables(self):
        bf = lambda t: np.ascontiguousarray(t).astype(ml_dtypes.bfloat16)
        g = self.group * self.xl
        eye = np.eye(g, dtype=np.float32)
        zf = pair_table(mode_angles(self.z_len, MZ, False), False)
        zf = zf.reshape(2, self.zl, 2, MZ, 2)
        zf = np.einsum("hzplq,ab->hpazbql", zf, eye).reshape(2, 2 * LANES, 2 * LANES)
        z_forward = np.stack([np.concatenate([zf[0], zf[1]], 0), np.concatenate([zf[1], zf[0]], 0)])
        zi = pair_table(mode_angles(self.z_len, MZ, False), True)
        zi = zi.reshape(2, self.zl, 2, MZ, 2)
        zi = np.einsum("hzplq,ab->hqazbpl", zi, eye).reshape(2, 2 * LANES, 2 * LANES)
        z_inverse = np.stack([np.concatenate([zi[1], zi[0]], 0), np.concatenate([zi[0], zi[1]], 0)])
        eye = np.eye(MZ, dtype=np.float32)
        xf = pair_table(mode_angles(self.x_len, MX, False), False)
        xf = xf.reshape(self.x_len, 2, 2, self.kxl, 2)
        x_forward = np.einsum("xpjkr,ab->jrxpakb", xf, eye)
        x_forward = x_forward.reshape(2, 2, self.xp * self.width, self.modes)
        xi = pair_table(mode_angles(self.x_len, MX, False), True)
        xi = xi.reshape(self.x_len, 2, 2, self.kxl, 2)
        x_inverse = np.einsum("xrjkq,ab->jrkaxqb", xi, eye)
        x_inverse = x_inverse.reshape(2, 2, self.modes, self.xp * self.width)
        owner = np.repeat(np.eye(self.chans, dtype=np.float32), self.xz, axis=0)
        return dict(
            plane=bf(plane_rows()),
            z_forward=bf(z_forward),
            z_inverse=bf(z_inverse),
            x_forward=bf(x_forward),
            x_inverse=bf(x_inverse),
            owner=bf(owner),
        )


def params(**kw):
    return pltpu.CompilerParams(vmem_limit_bytes=VMEM_LIMIT, **kw)


def cost(flops, nbytes):
    return pl.CostEstimate(flops=int(flops), bytes_accessed=int(nbytes), transcendentals=0)


def shape(dims, kind=BF):
    return jax.ShapeDtypeStruct(tuple(dims), kind)


def full(dims):
    return pl.BlockSpec(tuple(dims), lambda *_: (0,) * len(dims))


def dot(a, b):
    return lax.dot_general(a, b, (((1,), (0,)), ((), ())), preferred_element_type=F32)


def dot_t(a, b):
    return lax.dot_general(a, b, (((1,), (1,)), ((), ())), preferred_element_type=F32)


def plane_forward(plan, which, field, plane):
    tiles = 4
    width = plan.plane // tiles

    def kernel(_, field_ref, plane_ref, out_ref, acc_ref):
        step = pl.program_id(0)
        value = dot_t(plane_ref[...], field_ref[0])

        @pl.when(step == 0)
        def _():
            acc_ref[...] = value

        @pl.when(step > 0)
        def _():
            acc_ref[...] += value

        @pl.when(step == tiles - 1)
        def _():
            if plan.rows_pad > plan.rows:
                pad = plan.rows_pad - plan.rows
                out_ref[:, plan.rows :] = jnp.zeros((2 * plan.ms, pad), BF)
            out_ref[:, : plan.rows] = acc_ref[...].astype(BF)

    return pl.pallas_call(
        kernel,
        grid_spec=pltpu.PrefetchScalarGridSpec(
            num_scalar_prefetch=1,
            grid=(tiles,),
            in_specs=[
                pl.BlockSpec((1, plan.rows, width), lambda t, h: (h[0], 0, t)),
                pl.BlockSpec((2 * plan.ms, width), lambda t, h: (0, t)),
            ],
            out_specs=full((2 * plan.ms, plan.rows_pad)),
            scratch_shapes=[pltpu.VMEM((2 * plan.ms, plan.rows), F32)],
        ),
        out_shape=shape((2 * plan.ms, plan.rows_pad)),
        compiler_params=params(),
        cost_estimate=cost(4 * plan.ms * plan.rows * plan.plane, 3.2e6),
        name="plane_forward",
    )(which, field.reshape(2, plan.rows, plan.plane), plane)


def z_forward(plan, me, own, got, table):
    def kernel(_, own_ref, got_ref, table_ref, out_ref, lines, pieces):
        ms = plan.ms
        for g in range(plan.pairs):
            at = slice(g * LANES, (g + 1) * LANES)
            parts = [own_ref[:ms, at], own_ref[ms:, at], got_ref[:ms, at], got_ref[ms:, at]]
            value = dot(jnp.concatenate(parts, 1), table_ref[0])
            for b in (0, 1):
                if 2 * g + b < plan.blocks:
                    lines[2 * g + b] = value[:, b * LANES : (b + 1) * LANES]
        pad = plan.chunk - plan.used
        for i in range(plan.xp):
            for b in range(plan.blocks):
                pieces[i, b * plan.s : (b + 1) * plan.s, :] = lines[b, i * plan.s : (i + 1) * plan.s, :]
            pieces[i, plan.used :, :] = jnp.zeros((pad, LANES), F32)
            out_ref[i] = pieces[i].astype(BF)

    side = (2 * plan.ms, plan.rows_pad)
    return pl.pallas_call(
        kernel,
        grid_spec=pltpu.PrefetchScalarGridSpec(
            num_scalar_prefetch=1,
            grid=(1,),
            in_specs=[
                full(side),
                full(side),
                pl.BlockSpec((1, 4 * LANES, 2 * LANES), lambda t, j: (j[0], 0, 0)),
            ],
            out_specs=full((plan.xp, plan.chunk, LANES)),
            scratch_shapes=[
                pltpu.VMEM((plan.blocks, plan.ms, LANES), F32),
                pltpu.VMEM((plan.xp, plan.chunk, LANES), F32),
            ],
        ),
        out_shape=shape((plan.xp, plan.chunk, LANES)),
        compiler_params=params(),
        cost_estimate=cost(3e8, 1e6),
        name="z_forward",
    )(me, own, got, table)


def x_forward(plan, me, chunks, table):
    def kernel(me_ref, in_ref, table_ref, send_ref, keep_ref, lhs, lines):
        w = plan.width
        for i in range(0, plan.xp, 2):
            first, second = in_ref[i], in_ref[i + 1]
            at = slice(i * w, (i + 2) * w)
            lhs[: plan.chunk, at] = jnp.concatenate([first[:, :w], second[:, :w]], 1)
            lhs[plan.chunk :, at] = jnp.concatenate([first[:, w:], second[:, w:]], 1)
        me = me_ref[0]
        for slot, half, out_ref in ((0, 1 - me, send_ref), (1, me, keep_ref)):
            for r in (0, 1):
                lines[slot, r] = dot(lhs[...], table_ref[half, r])
                for c in range(plan.half):
                    start = (c % 2) * plan.chunk + (c // 2) * plan.s
                    out_ref[c, r] = lines[slot, r, start : start + plan.s, :].astype(BF)

    out = (plan.half, 2, plan.s, plan.modes)
    return pl.pallas_call(
        kernel,
        grid_spec=pltpu.PrefetchScalarGridSpec(
            num_scalar_prefetch=1,
            grid=(1,),
            in_specs=[full((plan.xp, plan.chunk, LANES)), full(table.shape)],
            out_specs=[full(out), full(out)],
            scratch_shapes=[
                pltpu.VMEM((2 * plan.chunk, plan.xp * plan.width), BF),
                pltpu.VMEM((2, 2, 2 * plan.chunk, plan.modes), F32),
            ],
        ),
        out_shape=[shape(out), shape(out)],
        compiler_params=params(),
        cost_estimate=cost(3e8, 3e6),
        name="x_forward",
    )(me, chunks, table)


def mode_product(plan, me, which, weight, own, got, adjoint):
    block = 2
    steps = plan.half // block

    def kernel(me_ref, _, weight_ref, own_ref, got_ref, out_ref, held):
        me = me_ref[0]

        @pl.when(pl.program_id(0) == 0)
        def _():
            held[me] = own_ref[...].astype(F32)
            held[1 - me] = got_ref[...].astype(F32)

        for k in range(block):
            real = jnp.zeros((plan.s, plan.modes), F32)
            imag = jnp.zeros((plan.s, plan.modes), F32)
            for c in range(plan.chans):
                pos = (k, c) if adjoint else (c, k)
                wr = weight_ref[0, pos[0], pos[1]].astype(F32)
                wi = weight_ref[1, pos[0], pos[1]].astype(F32)
                mr = held[c // plan.half, c % plan.half, 0]
                mi = held[c // plan.half, c % plan.half, 1]
                if adjoint:
                    real += wr * mr + wi * mi
                    imag += wr * mi - wi * mr
                else:
                    real += wr * mr - wi * mi
                    imag += wr * mi + wi * mr
            out_ref[k, 0] = real.astype(BF)
            out_ref[k, 1] = imag.astype(BF)

    side = (plan.half, 2, plan.s, plan.modes)
    if adjoint:
        w_block = (2, block, plan.chans, plan.s, plan.modes)
        w_map = lambda t, j, h: (0, h[0] * steps + t, 0, 0, 0)
    else:
        w_block = (2, plan.chans, block, plan.s, plan.modes)
        w_map = lambda t, j, h: (0, 0, h[0] * steps + t, 0, 0)
    return pl.pallas_call(
        kernel,
        grid_spec=pltpu.PrefetchScalarGridSpec(
            num_scalar_prefetch=2,
            grid=(steps,),
            in_specs=[pl.BlockSpec(w_block, w_map), full(side), full(side)],
            out_specs=pl.BlockSpec((block, 2, plan.s, plan.modes), lambda t, j, h: (t, 0, 0, 0)),
            scratch_shapes=[pltpu.VMEM((2,) + side, F32)],
        ),
        out_shape=shape(side),
        compiler_params=params(),
        cost_estimate=cost(4e9, 4e6),
        name="mode_product",
    )(me, which, weight, own, got)


def x_inverse(plan, me, own, got, table, mix):
    carry = mix is not None

    def kernel(me_ref, own_ref, got_ref, table_ref, *rest):
        mix_ref = rest[0] if carry else None
        out_ref, lhs, spare = rest[1:] if carry else rest
        me = me_ref[0]
        pad = plan.chunk - plan.used
        for slot, in_ref in ((0, own_ref), (1, got_ref)):
            for r in (0, 1):
                for c in range(plan.half):
                    start = (c % 2) * plan.chunk + (c // 2) * plan.s
                    lhs[slot, r, start : start + plan.s, :] = in_ref[c, r].astype(F32)
                for c in (0, 1):
                    start = c * plan.chunk + plan.used
                    lhs[slot, r, start : start + pad, :] = jnp.zeros((pad, plan.modes), F32)
        value = None
        for slot, half in ((0, me), (1, 1 - me)):
            for r in (0, 1):
                term = dot(lhs[slot, r].astype(BF), table_ref[half, r])
                value = term if value is None else value + term
        w = plan.width
        if carry:
            spare[...] = jnp.zeros((plan.chunk, LANES), F32)
            spare[plan.used : plan.used + MIX_ROWS, :] = mix_ref[...]
        for i in range(plan.xp):
            first = value[: plan.chunk, i * w : (i + 1) * w]
            second = value[plan.chunk :, i * w : (i + 1) * w]
            piece = jnp.concatenate([first, second], 1)
            if carry:
                piece = piece + spare[...]
            out_ref[i] = piece.astype(BF)

    side = (plan.half, 2, plan.s, plan.modes)
    extra = [full((MIX_ROWS, LANES))] if carry else []
    return pl.pallas_call(
        kernel,
        grid_spec=pltpu.PrefetchScalarGridSpec(
            num_scalar_prefetch=1,
            grid=(1,),
            in_specs=[full(side), full(side), full(table.shape)] + extra,
            out_specs=full((plan.xp, plan.chunk, LANES)),
            scratch_shapes=[
                pltpu.VMEM((2, 2, 2 * plan.chunk, plan.modes), F32),
                pltpu.VMEM((plan.chunk, LANES), F32),
            ],
        ),
        out_shape=shape((plan.xp, plan.chunk, LANES)),
        compiler_params=params(),
        cost_estimate=cost(3e8, 3e6),
        name="x_inverse",
    )(me, own, got, table, *([mix] if carry else []))


def z_inverse(plan, me, chunks, table, carry):
    def kernel(_, in_ref, table_ref, send_ref, keep_ref, *rest):
        mix_ref = rest[0] if carry else None
        lines, pieces = rest[-2:]
        s, ms = plan.s, plan.ms
        for i in range(plan.xp):
            pieces[i] = in_ref[i].astype(F32)
            for b in range(plan.blocks):
                lines[b, i * s : (i + 1) * s, :] = pieces[i, b * s : (b + 1) * s, :]
        for g in range(plan.pairs):
            first = lines[2 * g].astype(BF)
            if 2 * g + 1 < plan.blocks:
                second = lines[2 * g + 1].astype(BF)
            else:
                second = jnp.zeros((ms, LANES), BF)
            value = dot_t(table_ref[0], jnp.concatenate([first, second], 1))
            rows = min(LANES, plan.rows - g * LANES)
            for slot, out_ref in ((0, send_ref), (1, keep_ref)):
                for p in (0, 1):
                    start = (2 * slot + p) * LANES
                    out_ref[p, g * LANES : g * LANES + rows, :] = value[start : start + rows].astype(BF)
        if carry:
            total = pieces[0, plan.used : plan.used + MIX_ROWS, :]
            for i in range(1, plan.xp):
                total = total + pieces[i, plan.used : plan.used + MIX_ROWS, :]
            mix_ref[...] = total

    out = (2, plan.rows, plan.ms)
    outs = [out, out]
    out_shape = [shape(out), shape(out)]
    if carry:
        outs.append((MIX_ROWS, LANES))
        out_shape.append(shape((MIX_ROWS, LANES), F32))
    return pl.pallas_call(
        kernel,
        grid_spec=pltpu.PrefetchScalarGridSpec(
            num_scalar_prefetch=1,
            grid=(1,),
            in_specs=[
                full((plan.xp, plan.chunk, LANES)),
                pl.BlockSpec((1, 4 * LANES, 2 * LANES), lambda t, j: (j[0], 0, 0)),
            ],
            out_specs=[full(o) for o in outs],
            scratch_shapes=[
                pltpu.VMEM((plan.blocks, plan.ms, LANES), F32),
                pltpu.VMEM((plan.xp, plan.chunk, LANES), F32),
            ],
        ),
        out_shape=out_shape,
        compiler_params=params(),
        cost_estimate=cost(3e8, 1e6),
        name="z_inverse",
    )(me, chunks, table)


def mix_blocks(plan, mix, owner):
    cells = 2 * plan.rows

    def kernel(mix_ref, back_ref, owner_ref, owner_t_ref, out_ref):
        row = lax.broadcasted_iota(jnp.int32, (plan.rows, cells), 0) % plan.xz
        col = lax.broadcasted_iota(jnp.int32, (plan.rows, cells), 1) % plan.xz
        same = row == col
        for d, ref in ((0, mix_ref), (1, back_ref)):
            for h in (0, 1):
                spread = dot(owner_ref[h * plan.rows : (h + 1) * plan.rows, :], ref[...]).astype(BF)
                wide = dot(spread, owner_t_ref[...])
                out_ref[d, h] = jnp.where(same, wide, 0.0).astype(BF)

    return pl.pallas_call(
        kernel,
        out_shape=shape((2, 2, plan.rows, cells)),
        compiler_params=params(),
        cost_estimate=cost(4e7, 2e6),
        name="mix_blocks",
    )(mix.T, mix, owner, owner.T)


def gelu_slope(pre):
    size = jnp.abs(pre)
    bell = jnp.exp(pre * pre * -0.5)
    t = 1.0 / (1.0 + size * (0.3275911 / math.sqrt(2.0)))
    poly = 0.5 * 1.061405429
    for coef in (-1.453152027, 1.421413741, -0.284496736, 0.254829592):
        poly = poly * t + 0.5 * coef
    tail = poly * t * bell
    cdf = jnp.where(pre < 0.0, tail, 1.0 - tail)
    return cdf + pre * bell * (1.0 / math.sqrt(2.0 * math.pi))


def cells_forward(plan, me, own, got, plane, mixing, field, cotangent):
    tiles = 4
    width = plan.plane // tiles
    stripe = 32

    def kernel(me_ref, own_ref, got_ref, plane_ref, mix_ref, field_ref, cot_ref, grad_ref, send_ref, keep_ref, pre, acc):
        me = me_ref[0]
        step = pl.program_id(0)
        ms = plan.ms
        for slot, half, in_ref in ((0, me, own_ref), (1, 1 - me, got_ref)):
            spectral = dot(in_ref[0], plane_ref[:ms]) + dot(in_ref[1], plane_ref[ms:])
            mixed = dot(mix_ref[0, half], field_ref[...])
            pre[slot] = spectral * plan.scale + mixed
            for r in range(0, plan.rows, stripe):
                at = slice(r, r + stripe)
                slope = gelu_slope(pre[slot, at, :])
                grad_ref[half, at, :] = (cot_ref[half, at, :].astype(F32) * slope).astype(BF)
            value = dot_t(plane_ref[...], grad_ref[half])

            @pl.when(step == 0)
            def _():
                acc[slot] = value

            @pl.when(step > 0)
            def _():
                acc[slot] += value

        @pl.when(step == tiles - 1)
        def _():
            for slot, out_ref in ((0, keep_ref), (1, send_ref)):
                if plan.rows_pad > plan.rows:
                    pad = plan.rows_pad - plan.rows
                    out_ref[:, plan.rows :] = jnp.zeros((2 * ms, pad), BF)
                out_ref[:, : plan.rows] = acc[slot].astype(BF)

    side = (2, plan.rows, plan.ms)
    out = (2 * plan.ms, plan.rows_pad)
    cells = (2, plan.rows, plan.plane)
    tile = pl.BlockSpec((2, plan.rows, width), lambda t, j: (0, 0, t))
    return pl.pallas_call(
        kernel,
        grid_spec=pltpu.PrefetchScalarGridSpec(
            num_scalar_prefetch=1,
            grid=(tiles,),
            in_specs=[
                full(side),
                full(side),
                pl.BlockSpec((2 * plan.ms, width), lambda t, j: (0, t)),
                pl.BlockSpec((1, 2, plan.rows, 2 * plan.rows), lambda t, j: (0, 0, 0, 0)),
                pl.BlockSpec((2 * plan.rows, width), lambda t, j: (0, t)),
                tile,
            ],
            out_specs=[tile, full(out), full(out)],
            scratch_shapes=[
                pltpu.VMEM((2, plan.rows, width), F32),
                pltpu.VMEM((2, 2 * plan.ms, plan.rows), F32),
            ],
        ),
        out_shape=[shape(cells), shape(out), shape(out)],
        compiler_params=params(),
        cost_estimate=cost(6e9, 1e7),
        name="cells_forward",
    )(me, own, got, plane, mixing, field.reshape(2 * plan.rows, plan.plane), cotangent.reshape(cells))


def cells_back(plan, me, own, got, plane, mixing, grad):
    tiles = 4
    width = plan.plane // tiles

    def kernel(me_ref, own_ref, got_ref, plane_ref, mix_ref, grad_ref, out_ref):
        me = me_ref[0]
        ms = plan.ms
        for half, in_ref in ((me, own_ref), (1 - me, got_ref)):
            spectral = dot(in_ref[0], plane_ref[:ms]) + dot(in_ref[1], plane_ref[ms:])
            mixed = dot(mix_ref[0, half], grad_ref[...])
            out_ref[half] = (spectral * plan.scale + mixed).astype(BF)

    side = (2, plan.rows, plan.ms)
    cells = (2, plan.rows, plan.plane)
    return pl.pallas_call(
        kernel,
        grid_spec=pltpu.PrefetchScalarGridSpec(
            num_scalar_prefetch=1,
            grid=(tiles,),
            in_specs=[
                full(side),
                full(side),
                pl.BlockSpec((2 * plan.ms, width), lambda t, j: (0, t)),
                pl.BlockSpec((1, 2, plan.rows, 2 * plan.rows), lambda t, j: (1, 0, 0, 0)),
                pl.BlockSpec((2 * plan.rows, width), lambda t, j: (0, t)),
            ],
            out_specs=pl.BlockSpec((2, plan.rows, width), lambda t, j: (0, 0, t)),
        ),
        out_shape=shape(cells),
        compiler_params=params(),
        cost_estimate=cost(4e9, 8e6),
        name="cells_back",
    )(me, own, got, plane, mixing, grad.reshape(2 * plan.rows, plan.plane))


def pack_tables(plan):
    per_row = plan.chans // MIX_ROWS
    lane = LANES // per_row
    assert per_row * MIX_ROWS == plan.chans and lane >= plan.chans
    pick = np.zeros((per_row, MIX_ROWS, plan.chans), np.float32)
    place = np.zeros((per_row, 2 * plan.rows, LANES), np.float32)
    for k in range(per_row):
        for r in range(MIX_ROWS):
            pick[k, r, r * per_row + k] = 1.0
        for cell in range(2 * plan.rows):
            place[k, cell, k * lane + cell // plan.xz] = 1.0
    return pick, place.astype(ml_dtypes.bfloat16)


def mix_partial(plan, field, grad):
    tiles = 4
    width = plan.plane // tiles
    cells = 2 * plan.rows
    pick, place = pack_tables(plan)
    factor = 1.0 / math.sqrt(plan.count)

    def kernel(field_ref, grad_ref, pick_ref, place_ref, out_ref, acc):
        step = pl.program_id(0)
        value = dot_t(field_ref[...], grad_ref[...])

        @pl.when(step == 0)
        def _():
            acc[...] = value

        @pl.when(step > 0)
        def _():
            acc[...] += value

        @pl.when(step == tiles - 1)
        def _():
            row = lax.broadcasted_iota(jnp.int32, (plan.xz, cells), 0)
            col = lax.broadcasted_iota(jnp.int32, (plan.xz, cells), 1) % plan.xz
            same = row == col
            lines = []
            for c in range(plan.chans):
                part = jnp.where(same, acc[c * plan.xz : (c + 1) * plan.xz, :], 0.0)
                lines.append(jnp.sum(part, 0, keepdims=True))
            sums = jnp.concatenate(lines, 0) * factor
            high = sums.astype(BF)
            low = (sums - high.astype(F32)).astype(BF)
            total = jnp.zeros((MIX_ROWS, LANES), F32)
            for k in range(plan.chans // MIX_ROWS):
                spread = dot(high, place_ref[k]) + dot(low, place_ref[k])
                total += lax.dot_general(
                    pick_ref[k], spread, (((1,), (0,)), ((), ())),
                    precision=lax.Precision.HIGHEST, preferred_element_type=F32,
                )
            out_ref[...] = total

    tile = pl.BlockSpec((cells, width), lambda t: (0, t))
    return pl.pallas_call(
        kernel,
        grid=(tiles,),
        in_specs=[tile, tile, full(pick.shape), full(place.shape)],
        out_specs=full((MIX_ROWS, LANES)),
        scratch_shapes=[pltpu.VMEM((cells, cells), F32)],
        out_shape=shape((MIX_ROWS, LANES), F32),
        compiler_params=params(),
        cost_estimate=cost(4e9, 6e6),
        name="mix_partial",
    )(field.reshape(cells, plan.plane), grad.reshape(cells, plan.plane), pick, place)


def weight_grad(plan, me, field_own, field_got, grad_own, grad_got):
    chans, half = plan.chans, plan.half

    def kernel(me_ref, fo_ref, fg_ref, go_ref, gg_ref, out_ref, held, line):
        me = me_ref[0]
        step = pl.program_id(0)

        @pl.when(step == 0)
        def _():
            held[me] = go_ref[...].astype(F32)
            held[1 - me] = gg_ref[...].astype(F32)

        @pl.when(step < half)
        def _():
            line[...] = fo_ref[step % half].astype(F32) * plan.scale

        @pl.when(step >= half)
        def _():
            line[...] = fg_ref[step % half].astype(F32) * plan.scale

        vr, vi = line[0], line[1]
        for o in range(chans):
            dr = held[o // half, o % half, 0]
            di = held[o // half, o % half, 1]
            out_ref[0, 0, o] = vr * dr + vi * di
            out_ref[1, 0, o] = vr * di - vi * dr

    side = (half, 2, plan.s, plan.modes)
    return pl.pallas_call(
        kernel,
        grid_spec=pltpu.PrefetchScalarGridSpec(
            num_scalar_prefetch=1,
            grid=(chans,),
            in_specs=[full(side)] * 4,
            out_specs=pl.BlockSpec(
                (2, 1, chans, plan.s, plan.modes), lambda t, j: (0, (j[0] * half + t) % chans, 0, 0, 0)
            ),
            scratch_shapes=[pltpu.VMEM((2,) + side, F32), pltpu.VMEM(side[1:], F32)],
        ),
        out_shape=shape((2, chans, chans, plan.s, plan.modes), F32),
        compiler_params=params(),
        cost_estimate=cost(8e9, 1.3e7),
        name="weight_grad",
    )(me, field_own, field_got, grad_own, grad_got)


def local(x_parts, z_parts, field, cotangent, spec_weight, mix_weight):
    plan = Plan(field.shape, spec_weight.shape, x_parts, z_parts)
    const = {name: jnp.asarray(value) for name, value in plan.tables().items()}
    core = lax.axis_index("gz").astype(jnp.int32)
    me = core.reshape(1)
    other = (1 - core).reshape(1)
    plane = const["plane"]

    def swap(value):
        return lax.ppermute(value, "gz", [(0, 1), (1, 0)])

    def spread(chunks):
        return lax.all_to_all(chunks, "gx", split_axis=0, concat_axis=0, tiled=True)

    def to_modes(keep, got):
        chunks = spread(z_forward(plan, me, keep, got, const["z_forward"]))
        send, own = x_forward(plan, me, chunks, const["x_forward"])
        return own, swap(send)

    def product(own, got, adjoint):
        send = mode_product(plan, me, other, spec_weight, own, got, adjoint)
        keep = mode_product(plan, me, me, spec_weight, own, got, adjoint)
        return keep, swap(send)

    def to_cells(keep, got, mix):
        chunks = spread(x_inverse(plan, me, keep, got, const["x_inverse"], mix))
        outs = z_inverse(plan, me, chunks, const["z_inverse"], mix is not None)
        return outs[1], swap(outs[0]), outs[2:]

    mixing = mix_blocks(plan, mix_weight, const["owner"])
    send = plane_forward(plan, other, field, plane)
    keep = plane_forward(plan, me, field, plane)
    field_own, field_got = to_modes(keep, swap(send))
    keep, got = product(field_own, field_got, False)
    keep, got, _ = to_cells(keep, got, None)
    grad, send, keep = cells_forward(plan, me, keep, got, plane, mixing, field, cotangent)
    grad_own, grad_got = to_modes(keep, swap(send))
    partial_mix = mix_partial(plan, field, grad)
    partial_mix = partial_mix + swap(partial_mix)
    keep, got = product(grad_own, grad_got, True)
    spec_grad = weight_grad(plan, me, field_own, field_got, grad_own, grad_got)
    keep, got, mix = to_cells(keep, got, partial_mix)
    field_grad = cells_back(plan, me, keep, got, plane, mixing, grad).reshape(field.shape)
    per_row = plan.chans // MIX_ROWS
    lane = LANES // per_row
    mix_grad = mix[0][:, : per_row * lane].reshape(MIX_ROWS, per_row, lane)[:, :, : plan.chans]
    return (field_grad, spec_grad, mix_grad.reshape(plan.chans, plan.chans))


def solution(mesh):
    placed = (
        P(None, ("grp", "gx"), "gz", None),
        P(None, ("grp", "gx"), "gz", None),
        P(None, None, None, "gx", "gz"),
        P(),
    )
    return jax.shard_map(
        functools.partial(local, mesh.shape["gx"], mesh.shape["gz"]),
        mesh=mesh,
        in_specs=placed,
        out_specs=(
            P(None, ("grp", "gx"), "gz", None),
            P("grp", None, None, "gx", "gz"),
            P("grp", None),
        ),
        check_vma=False,
    )
```

profile of v0, /device:TPU:1, one launch (start us, length us, event | category | flops | bytes accessed | tf_op | source)
XLA Modules:
  0.0 134.7 jit_solution(15214075506968904816)
XLA Ops:
  0.6 1.7 %copy-done = bf16[20,2,16,2048]{3,2,1,0:T(8,128)(2,1)S(1)} copy-done((bf16[20,2,16,2048]{3,2,1,0:T(8,128)(2,1)S(1)}, bf16[20,2,16,2048]{3,2,1,0:T(8,128)(2,1)}, u32[]{:S(2)}) %copy-start) | copy-done | bytes 2621464
  2.4 1.4 %copy-done.5 = bf16[384,2048]{1,0:T(8,128)(2,1)S(1)} copy-done((bf16[384,2048]{1,0:T(8,128)(2,1)S(1)}, bf16[384,2048]{1,0:T(8,128)(2,1)}, u32[]{:S(2)}) %copy-start.5) | copy-done | bytes 1572888
  3.8 2.1 %plane_forward.3 = bf16[384,384]{1,0:T(8,128)(2,1)S(1)} custom-call(s32[1]{0:T(128)} %bitcast.2._, bf16[2,320,2048]{2,1,0:T(8,128)(2,1)S(1)} %bitcast.10, bf16[384,2048]{1,0:T(8,128)(2,1)S(1)} %copy-done.5), custom_call_target="tpu_custom_call" | custom-call | flops 503316480 | bytes 3200000 | tf_op jit(solution)/shard_map/plane_forward/pallas_call | solution.py:159
  6.0 2.1 %plane_forward.2.own_ref = bf16[384,384]{1,0:T(8,128)(2,1)S(1)} custom-call(s32[1]{0:T(128)} %bitcast._.me_ref, bf16[2,320,2048]{2,1,0:T(8,128)(2,1)S(1)} %bitcast.11, bf16[384,2048]{1,0:T(8,128)(2,1)S(1)} %copy-done.5), custom_call_target="tpu_custom_call" | custom-call | flops 503316480 | bytes 3200000 | tf_op jit(solution)/shard_map/plane_forward/pallas_call | solution.py:159
  8.5 16.8 %all_to_all.20.in_ref = bf16[16,64,128]{2,1,0:T(8,128)(2,1)S(1)} all-to-all(bf16[16,64,128]{2,1,0:T(8,128)(2,1)S(1)} %z_forward.2), channel_id=1, replica_groups=mesh['grp'=1,'gx'=16,'gz'=2] {'gx'}, dimensions={0} | all-to-all | bytes 524288 | tf_op jit(solution)/shard_map/all_to_all | solution.py:677
  25.8 1.9 %collective-permute-start.1 = (bf16[10,2,12,192]{3,2,1,0:T(8,128)(2,1)S(1)}, bf16[10,2,12,192]{3,2,1,0:T(8,128)(2,1)S(1)}, u32[]{:S(2)}, u32[]{:S(2)}) collective-permute-start(bf16[10,2,12,192]{3,2,1,0:T(8,128)(2,1)S(1)} %get-tuple-element.16), channel_id=1, source_target_pairs={{0,1},{1,0},{2,3},{3,2},{4,5},{5,4},{6,7},{7,6},{8,9},{9,8},{10,11... | collective-permute-start | bytes 276488 | tf_op jit(solution)/shard_map/ppermute | solution.py:674
  29.1 1.8 %mode_product.5 = bf16[10,2,12,192]{3,2,1,0:T(8,128)(2,1)S(1)} custom-call(s32[1]{0:T(128)} %bitcast._.me_ref, s32[1]{0:T(128)} %bitcast.2._, bf16[2,20,20,12,192]{4,3,2,1,0:T(8,128)(2,1)S(1)} %copy.24.weight_ref, bf16[10,2,12,192]{3,2,1,0:T(8,128)(2,1)S(1)} %get-tuple-element.15.own_ref.fo_ref, ...), custom_call_target="tpu_custom_call" | custom-call | flops 4000000000 | bytes 4000000 | tf_op jit(solution)/shard_map/mode_product/pallas_call | solution.py:292
  31.9 1.8 %mode_product.4.own_ref = bf16[10,2,12,192]{3,2,1,0:T(8,128)(2,1)S(1)} custom-call(s32[1]{0:T(128)} %bitcast._.me_ref, s32[1]{0:T(128)} %bitcast._.me_ref, bf16[2,20,20,12,192]{4,3,2,1,0:T(8,128)(2,1)S(1)} %copy.24.weight_ref, bf16[10,2,12,192]{3,2,1,0:T(8,128)(2,1)S(1)} %get-tuple-element.15.own_ref.fo_ref, ...), custom_call_target="tpu_custom_call" | custom-call | flops 4000000000 | bytes 4000000 | tf_op jit(solution)/shard_map/mode_product/pallas_call | solution.py:292
  34.3 12.1 %all_to_all.21.in_ref = bf16[16,64,128]{2,1,0:T(8,128)(2,1)S(1)} all-to-all(bf16[16,64,128]{2,1,0:T(8,128)(2,1)S(1)} %x_inverse.2), channel_id=1, replica_groups=mesh['grp'=1,'gx'=16,'gz'=2] {'gx'}, dimensions={0} | all-to-all | bytes 524288 | tf_op jit(solution)/shard_map/all_to_all | solution.py:677
  48.2 1.8 %collective-permute-start.3 = (bf16[2,320,192]{2,1,0:T(8,128)(2,1)}, bf16[2,320,192]{2,1,0:T(8,128)(2,1)}, u32[]{:S(2)}, u32[]{:S(2)}) collective-permute-start(bf16[2,320,192]{2,1,0:T(8,128)(2,1)} %get-tuple-element.18), channel_id=1, source_target_pairs={{0,1},{1,0},{2,3},{3,2},{4,5},{5,4},{6,7},{7,6},{8,9},{9,8},{10,11... | collective-permute-start | bytes 737288 | tf_op jit(solution)/shard_map/ppermute | solution.py:674
  51.6 1.6 %copy-done.6 = bf16[384,2048]{1,0:T(8,128)(2,1)S(1)} copy-done((bf16[384,2048]{1,0:T(8,128)(2,1)S(1)}, bf16[384,2048]{1,0:T(8,128)(2,1)}, u32[]{:S(2)}) %copy-start.6) | copy-done | bytes 1572888
  53.2 1.7 %copy-done.16 = bf16[20,2,16,2048]{3,2,1,0:T(8,128)(2,1)S(1)} copy-done((bf16[20,2,16,2048]{3,2,1,0:T(8,128)(2,1)S(1)}, bf16[20,2,16,2048]{3,2,1,0:T(8,128)(2,1)}, u32[]{:S(2)}) %copy-start.16) | copy-done | bytes 2621464
  55.9 13.7 %cells_forward.1 = (bf16[2,320,2048]{2,1,0:T(8,128)(2,1)S(1)}, bf16[384,384]{1,0:T(8,128)(2,1)S(1)}, bf16[384,384]{1,0:T(8,128)(2,1)S(1)}) custom-call(s32[1]{0:T(128)} %bitcast._.me_ref, bf16[2,320,192]{2,1,0:T(8,128)(2,1)S(1)} %copy-done.30, bf16[2,320,192]{2,1,0:T(8,128)(2,1)} %collective-permute-done.3.got_ref, bf16[384,2048]{1,0:T(8,128)(2,1)S(1)} %copy-done.6, ...), custom_call_target="tpu_custom_call" | custom-call | flops 6000000000 | bytes 10000000 | tf_op jit(solution)/shard_map/cells_forward/pallas_call | solution.py:490
  71.6 11.8 %all_to_all.22.in_ref = bf16[16,64,128]{2,1,0:T(8,128)(2,1)S(1)} all-to-all(bf16[16,64,128]{2,1,0:T(8,128)(2,1)S(1)} %z_forward.3), channel_id=1, replica_groups=mesh['grp'=1,'gx'=16,'gz'=2] {'gx'}, dimensions={0} | all-to-all | bytes 524288 | tf_op jit(solution)/shard_map/all_to_all | solution.py:677
  84.0 2.1 %collective-permute-start.5 = (bf16[10,2,12,192]{3,2,1,0:T(8,128)(2,1)S(1)}, bf16[10,2,12,192]{3,2,1,0:T(8,128)(2,1)S(1)}, u32[]{:S(2)}, u32[]{:S(2)}) collective-permute-start(bf16[10,2,12,192]{3,2,1,0:T(8,128)(2,1)S(1)} %get-tuple-element.22), channel_id=1, source_target_pairs={{0,1},{1,0},{2,3},{3,2},{4,5},{5,4},{6,7},{7,6},{8,9},{9,8},{10,11... | collective-permute-start | bytes 276488 | tf_op jit(solution)/shard_map/ppermute | solution.py:674
  86.1 5.0 %mix_partial.1 = f32[4,128]{1,0:T(4,128)S(1)} custom-call(bf16[640,2048]{1,0:T(8,128)(2,1)S(1)} %bitcast.13, bf16[640,2048]{1,0:T(8,128)(2,1)S(1)} %bitcast.19, f32[5,4,20]{2,1,0:T(4,128)S(1)} %copy-done.26, bf16[5,640,128]{2,1,0:T(8,128)(2,1)S(1)} %copy-done.23), custom_call_target="tpu_custom_call" | custom-call | flops 4000000000 | bytes 6000000 | tf_op jit(solution)/shard_map/mix_partial/pallas_call | solution.py:606
  92.3 1.7 %mode_product.7 = bf16[10,2,12,192]{3,2,1,0:T(8,128)(2,1)S(1)} custom-call(s32[1]{0:T(128)} %bitcast._.me_ref, s32[1]{0:T(128)} %bitcast.2._, bf16[2,20,20,12,192]{4,3,2,1,0:T(8,128)(2,1)S(1)} %bitcast.15, bf16[10,2,12,192]{3,2,1,0:T(8,128)(2,1)S(1)} %get-tuple-element.21.own_ref.go_ref, bf16[10,2,12,192]{3,2,1,0:T(8,128)(2,1)S(1)} %collective-permute-done.5.got_ref.gg_ref), custom_call_target="tpu_custom_call" | custom-call | flops 4000000000 | bytes 4000000 | tf_op jit(solution)/shard_map/mode_product/pallas_call | solution.py:292
  94.3 1.7 %mode_product.6.own_ref = bf16[10,2,12,192]{3,2,1,0:T(8,128)(2,1)S(1)} custom-call(s32[1]{0:T(128)} %bitcast._.me_ref, s32[1]{0:T(128)} %bitcast._.me_ref, bf16[2,20,20,12,192]{4,3,2,1,0:T(8,128)(2,1)S(1)} %bitcast.15, bf16[10,2,12,192]{3,2,1,0:T(8,128)(2,1)S(1)} %get-tuple-element.21.own_ref.go_ref, ...), custom_call_target="tpu_custom_call" | custom-call | flops 4000000000 | bytes 4000000 | tf_op jit(solution)/shard_map/mode_product/pallas_call | solution.py:292
  96.7 11.5 %all_to_all.23.in_ref = bf16[16,64,128]{2,1,0:T(8,128)(2,1)S(1)} all-to-all(bf16[16,64,128]{2,1,0:T(8,128)(2,1)S(1)} %x_inverse.3), channel_id=1, replica_groups=mesh['grp'=1,'gx'=16,'gz'=2] {'gx'}, dimensions={0} | all-to-all | bytes 524288 | tf_op jit(solution)/shard_map/all_to_all | solution.py:677
  109.3 2.4 %collective-permute-start.8 = (bf16[2,320,192]{2,1,0:T(8,128)(2,1)}, bf16[2,320,192]{2,1,0:T(8,128)(2,1)S(1)}, u32[]{:S(2)}, u32[]{:S(2)}) collective-permute-start(bf16[2,320,192]{2,1,0:T(8,128)(2,1)} %get-tuple-element.25), channel_id=1, source_target_pairs={{0,1},{1,0},{2,3},{3,2},{4,5},{5,4},{6,7},{7,6},{8,9},{9,8},{10,11... | collective-permute-start | bytes 737288 | tf_op jit(solution)/shard_map/ppermute | solution.py:674
  111.7 3.6 %weight_grad.1 = f32[2,20,20,12,192]{4,3,2,1,0:T(8,128)S(1)} custom-call(s32[1]{0:T(128)} %bitcast._.me_ref, bf16[10,2,12,192]{3,2,1,0:T(8,128)(2,1)S(1)} %copy-done.18, bf16[10,2,12,192]{3,2,1,0:T(8,128)(2,1)S(1)} %copy-done.20, bf16[10,2,12,192]{3,2,1,0:T(8,128)(2,1)S(1)} %get-tuple-element.21.own_ref.go_ref, ...), custom_call_target="tpu_custom_call" | custom-call | flops 8000000000 | bytes 13000000 | tf_op jit(solution)/shard_map/weight_grad/pallas_call | solution.py:647
  115.4 9.4 %copy.26 = f32[2,20,20,12,192]{4,0,3,2,1:T(2,128)} copy(f32[2,20,20,12,192]{4,3,2,1,0:T(8,128)S(1)} %weight_grad.1) | data formatting | bytes 14745600
  126.8 1.7 %copy-done.22 = bf16[2,320,2048]{2,1,0:T(8,128)(2,1)S(1)} copy-done((bf16[2,320,2048]{2,1,0:T(8,128)(2,1)S(1)}, bf16[2,320,2048]{2,1,0:T(8,128)(2,1)}, u32[]{:S(2)}) %copy-start.22) | copy-done | bytes 2621464
  129.5 5.2 %cells_back.1 = bf16[2,320,2048]{2,1,0:T(8,128)(2,1)} custom-call(s32[1]{0:T(128)} %bitcast._.me_ref, bf16[2,320,192]{2,1,0:T(8,128)(2,1)S(1)} %copy-done.28, bf16[2,320,192]{2,1,0:T(8,128)(2,1)S(1)} %collective-permute-done.8.got_ref, bf16[384,2048]{1,0:T(8,128)(2,1)S(1)} %copy-done.7, bf16[2,2,320,640]{3,2,1,0:T(8,128)(2,1)S(1)} %copy-done.12, ...), custom_call_target="tpu_custom_call" | custom-call | flops 4000000000 | bytes 8000000 | tf_op jit(solution)/shard_map/cells_back/pallas_call | solution.py:530
  (92 shorter events, 16.9 us)
Async XLA Ops:
  5.9 2.2 %collective-permute-start = (bf16[384,384]{1,0:T(8,128)(2,1)S(1)}, bf16[384,384]{1,0:T(8,128)(2,1)S(1)}, u32[]{:S(2)}, u32[]{:S(2)}) collective-permute-start(bf16[384,384]{1,0:T(8,128)(2,1)S(1)} %plane_forward.3), channel_id=1, source_target_pairs={{0,1},{1,0},{2,3},{3,2},{4,5},{5,4},{6,7},{7,6},{8,9},{9,8},{10,11... | collective-permute-start | bytes 884744 | tf_op jit(solution)/shard_map/ppermute | solution.py:674
  6.0 19.3 %copy-start.2 = (bf16[2,2,1024,192]{3,2,1,0:T(8,128)(2,1)S(1)}, bf16[2,2,1024,192]{3,2,1,0:T(8,128)(2,1)}, u32[]{:S(2)}) copy-start(bf16[2,2,1024,192]{3,2,1,0:T(8,128)(2,1)} %constant.25.clone.table_ref) | copy-start | bytes 4718596
  6.0 21.7 %copy-start.31 = (bf16[2,20,20,12,192]{4,0,3,2,1:T(2,128)(2,1)S(1)}, bf16[2,20,20,12,192]{4,0,3,2,1:T(2,128)(2,1)}, u32[]{:S(2)}) copy-start(bf16[2,20,20,12,192]{4,0,3,2,1:T(2,128)(2,1)} %param.14) | copy-start | bytes 11059204
  25.8 3.3 %collective-permute-start.1 = (bf16[10,2,12,192]{3,2,1,0:T(8,128)(2,1)S(1)}, bf16[10,2,12,192]{3,2,1,0:T(8,128)(2,1)S(1)}, u32[]{:S(2)}, u32[]{:S(2)}) collective-permute-start(bf16[10,2,12,192]{3,2,1,0:T(8,128)(2,1)S(1)} %get-tuple-element.16), channel_id=1, source_target_pairs={{0,1},{1,0},{2,3},{3,2},{4,5},{5,4},{6,7},{7,6},{8,9},{9,8},{10,11... | collective-permute-start | bytes 276488 | tf_op jit(solution)/shard_map/ppermute | solution.py:674
  31.0 2.8 %collective-permute-start.2 = (bf16[10,2,12,192]{3,2,1,0:T(8,128)(2,1)S(1)}, bf16[10,2,12,192]{3,2,1,0:T(8,128)(2,1)S(1)}, u32[]{:S(2)}, u32[]{:S(2)}) collective-permute-start(bf16[10,2,12,192]{3,2,1,0:T(8,128)(2,1)S(1)} %mode_product.5), channel_id=1, source_target_pairs={{0,1},{1,0},{2,3},{3,2},{4,5},{5,4},{6,7},{7,6},{8,9},{9,8},{10,11... | collective-permute-start | bytes 276488 | tf_op jit(solution)/shard_map/ppermute | solution.py:674
  33.7 12.6 %copy-start.24 = (bf16[2,512,256]{2,1,0:T(8,128)(2,1)S(1)}, bf16[2,512,256]{2,1,0:T(8,128)(2,1)}, u32[]{:S(2)}) copy-start(bf16[2,512,256]{2,1,0:T(8,128)(2,1)} %constant.24.clone.table_ref) | copy-start | bytes 1572868
  33.7 16.3 %copy-start.15 = (bf16[20,20]{1,0:T(8,128)(2,1)S(1)}, bf16[20,20]{1,0:T(8,128)(2,1)}, u32[]{:S(2)}) copy-start(bf16[20,20]{1,0:T(8,128)(2,1)} %back_ref.1) | copy-start | bytes 2404
  33.7 16.4 %copy-start.13 = (bf16[640,20]{1,0:T(8,128)(2,1)S(1)}, bf16[640,20]{1,0:T(8,128)(2,1)}, u32[]{:S(2)}) copy-start(bf16[640,20]{1,0:T(8,128)(2,1)} %constant.27.clone.owner_ref) | copy-start | bytes 76804
  33.8 16.4 %copy-start.14 = (bf16[20,640]{1,0:T(8,128)(2,1)S(1)}, bf16[20,640]{1,0:T(8,128)(2,1)}, u32[]{:S(2)}) copy-start(bf16[20,640]{1,0:T(8,128)(2,1)} %constant.33.owner_t_ref) | copy-start | bytes 76804
  48.2 3.4 %collective-permute-start.3 = (bf16[2,320,192]{2,1,0:T(8,128)(2,1)}, bf16[2,320,192]{2,1,0:T(8,128)(2,1)}, u32[]{:S(2)}, u32[]{:S(2)}) collective-permute-start(bf16[2,320,192]{2,1,0:T(8,128)(2,1)} %get-tuple-element.18), channel_id=1, source_target_pairs={{0,1},{1,0},{2,3},{3,2},{4,5},{5,4},{6,7},{7,6},{8,9},{9,8},{10,11... | collective-permute-start | bytes 737288 | tf_op jit(solution)/shard_map/ppermute | solution.py:674
  51.2 18.4 %copy-start.11 = (bf16[2,2,320,640]{3,2,1,0:T(8,128)(2,1)}, bf16[2,2,320,640]{3,2,1,0:T(8,128)(2,1)S(1)}, u32[]{:S(2)}) copy-start(bf16[2,2,320,640]{3,2,1,0:T(8,128)(2,1)S(1)} %mix_blocks.1.mix_ref) | copy-start | bytes 4915204
  55.9 27.6 %copy-start.3 = (bf16[2,2,1024,192]{3,2,1,0:T(8,128)(2,1)S(1)}, bf16[2,2,1024,192]{3,2,1,0:T(8,128)(2,1)}, u32[]{:S(2)}) copy-start(bf16[2,2,1024,192]{3,2,1,0:T(8,128)(2,1)} %constant.25.clone.table_ref) | copy-start | bytes 4718596
  69.6 21.5 %copy-start.21 = (bf16[2,320,2048]{2,1,0:T(8,128)(2,1)}, bf16[2,320,2048]{2,1,0:T(8,128)(2,1)S(1)}, u32[]{:S(2)}) copy-start(bf16[2,320,2048]{2,1,0:T(8,128)(2,1)S(1)} %get-tuple-element.23) | copy-start | bytes 7864324
  69.6 16.5 %copy-start.23 = (bf16[5,640,128]{2,1,0:T(8,128)(2,1)S(1)}, bf16[5,640,128]{2,1,0:T(8,128)(2,1)}, u32[]{:S(2)}) copy-start(bf16[5,640,128]{2,1,0:T(8,128)(2,1)} %constant.29.clone.place_ref) | copy-start | bytes 2457604
  69.6 16.5 %copy-start.26 = (f32[5,4,20]{2,1,0:T(4,128)S(1)}, f32[5,4,20]{2,1,0:T(4,128)}, u32[]{:S(2)}) copy-start(f32[5,4,20]{2,1,0:T(4,128)} %constant.28.clone.pick_ref) | copy-start | bytes 4804
  69.6 1.6 %collective-permute-start.4 = (bf16[384,384]{1,0:T(8,128)(2,1)S(1)}, bf16[384,384]{1,0:T(8,128)(2,1)S(1)}, u32[]{:S(2)}, u32[]{:S(2)}) collective-permute-start(bf16[384,384]{1,0:T(8,128)(2,1)S(1)} %get-tuple-element.20), channel_id=1, source_target_pairs={{0,1},{1,0},{2,3},{3,2},{4,5},{5,4},{6,7},{7,6},{8,9},{9,8},{10,11... | collective-permute-start | bytes 884744 | tf_op jit(solution)/shard_map/ppermute | solution.py:674
  84.0 8.3 %collective-permute-start.5 = (bf16[10,2,12,192]{3,2,1,0:T(8,128)(2,1)S(1)}, bf16[10,2,12,192]{3,2,1,0:T(8,128)(2,1)S(1)}, u32[]{:S(2)}, u32[]{:S(2)}) collective-permute-start(bf16[10,2,12,192]{3,2,1,0:T(8,128)(2,1)S(1)} %get-tuple-element.22), channel_id=1, source_target_pairs={{0,1},{1,0},{2,3},{3,2},{4,5},{5,4},{6,7},{7,6},{8,9},{9,8},{10,11... | collective-permute-start | bytes 276488 | tf_op jit(solution)/shard_map/ppermute | solution.py:674
  91.1 1.2 collective-permute-start.7
  94.1 2.0 %collective-permute-start.6 = (bf16[10,2,12,192]{3,2,1,0:T(8,128)(2,1)S(1)}, bf16[10,2,12,192]{3,2,1,0:T(8,128)(2,1)S(1)}, u32[]{:S(2)}, u32[]{:S(2)}) collective-permute-start(bf16[10,2,12,192]{3,2,1,0:T(8,128)(2,1)S(1)} %mode_product.7), channel_id=1, source_target_pairs={{0,1},{1,0},{2,3},{3,2},{4,5},{5,4},{6,7},{7,6},{8,9},{9,8},{10,11... | collective-permute-start | bytes 276488 | tf_op jit(solution)/shard_map/ppermute | solution.py:674
  96.1 12.2 %copy-start.25 = (bf16[2,512,256]{2,1,0:T(8,128)(2,1)S(1)}, bf16[2,512,256]{2,1,0:T(8,128)(2,1)}, u32[]{:S(2)}) copy-start(bf16[2,512,256]{2,1,0:T(8,128)(2,1)} %constant.24.clone.table_ref) | copy-start | bytes 1572868
  96.1 15.6 %copy-start.18 = (bf16[10,2,12,192]{3,2,1,0:T(8,128)(2,1)S(1)}, bf16[10,2,12,192]{3,2,1,0:T(8,128)(2,1)}, u32[]{:S(2)}) copy-start(bf16[10,2,12,192]{3,2,1,0:T(8,128)(2,1)} %copy-done.17) | copy-start | bytes 276484
  96.1 15.6 %copy-start.20 = (bf16[10,2,12,192]{3,2,1,0:T(8,128)(2,1)S(1)}, bf16[10,2,12,192]{3,2,1,0:T(8,128)(2,1)}, u32[]{:S(2)}) copy-start(bf16[10,2,12,192]{3,2,1,0:T(8,128)(2,1)} %copy-done.19) | copy-start | bytes 276484
  109.3 17.4 %collective-permute-start.8 = (bf16[2,320,192]{2,1,0:T(8,128)(2,1)}, bf16[2,320,192]{2,1,0:T(8,128)(2,1)S(1)}, u32[]{:S(2)}, u32[]{:S(2)}) collective-permute-start(bf16[2,320,192]{2,1,0:T(8,128)(2,1)} %get-tuple-element.25), channel_id=1, source_target_pairs={{0,1},{1,0},{2,3},{3,2},{4,5},{5,4},{6,7},{7,6},{8,9},{9,8},{10,11... | collective-permute-start | bytes 737288 | tf_op jit(solution)/shard_map/ppermute | solution.py:674
  115.3 11.4 %copy-start.7 = (bf16[384,2048]{1,0:T(8,128)(2,1)S(1)}, bf16[384,2048]{1,0:T(8,128)(2,1)}, u32[]{:S(2)}) copy-start(bf16[384,2048]{1,0:T(8,128)(2,1)} %constant.22.clone.plane_ref) | copy-start | bytes 4718596
  (19 other events, 63.5 us)
where the time goes:
time: 135 us
  blocking collectives  52.2 us (39%)
  Pallas kernels  44.8 us (33%)
  local copies, waits for them, and re-layouts  24.6 us (18%)
  starting transfers between devices  9.12 us (7%)
  waiting for transfers between devices  2.88 us (2%)
    all_to_all x4, blocking collectives, spread(): return lax.all_to_all(chunks, 'gx', split_axis=0, concat_axis=0, tiled=True)  52.2 us
    unnamed x71, local copies, waits for them, and re-layouts  22.6 us
    pallas_call x1, Pallas kernels, cells_forward(): pl.pallas_call(kernel, grid_spec=pltpu.PrefetchScalarGridSpec(num_scalar_...  13.7 us
    ppermute x9, starting transfers between devices, swap(): return lax.ppermute(value, 'gz', [(0, 1), (1, 0)])  9.12 us
    pallas_call x4, Pallas kernels, mode_product(): pl.pallas_call(kernel, grid_spec=pltpu.PrefetchScalarGridSpec(num_scalar_...  7.04 us
    pallas_call x1, Pallas kernels, cells_back(): pl.pallas_call(kernel, grid_spec=pltpu.PrefetchScalarGridSpec(num_scalar_...  5.23 us
    pallas_call x1, Pallas kernels, mix_partial(): pl.pallas_call(kernel, grid=(tiles,), in_specs=[tile, tile, full(pick.sha...  5 us
    pallas_call x2, Pallas kernels, plane_forward(): pl.pallas_call(kernel, grid_spec=pltpu.PrefetchScalarGridSpec(num_scalar_...  4.16 us
  transfers between devices with their start and end apart: 9, of which 3 were waited for; matrix products, arithmetic and copies ran while one was open for 10% of the time, Pallas kernels for 11%

commit v1 on v0

--- a/solution.py
+++ b/solution.py
@@ -7,6 +7,7 @@
 import numpy as np
 from jax import lax
 from jax.experimental import pallas as pl
+from jax.experimental.layout import Layout, with_layout_constraint
 from jax.experimental.pallas import tpu as pltpu
 from jax.sharding import PartitionSpec as P
 
@@ -20,7 +21,7 @@
 MIX_ROWS = 4
 BF = jnp.bfloat16
 F32 = jnp.float32
-VMEM_LIMIT = 40 * 1024 * 1024
+VMEM_LIMIT = 18 * 1024 * 1024
 
 
 def mode_angles(length, count, one_sided):
@@ -117,6 +118,19 @@
     return pl.CostEstimate(flops=int(flops), bytes_accessed=int(nbytes), transcendentals=0)
 
 
+def hbm(value):
+    return pltpu.with_memory_space_constraint(value, pltpu.HBM)
+
+
+def vmem(value):
+    return pltpu.with_memory_space_constraint(value, pltpu.VMEM)
+
+
+WHOLE = pl.BlockSpec(memory_space=pltpu.VMEM)
+SCALAR = pl.BlockSpec(memory_space=pltpu.SMEM)
+ANYWHERE = pl.BlockSpec(memory_space=pl.ANY)
+
+
 def shape(dims, kind=BF):
     return jax.ShapeDtypeStruct(tuple(dims), kind)
 
@@ -133,46 +147,85 @@
     return lax.dot_general(a, b, (((1,), (1,)), ((), ())), preferred_element_type=F32)
 
 
-def plane_forward(plan, which, field, plane):
+def pad_lanes(plan, out_ref):
+    if plan.rows_pad > plan.rows:
+        pad = plan.rows_pad - plan.rows
+        out_ref[:, plan.rows :] = jnp.zeros((2 * plan.ms, pad), BF)
+
+
+def half_rows(plan, half):
+    return pl.ds(pl.multiple_of(2 * plan.ms + half * plan.rows, math.gcd(2 * plan.ms, plan.rows)), plan.rows)
+
+
+def load_forward(plan, me, field, plane):
     tiles = 4
     width = plan.plane // tiles
-
-    def kernel(_, field_ref, plane_ref, out_ref, acc_ref):
-        step = pl.program_id(0)
-        value = dot_t(plane_ref[...], field_ref[0])
-
-        @pl.when(step == 0)
-        def _():
-            acc_ref[...] = value
-
-        @pl.when(step > 0)
-        def _():
-            acc_ref[...] += value
-
-        @pl.when(step == tiles - 1)
-        def _():
-            if plan.rows_pad > plan.rows:
-                pad = plan.rows_pad - plan.rows
-                out_ref[:, plan.rows :] = jnp.zeros((2 * plan.ms, pad), BF)
-            out_ref[:, : plan.rows] = acc_ref[...].astype(BF)
-
-    return pl.pallas_call(
-        kernel,
-        grid_spec=pltpu.PrefetchScalarGridSpec(
-            num_scalar_prefetch=1,
-            grid=(tiles,),
-            in_specs=[
-                pl.BlockSpec((1, plan.rows, width), lambda t, h: (h[0], 0, t)),
-                pl.BlockSpec((2 * plan.ms, width), lambda t, h: (0, t)),
-            ],
-            out_specs=full((2 * plan.ms, plan.rows_pad)),
-            scratch_shapes=[pltpu.VMEM((2 * plan.ms, plan.rows), F32)],
-        ),
-        out_shape=shape((2 * plan.ms, plan.rows_pad)),
-        compiler_params=params(),
-        cost_estimate=cost(4 * plan.ms * plan.rows * plan.plane, 3.2e6),
+    ms2 = 2 * plan.ms
+
+    def kernel(me_ref, field_ref, plane_ref, stack_ref, out_ref, acc, sems):
+        me = me_ref[0]
+        copies = []
+        for k in range(tiles):
+            at = slice(k * width, (k + 1) * width)
+            copies.append(
+                (
+                    pltpu.make_async_copy(plane_ref.at[:, at], stack_ref.at[:ms2, at], sems.at[0, k]),
+                    pltpu.make_async_copy(
+                        field_ref.at[1 - me, :, at], stack_ref.at[half_rows(plan, 1 - me), at], sems.at[1, k]
+                    ),
+                    pltpu.make_async_copy(
+                        field_ref.at[me, :, at], stack_ref.at[half_rows(plan, me), at], sems.at[2, k]
+                    ),
+                )
+            )
+        for group in copies:
+            group[0].start()
+            group[1].start()
+        for group in copies:
+            group[2].start()
+        for k, group in enumerate(copies):
+            at = slice(k * width, (k + 1) * width)
+            group[0].wait()
+            group[1].wait()
+            value = dot_t(stack_ref[:ms2, at], stack_ref[half_rows(plan, 1 - me), at])
+            if k == 0:
+                acc[...] = value
+            else:
+                acc[...] += value
+        pad_lanes(plan, out_ref)
+        out_ref[:, : plan.rows] = acc[...].astype(BF)
+        for group in copies:
+            group[2].wait()
+
+    return pl.pallas_call(
+        kernel,
+        in_specs=[SCALAR, ANYWHERE, ANYWHERE],
+        out_specs=[WHOLE, WHOLE],
+        out_shape=[pltpu.VMEM((ms2 + 2 * plan.rows, plan.plane), BF), shape((ms2, plan.rows_pad))],
+        scratch_shapes=[pltpu.VMEM((ms2, plan.rows), F32), pltpu.SemaphoreType.DMA((3, tiles))],
+        compiler_params=params(),
+        cost_estimate=cost(4 * plan.ms * plan.rows * plan.plane, 5e6),
+        name="load_forward",
+    )(me, hbm(field.reshape(2, plan.rows, plan.plane)), hbm(plane))
+
+
+def plane_forward(plan, me, stack):
+    ms2 = 2 * plan.ms
+
+    def kernel(me_ref, stack_ref, out_ref):
+        value = dot_t(stack_ref[:ms2, :], stack_ref[half_rows(plan, me_ref[0]), :])
+        pad_lanes(plan, out_ref)
+        out_ref[:, : plan.rows] = value.astype(BF)
+
+    return pl.pallas_call(
+        kernel,
+        in_specs=[SCALAR, WHOLE],
+        out_specs=WHOLE,
+        out_shape=shape((ms2, plan.rows_pad)),
+        compiler_params=params(),
+        cost_estimate=cost(4 * plan.ms * plan.rows * plan.plane, 3e6),
         name="plane_forward",
-    )(which, field.reshape(2, plan.rows, plan.plane), plane)
+    )(me, vmem(stack))
 
 
 def z_forward(plan, me, own, got, table):
@@ -252,23 +305,18 @@
     )(me, chunks, table)
 
 
-def mode_product(plan, me, which, weight, own, got, adjoint):
-    block = 2
-    steps = plan.half // block
-
-    def kernel(me_ref, _, weight_ref, own_ref, got_ref, out_ref, held):
+def mode_product(plan, me, mine, weight, own, got, adjoint):
+    def kernel(me_ref, weight_ref, own_ref, got_ref, out_ref, held):
         me = me_ref[0]
-
-        @pl.when(pl.program_id(0) == 0)
-        def _():
-            held[me] = own_ref[...].astype(F32)
-            held[1 - me] = got_ref[...].astype(F32)
-
-        for k in range(block):
+        held[me] = own_ref[...].astype(F32)
+        held[1 - me] = got_ref[...].astype(F32)
+        first = (me if mine else 1 - me) * plan.half
+
+        def one(k, carry):
             real = jnp.zeros((plan.s, plan.modes), F32)
             imag = jnp.zeros((plan.s, plan.modes), F32)
             for c in range(plan.chans):
-                pos = (k, c) if adjoint else (c, k)
+                pos = (first + k, c) if adjoint else (c, first + k)
                 wr = weight_ref[0, pos[0], pos[1]].astype(F32)
                 wi = weight_ref[1, pos[0], pos[1]].astype(F32)
                 mr = held[c // plan.half, c % plan.half, 0]
@@ -281,28 +329,21 @@
                     imag += wr * mi + wi * mr
             out_ref[k, 0] = real.astype(BF)
             out_ref[k, 1] = imag.astype(BF)
+            return carry
+
+        lax.fori_loop(0, plan.half, one, 0)
 
     side = (plan.half, 2, plan.s, plan.modes)
-    if adjoint:
-        w_block = (2, block, plan.chans, plan.s, plan.modes)
-        w_map = lambda t, j, h: (0, h[0] * steps + t, 0, 0, 0)
-    else:
-        w_block = (2, plan.chans, block, plan.s, plan.modes)
-        w_map = lambda t, j, h: (0, 0, h[0] * steps + t, 0, 0)
-    return pl.pallas_call(
-        kernel,
-        grid_spec=pltpu.PrefetchScalarGridSpec(
-            num_scalar_prefetch=2,
-            grid=(steps,),
-            in_specs=[pl.BlockSpec(w_block, w_map), full(side), full(side)],
-            out_specs=pl.BlockSpec((block, 2, plan.s, plan.modes), lambda t, j, h: (t, 0, 0, 0)),
-            scratch_shapes=[pltpu.VMEM((2,) + side, F32)],
-        ),
+    return pl.pallas_call(
+        kernel,
+        in_specs=[SCALAR, WHOLE, WHOLE, WHOLE],
+        out_specs=WHOLE,
         out_shape=shape(side),
-        compiler_params=params(),
-        cost_estimate=cost(4e9, 4e6),
+        scratch_shapes=[pltpu.VMEM((2,) + side, F32)],
+        compiler_params=params(),
+        cost_estimate=cost(2e9, 4e6),
         name="mode_product",
-    )(me, which, weight, own, got)
+    )(me, vmem(weight), own, got)
 
 
 def x_inverse(plan, me, own, got, table, mix):
@@ -377,21 +418,26 @@
             value = dot_t(table_ref[0], jnp.concatenate([first, second], 1))
             rows = min(LANES, plan.rows - g * LANES)
             for slot, out_ref in ((0, send_ref), (1, keep_ref)):
-                for p in (0, 1):
-                    start = (2 * slot + p) * LANES
-                    out_ref[p, g * LANES : g * LANES + rows, :] = value[start : start + rows].astype(BF)
+                start = 2 * slot * LANES
+                both = [value[start : start + rows], value[start + LANES : start + LANES + rows]]
+                both = jnp.concatenate(both, 1) * plan.scale
+                out_ref[g * LANES : g * LANES + rows, :] = both.astype(BF)
         if carry:
             total = pieces[0, plan.used : plan.used + MIX_ROWS, :]
             for i in range(1, plan.xp):
                 total = total + pieces[i, plan.used : plan.used + MIX_ROWS, :]
-            mix_ref[...] = total
-
-    out = (2, plan.rows, plan.ms)
+            per_row = plan.chans // MIX_ROWS
+            lane = LANES // per_row
+            for c in range(plan.chans):
+                row, start = c // per_row, (c % per_row) * lane
+                mix_ref[c : c + 1, :] = total[row : row + 1, start : start + plan.chans]
+
+    out = (plan.rows, 2 * plan.ms)
     outs = [out, out]
     out_shape = [shape(out), shape(out)]
     if carry:
-        outs.append((MIX_ROWS, LANES))
-        out_shape.append(shape((MIX_ROWS, LANES), F32))
+        outs.append((plan.chans, plan.chans))
+        out_shape.append(shape((plan.chans, plan.chans), F32))
     return pl.pallas_call(
         kernel,
         grid_spec=pltpu.PrefetchScalarGridSpec(
@@ -417,19 +463,19 @@
 def mix_blocks(plan, mix, owner):
     cells = 2 * plan.rows
 
-    def kernel(mix_ref, back_ref, owner_ref, owner_t_ref, out_ref):
+    def kernel(mix_ref, back_ref, owner_ref, owner_t_ref, *outs):
         row = lax.broadcasted_iota(jnp.int32, (plan.rows, cells), 0) % plan.xz
         col = lax.broadcasted_iota(jnp.int32, (plan.rows, cells), 1) % plan.xz
         same = row == col
-        for d, ref in ((0, mix_ref), (1, back_ref)):
+        for out_ref, ref in zip(outs, (mix_ref, back_ref)):
             for h in (0, 1):
                 spread = dot(owner_ref[h * plan.rows : (h + 1) * plan.rows, :], ref[...]).astype(BF)
                 wide = dot(spread, owner_t_ref[...])
-                out_ref[d, h] = jnp.where(same, wide, 0.0).astype(BF)
-
-    return pl.pallas_call(
-        kernel,
-        out_shape=shape((2, 2, plan.rows, cells)),
+                out_ref[h] = jnp.where(same, wide, 0.0).astype(BF)
+
+    return pl.pallas_call(
+        kernel,
+        out_shape=[pltpu.VMEM((2, plan.rows, cells), BF)] * 2,
         compiler_params=params(),
         cost_estimate=cost(4e7, 2e6),
         name="mix_blocks",
@@ -438,114 +484,133 @@
 
 def gelu_slope(pre):
     size = jnp.abs(pre)
-    bell = jnp.exp(pre * pre * -0.5)
+    bell = jnp.exp2(pre * pre * (-0.5 / math.log(2.0)))
     t = 1.0 / (1.0 + size * (0.3275911 / math.sqrt(2.0)))
     poly = 0.5 * 1.061405429
     for coef in (-1.453152027, 1.421413741, -0.284496736, 0.254829592):
         poly = poly * t + 0.5 * coef
-    tail = poly * t * bell
-    cdf = jnp.where(pre < 0.0, tail, 1.0 - tail)
-    return cdf + pre * bell * (1.0 / math.sqrt(2.0 * math.pi))
-
-
-def cells_forward(plan, me, own, got, plane, mixing, field, cotangent):
-    tiles = 4
+    low = bell * (poly * t - size * (1.0 / math.sqrt(2.0 * math.pi)))
+    return jnp.where(pre < 0.0, low, 1.0 - low)
+
+
+def fill_lhs(plan, me, lhs, own_ref, got_ref, mix_ref):
+    ms2 = 2 * plan.ms
+    for half, in_ref in ((me, own_ref), (1 - me, got_ref)):
+        lhs[half, :, :ms2] = in_ref[...]
+    for half in (0, 1):
+        lhs[half, :, ms2:] = mix_ref[half]
+
+
+def cells_forward(plan, me, own, got, plane, mixing, stack, cotangent):
+    tiles = 2
     width = plan.plane // tiles
     stripe = 32
-
-    def kernel(me_ref, own_ref, got_ref, plane_ref, mix_ref, field_ref, cot_ref, grad_ref, send_ref, keep_ref, pre, acc):
+    ms2 = 2 * plan.ms
+    deep = ms2 + 2 * plan.rows
+    items = [(t, h) for t in range(tiles) for h in (0, 1)]
+
+    def kernel(
+        me_ref, own_ref, got_ref, plane_ref, mix_ref, stack_ref, cot_ref,
+        grad_ref, send_ref, keep_ref, lhs, pre, acc, cot, sems,
+    ):
         me = me_ref[0]
-        step = pl.program_id(0)
-        ms = plan.ms
-        for slot, half, in_ref in ((0, me, own_ref), (1, 1 - me, got_ref)):
-            spectral = dot(in_ref[0], plane_ref[:ms]) + dot(in_ref[1], plane_ref[ms:])
-            mixed = dot(mix_ref[0, half], field_ref[...])
-            pre[slot] = spectral * plan.scale + mixed
+        copies = []
+        for n, (t, h) in enumerate(items):
+            at = slice(t * width, (t + 1) * width)
+            copies.append(pltpu.make_async_copy(cot_ref.at[h, :, at], cot.at[h, :, at], sems.at[n]))
+            copies[-1].start()
+        table = pltpu.make_async_copy(plane_ref, grad_ref.at[:ms2, :], sems.at[len(items)])
+        table.start()
+        fill_lhs(plan, me, lhs, own_ref, got_ref, mix_ref)
+
+        def product(n):
+            t, h = items[n]
+            pre[n % 2] = dot(lhs[h], stack_ref[:, t * width : (t + 1) * width])
+
+        def slope(n):
+            t, h = items[n]
+            at = slice(t * width, (t + 1) * width)
+            copies[n].wait()
             for r in range(0, plan.rows, stripe):
-                at = slice(r, r + stripe)
-                slope = gelu_slope(pre[slot, at, :])
-                grad_ref[half, at, :] = (cot_ref[half, at, :].astype(F32) * slope).astype(BF)
-            value = dot_t(plane_ref[...], grad_ref[half])
-
-            @pl.when(step == 0)
-            def _():
-                acc[slot] = value
-
-            @pl.when(step > 0)
-            def _():
-                acc[slot] += value
-
-        @pl.when(step == tiles - 1)
-        def _():
-            for slot, out_ref in ((0, keep_ref), (1, send_ref)):
-                if plan.rows_pad > plan.rows:
-                    pad = plan.rows_pad - plan.rows
-                    out_ref[:, plan.rows :] = jnp.zeros((2 * ms, pad), BF)
-                out_ref[:, : plan.rows] = acc[slot].astype(BF)
-
-    side = (2, plan.rows, plan.ms)
-    out = (2 * plan.ms, plan.rows_pad)
-    cells = (2, plan.rows, plan.plane)
-    tile = pl.BlockSpec((2, plan.rows, width), lambda t, j: (0, 0, t))
-    return pl.pallas_call(
-        kernel,
-        grid_spec=pltpu.PrefetchScalarGridSpec(
-            num_scalar_prefetch=1,
-            grid=(tiles,),
-            in_specs=[
-                full(side),
-                full(side),
-                pl.BlockSpec((2 * plan.ms, width), lambda t, j: (0, t)),
-                pl.BlockSpec((1, 2, plan.rows, 2 * plan.rows), lambda t, j: (0, 0, 0, 0)),
-                pl.BlockSpec((2 * plan.rows, width), lambda t, j: (0, t)),
-                tile,
-            ],
-            out_specs=[tile, full(out), full(out)],
-            scratch_shapes=[
-                pltpu.VMEM((2, plan.rows, width), F32),
-                pltpu.VMEM((2, 2 * plan.ms, plan.rows), F32),
-            ],
-        ),
-        out_shape=[shape(cells), shape(out), shape(out)],
+                value = cot[h, r : r + stripe, at].astype(F32) * gelu_slope(pre[n % 2, r : r + stripe, :])
+                start = ms2 + h * plan.rows + r
+                grad_ref[start : start + stripe, at] = value.astype(BF)
+
+        def transform(n):
+            t, h = items[n]
+            at = slice(t * width, (t + 1) * width)
+            start = ms2 + h * plan.rows
+            value = dot_t(stack_ref[:ms2, at], grad_ref[start : start + plan.rows, at])
+            if t == 0:
+                acc[h] = value
+            else:
+                acc[h] += value
+
+        product(0)
+        for n in range(len(items)):
+            if n + 1 < len(items):
+                product(n + 1)
+            slope(n)
+            if n > 0:
+                transform(n - 1)
+        transform(len(items) - 1)
+        for half, out_ref in ((me, keep_ref), (1 - me, send_ref)):
+            pad_lanes(plan, out_ref)
+            out_ref[:, : plan.rows] = acc[half].astype(BF)
+        table.wait()
+
+    out = (ms2, plan.rows_pad)
+    return pl.pallas_call(
+        kernel,
+        in_specs=[SCALAR, WHOLE, WHOLE, ANYWHERE, WHOLE, WHOLE, ANYWHERE],
+        out_specs=[WHOLE] * 3,
+        out_shape=[pltpu.VMEM((deep, plan.plane), BF), shape(out), shape(out)],
+        scratch_shapes=[
+            pltpu.VMEM((2, plan.rows, deep), BF),
+            pltpu.VMEM((2, plan.rows, width), F32),
+            pltpu.VMEM((2, ms2, plan.rows), F32),
+            pltpu.VMEM((2, plan.rows, plan.plane), BF),
+            pltpu.SemaphoreType.DMA((len(items) + 1,)),
+        ],
         compiler_params=params(),
         cost_estimate=cost(6e9, 1e7),
         name="cells_forward",
-    )(me, own, got, plane, mixing, field.reshape(2 * plan.rows, plan.plane), cotangent.reshape(cells))
-
-
-def cells_back(plan, me, own, got, plane, mixing, grad):
-    tiles = 4
+    )(me, own, got, hbm(plane), vmem(mixing), vmem(stack), hbm(cotangent.reshape(2, plan.rows, plan.plane)))
+
+
+def cells_back(plan, me, own, got, mixing, grads):
+    tiles = 2
     width = plan.plane // tiles
-
-    def kernel(me_ref, own_ref, got_ref, plane_ref, mix_ref, grad_ref, out_ref):
-        me = me_ref[0]
-        ms = plan.ms
-        for half, in_ref in ((me, own_ref), (1 - me, got_ref)):
-            spectral = dot(in_ref[0], plane_ref[:ms]) + dot(in_ref[1], plane_ref[ms:])
-            mixed = dot(mix_ref[0, half], grad_ref[...])
-            out_ref[half] = (spectral * plan.scale + mixed).astype(BF)
-
-    side = (2, plan.rows, plan.ms)
+    ms2 = 2 * plan.ms
+    deep = ms2 + 2 * plan.rows
+    items = [(t, h) for t in range(tiles) for h in (0, 1)]
+
+    def kernel(me_ref, own_ref, got_ref, mix_ref, grad_ref, out_ref, lhs, held, sems):
+        fill_lhs(plan, me_ref[0], lhs, own_ref, got_ref, mix_ref)
+        copies = []
+        for n, (t, h) in enumerate(items):
+            at = slice(t * width, (t + 1) * width)
+            held[h, :, at] = dot(lhs[h], grad_ref[:, at]).astype(BF)
+            copies.append(pltpu.make_async_copy(held.at[h, :, at], out_ref.at[h, :, at], sems.at[n]))
+            copies[-1].start()
+        for copy in copies:
+            copy.wait()
+
     cells = (2, plan.rows, plan.plane)
     return pl.pallas_call(
         kernel,
-        grid_spec=pltpu.PrefetchScalarGridSpec(
-            num_scalar_prefetch=1,
-            grid=(tiles,),
-            in_specs=[
-                full(side),
-                full(side),
-                pl.BlockSpec((2 * plan.ms, width), lambda t, j: (0, t)),
-                pl.BlockSpec((1, 2, plan.rows, 2 * plan.rows), lambda t, j: (1, 0, 0, 0)),
-                pl.BlockSpec((2 * plan.rows, width), lambda t, j: (0, t)),
-            ],
-            out_specs=pl.BlockSpec((2, plan.rows, width), lambda t, j: (0, 0, t)),
-        ),
+        in_specs=[SCALAR, WHOLE, WHOLE, WHOLE, WHOLE],
+        out_specs=ANYWHERE,
         out_shape=shape(cells),
+        scratch_shapes=[
+            pltpu.VMEM((2, plan.rows, deep), BF),
+            pltpu.VMEM(cells, BF),
+            pltpu.SemaphoreType.DMA((len(items),)),
+        ],
         compiler_params=params(),
         cost_estimate=cost(4e9, 8e6),
         name="cells_back",
-    )(me, own, got, plane, mixing, grad.reshape(2 * plan.rows, plan.plane))
+    )(me, own, got, vmem(mixing), vmem(grads))
 
 
 def pack_tables(plan):
@@ -562,100 +627,89 @@
     return pick, place.astype(ml_dtypes.bfloat16)
 
 
-def mix_partial(plan, field, grad):
-    tiles = 4
-    width = plan.plane // tiles
+def mix_partial(plan, stack, grads):
     cells = 2 * plan.rows
+    ms2 = 2 * plan.ms
     pick, place = pack_tables(plan)
     factor = 1.0 / math.sqrt(plan.count)
 
     def kernel(field_ref, grad_ref, pick_ref, place_ref, out_ref, acc):
+        acc[...] = dot_t(field_ref[ms2:, :], grad_ref[ms2:, :])
+        row = lax.broadcasted_iota(jnp.int32, (plan.xz, cells), 0)
+        col = lax.broadcasted_iota(jnp.int32, (plan.xz, cells), 1) % plan.xz
+        same = row == col
+        lines = []
+        for c in range(plan.chans):
+            part = jnp.where(same, acc[c * plan.xz : (c + 1) * plan.xz, :], 0.0)
+            lines.append(jnp.sum(part, 0, keepdims=True))
+        sums = jnp.concatenate(lines, 0) * factor
+        high = sums.astype(BF)
+        low = (sums - high.astype(F32)).astype(BF)
+        total = jnp.zeros((MIX_ROWS, LANES), F32)
+        for k in range(plan.chans // MIX_ROWS):
+            spread = dot(high, place_ref[k]) + dot(low, place_ref[k])
+            total += lax.dot_general(
+                pick_ref[k], spread, (((1,), (0,)), ((), ())),
+                precision=lax.Precision.HIGHEST, preferred_element_type=F32,
+            )
+        out_ref[...] = total
+
+    return pl.pallas_call(
+        kernel,
+        in_specs=[WHOLE] * 4,
+        out_specs=WHOLE,
+        scratch_shapes=[pltpu.VMEM((cells, cells), F32)],
+        out_shape=shape((MIX_ROWS, LANES), F32),
+        compiler_params=params(),
+        cost_estimate=cost(4e9, 6e6),
+        name="mix_partial",
+    )(vmem(stack), vmem(grads), pick, place)
+
+
+def weight_grad(plan, me, field_own, field_got, grad_own, grad_got):
+    chans, half = plan.chans, plan.half
+    block = 2
+
+    def kernel(me_ref, fo_ref, fg_ref, go_ref, gg_ref, out_ref, plain, turned, real, imag):
+        me = me_ref[0]
         step = pl.program_id(0)
-        value = dot_t(field_ref[...], grad_ref[...])
 
         @pl.when(step == 0)
         def _():
-            acc[...] = value
-
-        @pl.when(step > 0)
-        def _():
-            acc[...] += value
-
-        @pl.when(step == tiles - 1)
-        def _():
-            row = lax.broadcasted_iota(jnp.int32, (plan.xz, cells), 0)
-            col = lax.broadcasted_iota(jnp.int32, (plan.xz, cells), 1) % plan.xz
-            same = row == col
-            lines = []
-            for c in range(plan.chans):
-                part = jnp.where(same, acc[c * plan.xz : (c + 1) * plan.xz, :], 0.0)
-                lines.append(jnp.sum(part, 0, keepdims=True))
-            sums = jnp.concatenate(lines, 0) * factor
-            high = sums.astype(BF)
-            low = (sums - high.astype(F32)).astype(BF)
-            total = jnp.zeros((MIX_ROWS, LANES), F32)
-            for k in range(plan.chans // MIX_ROWS):
-                spread = dot(high, place_ref[k]) + dot(low, place_ref[k])
-                total += lax.dot_general(
-                    pick_ref[k], spread, (((1,), (0,)), ((), ())),
-                    precision=lax.Precision.HIGHEST, preferred_element_type=F32,
-                )
-            out_ref[...] = total
-
-    tile = pl.BlockSpec((cells, width), lambda t: (0, t))
-    return pl.pallas_call(
-        kernel,
-        grid=(tiles,),
-        in_specs=[tile, tile, full(pick.shape), full(place.shape)],
-        out_specs=full((MIX_ROWS, LANES)),
-        scratch_shapes=[pltpu.VMEM((cells, cells), F32)],
-        out_shape=shape((MIX_ROWS, LANES), F32),
-        compiler_params=params(),
-        cost_estimate=cost(4e9, 6e6),
-        name="mix_partial",
-    )(field.reshape(cells, plan.plane), grad.reshape(cells, plan.plane), pick, place)
-
-
-def weight_grad(plan, me, field_own, field_got, grad_own, grad_got):
-    chans, half = plan.chans, plan.half
-
-    def kernel(me_ref, fo_ref, fg_ref, go_ref, gg_ref, out_ref, held, line):
-        me = me_ref[0]
-        step = pl.program_id(0)
-
-        @pl.when(step == 0)
-        def _():
-            held[me] = go_ref[...].astype(F32)
-            held[1 - me] = gg_ref[...].astype(F32)
-
-        @pl.when(step < half)
-        def _():
-            line[...] = fo_ref[step % half].astype(F32) * plan.scale
-
-        @pl.when(step >= half)
-        def _():
-            line[...] = fg_ref[step % half].astype(F32) * plan.scale
-
-        vr, vi = line[0], line[1]
-        for o in range(chans):
-            dr = held[o // half, o % half, 0]
-            di = held[o // half, o % half, 1]
-            out_ref[0, 0, o] = vr * dr + vi * di
-            out_ref[1, 0, o] = vr * di - vi * dr
+            for core, ref in ((me, go_ref), (1 - me, gg_ref)):
+                for o in range(half):
+                    r, i = ref[o, 0].astype(F32), ref[o, 1].astype(F32)
+                    plain[core, o, :, 0, :] = r
+                    plain[core, o, :, 1, :] = i
+                    turned[core, o, :, 0, :] = i
+                    turned[core, o, :, 1, :] = r
+            for core, ref in ((me, fo_ref), (1 - me, fg_ref)):
+                for c in range(half):
+                    r, i = ref[c, 0].astype(F32) * plan.scale, ref[c, 1].astype(F32) * plan.scale
+                    real[core, c, :, 0, :] = r
+                    real[core, c, :, 1, :] = r
+                    imag[core, c, :, 0, :] = i
+                    imag[core, c, :, 1, :] = -i
+
+        for k in range(block):
+            c = step * block + k
+            core = (c >= half).astype(jnp.int32)
+            vr, vi = real[core, c - core * half], imag[core, c - core * half]
+            for o in range(chans):
+                out_ref[k, o] = vr * plain[o // half, o % half] + vi * turned[o // half, o % half]
 
     side = (half, 2, plan.s, plan.modes)
+    held = pltpu.VMEM((2, half, plan.s, 2, plan.modes), F32)
     return pl.pallas_call(
         kernel,
         grid_spec=pltpu.PrefetchScalarGridSpec(
             num_scalar_prefetch=1,
-            grid=(chans,),
+            grid=(chans // block,),
             in_specs=[full(side)] * 4,
-            out_specs=pl.BlockSpec(
-                (2, 1, chans, plan.s, plan.modes), lambda t, j: (0, (j[0] * half + t) % chans, 0, 0, 0)
-            ),
-            scratch_shapes=[pltpu.VMEM((2,) + side, F32), pltpu.VMEM(side[1:], F32)],
+            out_specs=pl.BlockSpec((block, chans, plan.s, 2, plan.modes), lambda t, j: (t, 0, 0, 0, 0)),
+            scratch_shapes=[held] * 4,
         ),
-        out_shape=shape((2, chans, chans, plan.s, plan.modes), F32),
+        out_shape=shape((chans, chans, plan.s, 2, plan.modes), F32),
         compiler_params=params(),
         cost_estimate=cost(8e9, 1.3e7),
         name="weight_grad",
@@ -667,7 +721,6 @@
     const = {name: jnp.asarray(value) for name, value in plan.tables().items()}
     core = lax.axis_index("gz").astype(jnp.int32)
     me = core.reshape(1)
-    other = (1 - core).reshape(1)
     plane = const["plane"]
 
     def swap(value):
@@ -676,39 +729,40 @@
     def spread(chunks):
         return lax.all_to_all(chunks, "gx", split_axis=0, concat_axis=0, tiled=True)
 
-    def to_modes(keep, got):
+    def to_modes(keep, got, beside):
         chunks = spread(z_forward(plan, me, keep, got, const["z_forward"]))
+        chunks, beside = lax.optimization_barrier((chunks, beside))
         send, own = x_forward(plan, me, chunks, const["x_forward"])
-        return own, swap(send)
-
-    def product(own, got, adjoint):
-        send = mode_product(plan, me, other, spec_weight, own, got, adjoint)
-        keep = mode_product(plan, me, me, spec_weight, own, got, adjoint)
+        return own, swap(send), beside
+
+    def product(weight, own, got, adjoint):
+        send = mode_product(plan, me, False, weight, own, got, adjoint)
+        keep = mode_product(plan, me, True, weight, own, got, adjoint)
         return keep, swap(send)
 
-    def to_cells(keep, got, mix):
+    def to_cells(keep, got, mix, beside):
         chunks = spread(x_inverse(plan, me, keep, got, const["x_inverse"], mix))
+        chunks, beside = lax.optimization_barrier((chunks, beside))
         outs = z_inverse(plan, me, chunks, const["z_inverse"], mix is not None)
-        return outs[1], swap(outs[0]), outs[2:]
-
+        return outs[1], swap(outs[0]), outs[2:], beside
+
+    stack, send = load_forward(plan, me, field, plane)
+    got = swap(send)
+    keep = plane_forward(plan, me, stack)
     mixing = mix_blocks(plan, mix_weight, const["owner"])
-    send = plane_forward(plan, other, field, plane)
-    keep = plane_forward(plan, me, field, plane)
-    field_own, field_got = to_modes(keep, swap(send))
-    keep, got = product(field_own, field_got, False)
-    keep, got, _ = to_cells(keep, got, None)
-    grad, send, keep = cells_forward(plan, me, keep, got, plane, mixing, field, cotangent)
-    grad_own, grad_got = to_modes(keep, swap(send))
-    partial_mix = mix_partial(plan, field, grad)
+    weight = with_layout_constraint(spec_weight, Layout(major_to_minor=(0, 1, 2, 3, 4)))
+    field_own, field_got, (mixing, weight) = to_modes(keep, got, (mixing, weight))
+    keep, got = product(weight, field_own, field_got, False)
+    keep, got, _, _ = to_cells(keep, got, None, ())
+    grads, send, keep = cells_forward(plan, me, keep, got, plane, mixing[0], stack, cotangent)
+    partial_mix = mix_partial(plan, stack, grads)
+    grad_own, grad_got, partial_mix = to_modes(keep, swap(send), partial_mix)
     partial_mix = partial_mix + swap(partial_mix)
-    keep, got = product(grad_own, grad_got, True)
+    keep, got = product(weight, grad_own, grad_got, True)
     spec_grad = weight_grad(plan, me, field_own, field_got, grad_own, grad_got)
-    keep, got, mix = to_cells(keep, got, partial_mix)
-    field_grad = cells_back(plan, me, keep, got, plane, mixing, grad).reshape(field.shape)
-    per_row = plan.chans // MIX_ROWS
-    lane = LANES // per_row
-    mix_grad = mix[0][:, : per_row * lane].reshape(MIX_ROWS, per_row, lane)[:, :, : plan.chans]
-    return (field_grad, spec_grad, mix_grad.reshape(plan.chans, plan.chans))
+    keep, got, mix, spec_grad = to_cells(keep, got, partial_mix, spec_grad)
+    field_grad = cells_back(plan, me, keep, got, mixing[1], grads).reshape(field.shape)
+    return (field_grad, spec_grad.transpose(3, 0, 1, 2, 4), mix[0])
 
 
 def solution(mesh):

time: 135 us -> 117 us (0.87)
  blocking collectives: 52.2 us -> 14.4 us
  starting transfers between devices: 9.12 us -> 25.3 us
  waiting for transfers between devices: 2.88 us -> 7.26 us
  Pallas kernels: 44.8 us -> 42 us
  local copies, waits for them, and re-layouts: 24.6 us -> 26 us
    all_to_all x4 -> x1, blocking collectives: 52.2 us -> 14.4 us  [spread(): return lax.all_to_all(chunks, 'gx', split_axis=0, concat_axis=0, tiled=True)]
    all_to_all x0 -> x3, starting transfers between devices: none -> 17.3 us  [spread(): return lax.all_to_all(chunks, 'gx', split_axis=0, concat_axis=0, tiled=True)]
    pallas_call x10, Pallas kernels: 36.2 us -> 28.3 us  [the longest x1 9.8 us: cells_forward(): pl.pallas_call(kernel, in_specs=[SCALAR, WHOLE, WHOLE, ANYWHERE, WHOLE, W...]
    pallas_call x1, Pallas kernels: 3.63 us -> 7.04 us  [weight_grad(): pl.pallas_call(kernel, grid_spec=pltpu.PrefetchScalarGridSpec(num_scalar_...]
    unnamed x71 -> x48, local copies, waits for them, and re-layouts: 22.6 us -> 26 us
    ppermute x9, waiting for transfers between devices: 2.88 us -> 5.6 us  [swap(): return lax.ppermute(value, 'gz', [(0, 1), (1, 0)])]
    reshape x2 -> x0, local copies, waits for them, and re-layouts: 1.99 us -> none  [the longest x1 1.32 us: local(): return (field_grad, spec_grad, mix_grad.reshape(plan.chans, plan.chans))]
    all_to_all x0 -> x3, waiting for transfers between devices: none -> 1.66 us  [spread(): return lax.all_to_all(chunks, 'gx', split_axis=0, concat_axis=0, tiled=True)]
  transfers between devices with their start and end apart: 9 -> 12, of which waited for: 3 -> 6; matrix products, arithmetic and copies ran while one was open for 10% -> 6% of each run, Pallas kernels for 11% -> 14%
where the time goes in v1:
time: 117 us; the launch traced here: 116 us
  Pallas kernels  42 us (36%)
  local copies, waits for them, and re-layouts  26 us (22%)
  starting transfers between devices  25.3 us (22%)
  blocking collectives  14.4 us (12%)
  waiting for transfers between devices  7.26 us (6%)
    unnamed x48, local copies, waits for them, and re-layouts  26 us
    all_to_all x3, starting transfers between devices, spread(): return lax.all_to_all(chunks, 'gx', split_axis=0, concat_axis=0, tiled=True)  17.3 us
    all_to_all x1, blocking collectives, spread(): return lax.all_to_all(chunks, 'gx', split_axis=0, concat_axis=0, tiled=True)  14.4 us
    pallas_call x1, Pallas kernels, cells_forward(): pl.pallas_call(kernel, in_specs=[SCALAR, WHOLE, WHOLE, ANYWHERE, WHOLE, W...  9.8 us
    ppermute x9, starting transfers between devices, swap(): return lax.ppermute(value, 'gz', [(0, 1), (1, 0)])  8.03 us
    pallas_call x1, Pallas kernels, weight_grad(): pl.pallas_call(kernel, grid_spec=pltpu.PrefetchScalarGridSpec(num_scalar_...  7.04 us
    pallas_call x4, Pallas kernels, mode_product(): pl.pallas_call(kernel, in_specs=[SCALAR, WHOLE, WHOLE, WHOLE], out_specs=...  6.09 us
    ppermute x9, waiting for transfers between devices, swap(): return lax.ppermute(value, 'gz', [(0, 1), (1, 0)])  5.6 us
  transfers between devices with their start and end apart: 12, of which 6 were waited for; matrix products, arithmetic and copies ran while one was open for 6% of the time, Pallas kernels for 14%

profile of v1, /device:TPU:1, one launch (start us, length us, event | category | flops | bytes accessed | tf_op | source)
XLA Modules:
  0.0 116.1 jit_solution(17310944809275687172)
XLA Ops:
  0.6 2.8 %load_forward.1 = (bf16[1024,2048]{1,0:T(8,128)(2,1)S(1)}, bf16[384,384]{1,0:T(8,128)(2,1)S(1)}) custom-call(s32[1]{0:T(128)} %bitcast.me_ref._, bf16[2,320,2048]{2,1,0:T(8,128)(2,1)} %bitcast.7, bf16[384,2048]{1,0:T(8,128)(2,1)} %constant.20.clone.plane_ref), custom_call_target="tpu_custom_call" | custom-call | flops 503316480 | bytes 5000000 | tf_op jit(solution)/shard_map/load_forward/pallas_call | solution.py:200
  4.6 2.0 %copy-done.5 = bf16[1024,2048]{1,0:T(8,128)(2,1)} copy-done((bf16[1024,2048]{1,0:T(8,128)(2,1)}, bf16[1024,2048]{1,0:T(8,128)(2,1)S(1)}, u32[]{:S(2)}) %copy-start.5) | copy-done | bytes 4194328
  7.7 8.0 %all-to-all-start = ((bf16[16,64,128]{2,1,0:T(8,128)(2,1)}), bf16[16,64,128]{2,1,0:T(8,128)(2,1)S(1)}, u32[]{:S(2)}, u32[]{:S(2)}) async-start(bf16[16,64,128]{2,1,0:T(8,128)(2,1)} %z_forward.2), calls=%async_computation | async-start | bytes 524288 | tf_op jit(solution)/shard_map/all_to_all | solution.py:730
  15.9 6.7 %copy.16.weight_ref = bf16[2,20,20,12,192]{4,3,2,1,0:T(8,128)(2,1)} copy(bf16[2,20,20,12,192]{4,0,3,2,1:T(2,128)(2,1)} %param.14) | data formatting | bytes 7372800 | tf_op args[2]
  28.2 2.9 %copy-done.1 = bf16[2,20,20,12,192]{4,3,2,1,0:T(8,128)(2,1)S(1)} copy-done((bf16[2,20,20,12,192]{4,3,2,1,0:T(8,128)(2,1)S(1)}, bf16[2,20,20,12,192]{4,3,2,1,0:T(8,128)(2,1)}, u32[]{:S(2)}) %copy-start.1) | copy-done | bytes 3686424
  31.1 1.5 %mode_product.5 = bf16[10,2,12,192]{3,2,1,0:T(8,128)(2,1)S(1)} custom-call(s32[1]{0:T(128)} %bitcast.me_ref._, bf16[2,20,20,12,192]{4,3,2,1,0:T(8,128)(2,1)S(1)} %copy-done.1, bf16[10,2,12,192]{3,2,1,0:T(8,128)(2,1)S(1)} %get-tuple-element.33.own_ref.fo_ref, bf16[10,2,12,192]{3,2,1,0:T(8,128)(2,1)S(1)} %collective-permute-done.1.got_ref.fg_ref), custom_call_target="tpu_custom_call" | custom-call | flops 2000000000 | bytes 4000000 | tf_op jit(solution)/shard_map/mode_product/pallas_call | solution.py:337
  33.0 1.5 %mode_product.4.own_ref = bf16[10,2,12,192]{3,2,1,0:T(8,128)(2,1)S(1)} custom-call(s32[1]{0:T(128)} %bitcast.me_ref._, bf16[2,20,20,12,192]{4,3,2,1,0:T(8,128)(2,1)S(1)} %copy-done.1, bf16[10,2,12,192]{3,2,1,0:T(8,128)(2,1)S(1)} %get-tuple-element.33.own_ref.fo_ref, bf16[10,2,12,192]{3,2,1,0:T(8,128)(2,1)S(1)} %collective-permute-done.1.got_ref.fg_ref), custom_call_target="tpu_custom_call" | custom-call | flops 2000000000 | bytes 4000000 | tf_op jit(solution)/shard_map/mode_product/pallas_call | solution.py:337
  35.2 14.4 %all_to_all.20.in_ref = bf16[16,64,128]{2,1,0:T(8,128)(2,1)S(1)} all-to-all(bf16[16,64,128]{2,1,0:T(8,128)(2,1)S(1)} %x_inverse.2), channel_id=1, replica_groups=mesh['grp'=1,'gx'=16,'gz'=2] {'gx'}, dimensions={0} | all-to-all | bytes 524288 | tf_op jit(solution)/shard_map/all_to_all | solution.py:730
  50.1 2.0 %collective-permute-start.3 = (bf16[320,384]{1,0:T(8,128)(2,1)S(1)}, bf16[320,384]{1,0:T(8,128)(2,1)S(1)}, u32[]{:S(2)}, u32[]{:S(2)}) collective-permute-start(bf16[320,384]{1,0:T(8,128)(2,1)S(1)} %get-tuple-element.36), channel_id=1, source_target_pairs={{0,1},{1,0},{2,3},{3,2},{4,5},{5,4},{6,7},{7,6},{8,9},{9,8},{10,11... | collective-permute-start | bytes 737288 | tf_op jit(solution)/shard_map/ppermute | solution.py:727
  53.3 9.8 %cells_forward.1 = (bf16[1024,2048]{1,0:T(8,128)(2,1)S(1)}, bf16[384,384]{1,0:T(8,128)(2,1)S(1)}, bf16[384,384]{1,0:T(8,128)(2,1)S(1)}) custom-call(s32[1]{0:T(128)} %bitcast.me_ref._, bf16[320,384]{1,0:T(8,128)(2,1)S(1)} %get-tuple-element.35.own_ref, bf16[320,384]{1,0:T(8,128)(2,1)S(1)} %collective-permute-done.3.got_ref, ...), custom_call_target="tpu_custom_call" | custom-call | flops 6000000000 | bytes 10000000 | tf_op jit(solution)/shard_map/cells_forward/pallas_call | solution.py:563
  63.1 2.0 %copy-done.20 = bf16[1024,2048]{1,0:T(8,128)(2,1)} copy-done((bf16[1024,2048]{1,0:T(8,128)(2,1)}, bf16[1024,2048]{1,0:T(8,128)(2,1)S(1)}, u32[]{:S(2)}) %copy-start.20) | copy-done | bytes 4194328
  67.8 3.8 %all-to-all-start.2 = ((bf16[16,64,128]{2,1,0:T(8,128)(2,1)}), bf16[16,64,128]{2,1,0:T(8,128)(2,1)S(1)}, u32[]{:S(2)}, u32[]{:S(2)}) async-start(bf16[16,64,128]{2,1,0:T(8,128)(2,1)} %z_forward.3), calls=%async_computation.2 | async-start | bytes 524288 | tf_op jit(solution)/shard_map/all_to_all | solution.py:730
  71.6 2.2 %copy-done.7 = bf16[1024,2048]{1,0:T(8,128)(2,1)S(1)} copy-done((bf16[1024,2048]{1,0:T(8,128)(2,1)S(1)}, bf16[1024,2048]{1,0:T(8,128)(2,1)}, u32[]{:S(2)}) %copy-start.7) | copy-done | bytes 4194328
  74.9 2.2 %copy-done.21 = bf16[1024,2048]{1,0:T(8,128)(2,1)S(1)} copy-done((bf16[1024,2048]{1,0:T(8,128)(2,1)S(1)}, bf16[1024,2048]{1,0:T(8,128)(2,1)}, u32[]{:S(2)}) %copy-start.21) | copy-done | bytes 4194328
  77.1 3.7 %mix_partial.1 = f32[4,128]{1,0:T(4,128)S(1)} custom-call(bf16[1024,2048]{1,0:T(8,128)(2,1)S(1)} %copy-done.7, bf16[1024,2048]{1,0:T(8,128)(2,1)S(1)} %copy-done.21, f32[5,4,20]{2,1,0:T(4,128)S(1)} %copy-done.19, bf16[5,640,128]{2,1,0:T(8,128)(2,1)S(1)} %copy-done.16), custom_call_target="tpu_custom_call" | custom-call | flops 4000000000 | bytes 6000000 | tf_op jit(solution)/shard_map/mix_partial/pallas_call | solution.py:657
  83.9 2.9 %copy-done.2 = bf16[2,20,20,12,192]{4,3,2,1,0:T(8,128)(2,1)S(1)} copy-done((bf16[2,20,20,12,192]{4,3,2,1,0:T(8,128)(2,1)S(1)}, bf16[2,20,20,12,192]{4,3,2,1,0:T(8,128)(2,1)}, u32[]{:S(2)}) %copy-start.2) | copy-done | bytes 3686424
  86.7 1.5 %mode_product.7 = bf16[10,2,12,192]{3,2,1,0:T(8,128)(2,1)S(1)} custom-call(s32[1]{0:T(128)} %bitcast.me_ref._, bf16[2,20,20,12,192]{4,3,2,1,0:T(8,128)(2,1)S(1)} %copy-done.2, bf16[10,2,12,192]{3,2,1,0:T(8,128)(2,1)S(1)} %get-tuple-element.42.own_ref.go_ref, bf16[10,2,12,192]{3,2,1,0:T(8,128)(2,1)S(1)} %collective-permute-done.5.got_ref.gg_ref), custom_call_target="tpu_custom_call" | custom-call | flops 2000000000 | bytes 4000000 | tf_op jit(solution)/shard_map/mode_product/pallas_call | solution.py:337
  88.5 1.5 %mode_product.6.own_ref = bf16[10,2,12,192]{3,2,1,0:T(8,128)(2,1)S(1)} custom-call(s32[1]{0:T(128)} %bitcast.me_ref._, bf16[2,20,20,12,192]{4,3,2,1,0:T(8,128)(2,1)S(1)} %copy-done.2, bf16[10,2,12,192]{3,2,1,0:T(8,128)(2,1)S(1)} %get-tuple-element.42.own_ref.go_ref, bf16[10,2,12,192]{3,2,1,0:T(8,128)(2,1)S(1)} %collective-permute-done.5.got_ref.gg_ref), custom_call_target="tpu_custom_call" | custom-call | flops 2000000000 | bytes 4000000 | tf_op jit(solution)/shard_map/mode_product/pallas_call | solution.py:337
  91.4 5.5 %all-to-all-start.3 = ((bf16[16,64,128]{2,1,0:T(8,128)(2,1)}), bf16[16,64,128]{2,1,0:T(8,128)(2,1)S(1)}, u32[]{:S(2)}, u32[]{:S(2)}) async-start(bf16[16,64,128]{2,1,0:T(8,128)(2,1)} %x_inverse.3), calls=%async_computation.3 | async-start | bytes 524288 | tf_op jit(solution)/shard_map/all_to_all | solution.py:730
  96.9 7.0 %weight_grad.1 = f32[20,20,12,2,192]{4,3,2,1,0:T(2,128)} custom-call(s32[1]{0:T(128)} %bitcast.me_ref._, bf16[10,2,12,192]{3,2,1,0:T(8,128)(2,1)S(1)} %get-tuple-element.33.own_ref.fo_ref, bf16[10,2,12,192]{3,2,1,0:T(8,128)(2,1)S(1)} %collective-permute-done.1.got_ref.fg_ref, bf16[10,2,12,192]{3,2,1,0:T(8,128)(2,1)S(1)} %get-tuple-element.42.own_ref.go_ref, ...), custom_call_target="tpu_custom_call" | custom-call | flops 8000000000 | bytes 13000000 | tf_op jit(solution)/shard_map/weight_grad/pallas_call | solution.py:703
  103.9 1.7 %all-to-all-done.3.in_ref = bf16[16,64,128]{2,1,0:T(8,128)(2,1)S(1)} async-done(((bf16[16,64,128]{2,1,0:T(8,128)(2,1)}), bf16[16,64,128]{2,1,0:T(8,128)(2,1)S(1)}, u32[]{:S(2)}, u32[]{:S(2)}) %all-to-all-start.3) | async-done | bytes 262176 | tf_op jit(solution)/shard_map/all_to_all | solution.py:730
  106.7 2.1 %collective-permute-start.8 = (bf16[320,384]{1,0:T(8,128)(2,1)S(1)}, bf16[320,384]{1,0:T(8,128)(2,1)S(1)}, u32[]{:S(2)}, u32[]{:S(2)}) collective-permute-start(bf16[320,384]{1,0:T(8,128)(2,1)S(1)} %get-tuple-element.47), channel_id=1, source_target_pairs={{0,1},{1,0},{2,3},{3,2},{4,5},{5,4},{6,7},{7,6},{8,9},{9,8},{10,11... | collective-permute-start | bytes 737288 | tf_op jit(solution)/shard_map/ppermute | solution.py:727
  110.0 2.2 %copy-done.22 = bf16[1024,2048]{1,0:T(8,128)(2,1)S(1)} copy-done((bf16[1024,2048]{1,0:T(8,128)(2,1)S(1)}, bf16[1024,2048]{1,0:T(8,128)(2,1)}, u32[]{:S(2)}) %copy-start.22) | copy-done | bytes 4194328
  112.2 3.8 %cells_back.1 = bf16[2,320,2048]{2,1,0:T(8,128)(2,1)} custom-call(s32[1]{0:T(128)} %bitcast.me_ref._, bf16[320,384]{1,0:T(8,128)(2,1)S(1)} %get-tuple-element.46.own_ref, bf16[320,384]{1,0:T(8,128)(2,1)S(1)} %collective-permute-done.8.got_ref, bf16[2,320,640]{2,1,0:T(8,128)(2,1)S(1)} %copy-done.13, bf16[1024,2048]{1,0:T(8,128)(2,1)S(1)} %copy-done.22), custom_call_target="tpu_custom_call" | custom-call | flops 4000000000 | bytes 8000000 | tf_op jit(solution)/shard_map/cells_back/pallas_call | solution.py:600
  (69 shorter events, 21.3 us)
Async XLA Ops:
  3.5 3.1 %copy-start.8 = (bf16[2,512,256]{2,1,0:T(8,128)(2,1)S(1)}, bf16[2,512,256]{2,1,0:T(8,128)(2,1)}, u32[]{:S(2)}) copy-start(bf16[2,512,256]{2,1,0:T(8,128)(2,1)} %constant.21.clone.table_ref) | copy-start | bytes 1572868
  3.5 3.1 %collective-permute-start = (bf16[384,384]{1,0:T(8,128)(2,1)S(1)}, bf16[384,384]{1,0:T(8,128)(2,1)S(1)}, u32[]{:S(2)}, u32[]{:S(2)}) collective-permute-start(bf16[384,384]{1,0:T(8,128)(2,1)S(1)} %get-tuple-element.28), channel_id=1, source_target_pairs={{0,1},{1,0},{2,3},{3,2},{4,5},{5,4},{6,7},{7,6},{8,9},{9,8},{10,11... | collective-permute-start | bytes 884744 | tf_op jit(solution)/shard_map/ppermute | solution.py:727
  3.6 12.1 %copy-start.11 = (bf16[20,20]{1,0:T(8,128)(2,1)S(1)}, bf16[20,20]{1,0:T(8,128)(2,1)}, u32[]{:S(2)}) copy-start(bf16[20,20]{1,0:T(8,128)(2,1)} %back_ref.1) | copy-start | bytes 2404
  7.7 17.7 %all-to-all-start = ((bf16[16,64,128]{2,1,0:T(8,128)(2,1)}), bf16[16,64,128]{2,1,0:T(8,128)(2,1)S(1)}, u32[]{:S(2)}, u32[]{:S(2)}) async-start(bf16[16,64,128]{2,1,0:T(8,128)(2,1)} %z_forward.2), calls=%async_computation | async-start | bytes 524288 | tf_op jit(solution)/shard_map/all_to_all | solution.py:730
  15.9 6.7 %copy-start.9 = (bf16[640,20]{1,0:T(8,128)(2,1)S(1)}, bf16[640,20]{1,0:T(8,128)(2,1)}, u32[]{:S(2)}) copy-start(bf16[640,20]{1,0:T(8,128)(2,1)} %constant.25.clone.owner_ref) | copy-start | bytes 76804
  15.9 6.7 %copy-start.10 = (bf16[20,640]{1,0:T(8,128)(2,1)S(1)}, bf16[20,640]{1,0:T(8,128)(2,1)}, u32[]{:S(2)}) copy-start(bf16[20,640]{1,0:T(8,128)(2,1)} %constant.31.owner_t_ref) | copy-start | bytes 76804
  15.9 9.5 %copy-start = (bf16[2,2,1024,192]{3,2,1,0:T(8,128)(2,1)S(1)}, bf16[2,2,1024,192]{3,2,1,0:T(8,128)(2,1)}, u32[]{:S(2)}) copy-start(bf16[2,2,1024,192]{3,2,1,0:T(8,128)(2,1)} %constant.23.clone.table_ref) | copy-start | bytes 4718596
  25.9 2.3 %collective-permute-start.1 = (bf16[10,2,12,192]{3,2,1,0:T(8,128)(2,1)S(1)}, bf16[10,2,12,192]{3,2,1,0:T(8,128)(2,1)S(1)}, u32[]{:S(2)}, u32[]{:S(2)}) collective-permute-start(bf16[10,2,12,192]{3,2,1,0:T(8,128)(2,1)S(1)} %get-tuple-element.34), channel_id=1, source_target_pairs={{0,1},{1,0},{2,3},{3,2},{4,5},{5,4},{6,7},{7,6},{8,9},{9,8},{10,11... | collective-permute-start | bytes 276488 | tf_op jit(solution)/shard_map/ppermute | solution.py:727
  32.6 2.0 %collective-permute-start.2 = (bf16[10,2,12,192]{3,2,1,0:T(8,128)(2,1)S(1)}, bf16[10,2,12,192]{3,2,1,0:T(8,128)(2,1)S(1)}, u32[]{:S(2)}, u32[]{:S(2)}) collective-permute-start(bf16[10,2,12,192]{3,2,1,0:T(8,128)(2,1)S(1)} %mode_product.5), channel_id=1, source_target_pairs={{0,1},{1,0},{2,3},{3,2},{4,5},{5,4},{6,7},{7,6},{8,9},{9,8},{10,11... | collective-permute-start | bytes 276488 | tf_op jit(solution)/shard_map/ppermute | solution.py:727
  33.0 20.2 %copy-start.6 = (bf16[1024,2048]{1,0:T(8,128)(2,1)S(1)}, bf16[1024,2048]{1,0:T(8,128)(2,1)}, u32[]{:S(2)}) copy-start(bf16[1024,2048]{1,0:T(8,128)(2,1)} %copy-done.5) | copy-start | bytes 12582916
  34.6 15.0 %copy-start.17 = (bf16[2,512,256]{2,1,0:T(8,128)(2,1)S(1)}, bf16[2,512,256]{2,1,0:T(8,128)(2,1)}, u32[]{:S(2)}) copy-start(bf16[2,512,256]{2,1,0:T(8,128)(2,1)} %constant.22.clone.table_ref) | copy-start | bytes 1572868
  34.6 18.7 %copy-start.15 = (bf16[2,320,640]{2,1,0:T(8,128)(2,1)S(1)}, bf16[2,320,640]{2,1,0:T(8,128)(2,1)}, u32[]{:S(2)}) copy-start(bf16[2,320,640]{2,1,0:T(8,128)(2,1)} %copy-done.14) | copy-start | bytes 2457604
  50.1 3.2 %collective-permute-start.3 = (bf16[320,384]{1,0:T(8,128)(2,1)S(1)}, bf16[320,384]{1,0:T(8,128)(2,1)S(1)}, u32[]{:S(2)}, u32[]{:S(2)}) collective-permute-start(bf16[320,384]{1,0:T(8,128)(2,1)S(1)} %get-tuple-element.36), channel_id=1, source_target_pairs={{0,1},{1,0},{2,3},{3,2},{4,5},{5,4},{6,7},{7,6},{8,9},{9,8},{10,11... | collective-permute-start | bytes 737288 | tf_op jit(solution)/shard_map/ppermute | solution.py:727
  53.3 18.3 %copy-start.19 = (f32[5,4,20]{2,1,0:T(4,128)S(1)}, f32[5,4,20]{2,1,0:T(4,128)}, u32[]{:S(2)}) copy-start(f32[5,4,20]{2,1,0:T(4,128)} %constant.26.clone.pick_ref) | copy-start | bytes 4804
  65.1 1.6 %collective-permute-start.4 = (bf16[384,384]{1,0:T(8,128)(2,1)S(1)}, bf16[384,384]{1,0:T(8,128)(2,1)S(1)}, u32[]{:S(2)}, u32[]{:S(2)}) collective-permute-start(bf16[384,384]{1,0:T(8,128)(2,1)S(1)} %get-tuple-element.39), channel_id=1, source_target_pairs={{0,1},{1,0},{2,3},{3,2},{4,5},{5,4},{6,7},{7,6},{8,9},{9,8},{10,11... | collective-permute-start | bytes 884744 | tf_op jit(solution)/shard_map/ppermute | solution.py:727
  67.8 13.0 %all-to-all-start.2 = ((bf16[16,64,128]{2,1,0:T(8,128)(2,1)}), bf16[16,64,128]{2,1,0:T(8,128)(2,1)S(1)}, u32[]{:S(2)}, u32[]{:S(2)}) async-start(bf16[16,64,128]{2,1,0:T(8,128)(2,1)} %z_forward.3), calls=%async_computation.2 | async-start | bytes 524288 | tf_op jit(solution)/shard_map/all_to_all | solution.py:730
  81.4 2.5 %collective-permute-start.5 = (bf16[10,2,12,192]{3,2,1,0:T(8,128)(2,1)S(1)}, bf16[10,2,12,192]{3,2,1,0:T(8,128)(2,1)S(1)}, u32[]{:S(2)}, u32[]{:S(2)}) collective-permute-start(bf16[10,2,12,192]{3,2,1,0:T(8,128)(2,1)S(1)} %get-tuple-element.43), channel_id=1, source_target_pairs={{0,1},{1,0},{2,3},{3,2},{4,5},{5,4},{6,7},{7,6},{8,9},{9,8},{10,11... | collective-permute-start | bytes 276488 | tf_op jit(solution)/shard_map/ppermute | solution.py:727
  82.7 1.2 collective-permute-start.7
  83.9 2.9 %copy-start.2 = (bf16[2,20,20,12,192]{4,3,2,1,0:T(8,128)(2,1)S(1)}, bf16[2,20,20,12,192]{4,3,2,1,0:T(8,128)(2,1)}, u32[]{:S(2)}) copy-start(bf16[2,20,20,12,192]{4,3,2,1,0:T(8,128)(2,1)} %copy.16.weight_ref) | copy-start | bytes 11059204
  88.2 1.8 %collective-permute-start.6 = (bf16[10,2,12,192]{3,2,1,0:T(8,128)(2,1)S(1)}, bf16[10,2,12,192]{3,2,1,0:T(8,128)(2,1)S(1)}, u32[]{:S(2)}, u32[]{:S(2)}) collective-permute-start(bf16[10,2,12,192]{3,2,1,0:T(8,128)(2,1)S(1)} %mode_product.7), channel_id=1, source_target_pairs={{0,1},{1,0},{2,3},{3,2},{4,5},{5,4},{6,7},{7,6},{8,9},{9,8},{10,11... | collective-permute-start | bytes 276488 | tf_op jit(solution)/shard_map/ppermute | solution.py:727
  91.4 14.2 %all-to-all-start.3 = ((bf16[16,64,128]{2,1,0:T(8,128)(2,1)}), bf16[16,64,128]{2,1,0:T(8,128)(2,1)S(1)}, u32[]{:S(2)}, u32[]{:S(2)}) async-start(bf16[16,64,128]{2,1,0:T(8,128)(2,1)} %x_inverse.3), calls=%async_computation.3 | async-start | bytes 524288 | tf_op jit(solution)/shard_map/all_to_all | solution.py:730
  96.9 8.7 %copy-start.18 = (bf16[2,512,256]{2,1,0:T(8,128)(2,1)S(1)}, bf16[2,512,256]{2,1,0:T(8,128)(2,1)}, u32[]{:S(2)}) copy-start(bf16[2,512,256]{2,1,0:T(8,128)(2,1)} %constant.22.clone.table_ref) | copy-start | bytes 1572868
  96.9 13.1 %copy-start.13 = (bf16[2,320,640]{2,1,0:T(8,128)(2,1)S(1)}, bf16[2,320,640]{2,1,0:T(8,128)(2,1)}, u32[]{:S(2)}) copy-start(bf16[2,320,640]{2,1,0:T(8,128)(2,1)} %copy-done.12) | copy-start | bytes 2457604
  106.7 3.2 %collective-permute-start.8 = (bf16[320,384]{1,0:T(8,128)(2,1)S(1)}, bf16[320,384]{1,0:T(8,128)(2,1)S(1)}, u32[]{:S(2)}, u32[]{:S(2)}) collective-permute-start(bf16[320,384]{1,0:T(8,128)(2,1)S(1)} %get-tuple-element.47), channel_id=1, source_target_pairs={{0,1},{1,0},{2,3},{3,2},{4,5},{5,4},{6,7},{7,6},{8,9},{9,8},{10,11... | collective-permute-start | bytes 737288 | tf_op jit(solution)/shard_map/ppermute | solution.py:727
  (11 other events, 20.2 us)

commit v2 on v1

--- a/solution.py
+++ b/solution.py
@@ -157,12 +157,28 @@
     return pl.ds(pl.multiple_of(2 * plan.ms + half * plan.rows, math.gcd(2 * plan.ms, plan.rows)), plan.rows)
 
 
-def load_forward(plan, me, field, plane):
+def mix_matrix(plan, mix, back, out_ref):
+    cells = 2 * plan.rows
+    iota = lambda dims, axis: lax.broadcasted_iota(jnp.int32, dims, axis)
+    one_hot = lambda hit: hit.astype(F32).astype(BF)
+    owner = one_hot(iota((cells, plan.chans), 0) // plan.xz == iota((cells, plan.chans), 1))
+    owned = one_hot(iota((plan.chans, cells), 1) // plan.xz == iota((plan.chans, cells), 0))
+    spread = (dot if back else dot_t)(owner, mix).astype(BF)
+    same = iota((plan.rows, cells), 0) % plan.xz == iota((plan.rows, cells), 1) % plan.xz
+    for h in (0, 1):
+        wide = dot(spread[h * plan.rows : (h + 1) * plan.rows], owned)
+        out_ref[h] = jnp.where(same, wide, 0.0).astype(BF)
+
+
+def load_forward(plan, me, field, plane, mix):
     tiles = 4
     width = plan.plane // tiles
     ms2 = 2 * plan.ms
-
-    def kernel(me_ref, field_ref, plane_ref, stack_ref, out_ref, acc, sems):
+    cells = 2 * plan.rows
+
+    def kernel(
+        me_ref, field_ref, plane_ref, mix_ref, stack_ref, out_ref, mixing_ref, acc, small, sems, mix_sem,
+    ):
         me = me_ref[0]
         copies = []
         for k in range(tiles):
@@ -178,11 +194,15 @@
                     ),
                 )
             )
+        mix_load = pltpu.make_async_copy(mix_ref, small, mix_sem)
+        mix_load.start()
         for group in copies:
             group[0].start()
             group[1].start()
         for group in copies:
             group[2].start()
+        mix_load.wait()
+        mix_matrix(plan, small[...], False, mixing_ref)
         for k, group in enumerate(copies):
             at = slice(k * width, (k + 1) * width)
             group[0].wait()
@@ -197,16 +217,22 @@
         for group in copies:
             group[2].wait()
 
-    return pl.pallas_call(
-        kernel,
-        in_specs=[SCALAR, ANYWHERE, ANYWHERE],
-        out_specs=[WHOLE, WHOLE],
-        out_shape=[pltpu.VMEM((ms2 + 2 * plan.rows, plan.plane), BF), shape((ms2, plan.rows_pad))],
-        scratch_shapes=[pltpu.VMEM((ms2, plan.rows), F32), pltpu.SemaphoreType.DMA((3, tiles))],
+    matrix = pltpu.VMEM((2, plan.rows, cells), BF)
+    return pl.pallas_call(
+        kernel,
+        in_specs=[SCALAR, ANYWHERE, ANYWHERE, ANYWHERE],
+        out_specs=[WHOLE, WHOLE, WHOLE],
+        out_shape=[pltpu.VMEM((ms2 + cells, plan.plane), BF), shape((ms2, plan.rows_pad)), matrix],
+        scratch_shapes=[
+            pltpu.VMEM((ms2, plan.rows), F32),
+            pltpu.VMEM((plan.chans, plan.chans), BF),
+            pltpu.SemaphoreType.DMA((3, tiles)),
+            pltpu.SemaphoreType.DMA,
+        ],
         compiler_params=params(),
         cost_estimate=cost(4 * plan.ms * plan.rows * plan.plane, 5e6),
         name="load_forward",
-    )(me, hbm(field.reshape(2, plan.rows, plan.plane)), hbm(plane))
+    )(me, hbm(field.reshape(2, plan.rows, plan.plane)), hbm(plane), hbm(mix))
 
 
 def plane_forward(plan, me, stack):
@@ -305,45 +331,106 @@
     )(me, chunks, table)
 
 
-def mode_product(plan, me, mine, weight, own, got, adjoint):
-    def kernel(me_ref, weight_ref, own_ref, got_ref, out_ref, held):
-        me = me_ref[0]
+def mode_sums(plan, weight_ref, held, out_ref, adjoint, arrive, start=0):
+    def one(k, carry):
+        arrive(k)
+        real = jnp.zeros((plan.s, plan.modes), F32)
+        imag = jnp.zeros((plan.s, plan.modes), F32)
+        for c in range(plan.chans):
+            pos = (start + k, c) if adjoint else (c, start + k)
+            wr = weight_ref[0, pos[0], pos[1]].astype(F32)
+            wi = weight_ref[1, pos[0], pos[1]].astype(F32)
+            mr = held[c // plan.half, c % plan.half, 0]
+            mi = held[c // plan.half, c % plan.half, 1]
+            if adjoint:
+                real += wr * mr + wi * mi
+                imag += wr * mi - wi * mr
+            else:
+                real += wr * mr - wi * mi
+                imag += wr * mi + wi * mr
+        out_ref[k, 0] = real.astype(BF)
+        out_ref[k, 1] = imag.astype(BF)
+        return carry
+
+    lax.fori_loop(0, plan.half, one, 0)
+
+
+def mode_product(plan, me, weight, own, got, adjoint):
+    side = (plan.half, 2, plan.s, plan.modes)
+    if adjoint:
+        part = (2, plan.half, plan.chans, plan.s, plan.modes)
+    else:
+        part = (2, plan.chans, plan.half, plan.s, plan.modes)
+    held = pltpu.VMEM((2,) + side, F32)
+
+    def hold(me, held, own_ref, got_ref):
         held[me] = own_ref[...].astype(F32)
         held[1 - me] = got_ref[...].astype(F32)
-        first = (me if mine else 1 - me) * plan.half
-
-        def one(k, carry):
-            real = jnp.zeros((plan.s, plan.modes), F32)
-            imag = jnp.zeros((plan.s, plan.modes), F32)
-            for c in range(plan.chans):
-                pos = (first + k, c) if adjoint else (c, first + k)
-                wr = weight_ref[0, pos[0], pos[1]].astype(F32)
-                wi = weight_ref[1, pos[0], pos[1]].astype(F32)
-                mr = held[c // plan.half, c % plan.half, 0]
-                mi = held[c // plan.half, c % plan.half, 1]
-                if adjoint:
-                    real += wr * mr + wi * mi
-                    imag += wr * mi - wi * mr
-                else:
-                    real += wr * mr - wi * mi
-                    imag += wr * mi + wi * mr
-            out_ref[k, 0] = real.astype(BF)
-            out_ref[k, 1] = imag.astype(BF)
-            return carry
-
-        lax.fori_loop(0, plan.half, one, 0)
-
-    side = (plan.half, 2, plan.s, plan.modes)
-    return pl.pallas_call(
-        kernel,
+
+    def first(me_ref, weight_ref, own_ref, got_ref, out_ref, rest_ref, held, part_ref, sems):
+        me = me_ref[0]
+
+        def copy(k, half, to, sem):
+            if adjoint:
+                return pltpu.make_async_copy(weight_ref.at[:, half * plan.half + k], to.at[:, k], sem)
+            return pltpu.make_async_copy(weight_ref.at[:, :, half * plan.half + k], to.at[:, :, k], sem)
+
+        for k in range(plan.half):
+            copy(k, 1 - me, part_ref, sems.at[0, k]).start()
+        for k in range(plan.half):
+            copy(k, me, rest_ref, sems.at[1, k]).start()
+        hold(me, held, own_ref, got_ref)
+        arrive = lambda k: copy(k, 1 - me, part_ref, sems.at[0, k]).wait()
+        mode_sums(plan, part_ref, held, out_ref, adjoint, arrive)
+        for k in range(plan.half):
+            copy(k, me, rest_ref, sems.at[1, k]).wait()
+
+    def second(me_ref, weight_ref, own_ref, got_ref, out_ref, held):
+        hold(me_ref[0], held, own_ref, got_ref)
+        mode_sums(plan, weight_ref, held, out_ref, adjoint, lambda k: None)
+
+    def resident(mine, me_ref, weight_ref, own_ref, got_ref, out_ref, held):
+        me = me_ref[0]
+        hold(me, held, own_ref, got_ref)
+        start = (me if mine else 1 - me) * plan.half
+        mode_sums(plan, weight_ref, held, out_ref, adjoint, lambda k: None, start)
+
+    if not adjoint:
+        return [
+            pl.pallas_call(
+                functools.partial(resident, mine),
+                in_specs=[SCALAR, WHOLE, WHOLE, WHOLE],
+                out_specs=WHOLE,
+                out_shape=shape(side),
+                scratch_shapes=[held],
+                compiler_params=params(),
+                cost_estimate=cost(2e9, 4e6),
+                name="mode_product",
+            )(me, vmem(weight), own, got)
+            for mine in (False, True)
+        ]
+
+    send, rest = pl.pallas_call(
+        first,
+        in_specs=[SCALAR, ANYWHERE, WHOLE, WHOLE],
+        out_specs=[WHOLE, WHOLE],
+        out_shape=[shape(side), pltpu.VMEM(part, BF)],
+        scratch_shapes=[held, pltpu.VMEM(part, BF), pltpu.SemaphoreType.DMA((2, plan.half))],
+        compiler_params=params(),
+        cost_estimate=cost(2e9, 6e6),
+        name="mode_product_send",
+    )(me, hbm(weight), own, got)
+    keep = pl.pallas_call(
+        second,
         in_specs=[SCALAR, WHOLE, WHOLE, WHOLE],
         out_specs=WHOLE,
         out_shape=shape(side),
-        scratch_shapes=[pltpu.VMEM((2,) + side, F32)],
+        scratch_shapes=[held],
         compiler_params=params(),
         cost_estimate=cost(2e9, 4e6),
-        name="mode_product",
-    )(me, vmem(weight), own, got)
+        name="mode_product_keep",
+    )(me, vmem(rest), own, got)
+    return send, keep
 
 
 def x_inverse(plan, me, own, got, table, mix):
@@ -426,18 +513,19 @@
             total = pieces[0, plan.used : plan.used + MIX_ROWS, :]
             for i in range(1, plan.xp):
                 total = total + pieces[i, plan.used : plan.used + MIX_ROWS, :]
-            per_row = plan.chans // MIX_ROWS
-            lane = LANES // per_row
-            for c in range(plan.chans):
-                row, start = c // per_row, (c % per_row) * lane
-                mix_ref[c : c + 1, :] = total[row : row + 1, start : start + plan.chans]
+            mix_ref[...] = total
+            high = total.astype(BF).astype(F32)
+            fill = jnp.zeros((16 - 2 * MIX_ROWS, LANES), F32)
+            send_ref[plan.rows :, :] = jnp.zeros((16, 2 * ms), BF)
+            send_ref[plan.rows :, :LANES] = jnp.concatenate([high, total - high, fill], 0).astype(BF)
 
     out = (plan.rows, 2 * plan.ms)
-    outs = [out, out]
-    out_shape = [shape(out), shape(out)]
+    sent = (plan.rows + 16, 2 * plan.ms) if carry else out
+    outs = [sent, out]
+    out_shape = [shape(sent), shape(out)]
     if carry:
-        outs.append((plan.chans, plan.chans))
-        out_shape.append(shape((plan.chans, plan.chans), F32))
+        outs.append((MIX_ROWS, LANES))
+        out_shape.append(shape((MIX_ROWS, LANES), F32))
     return pl.pallas_call(
         kernel,
         grid_spec=pltpu.PrefetchScalarGridSpec(
@@ -460,26 +548,16 @@
     )(me, chunks, table)
 
 
-def mix_blocks(plan, mix, owner):
-    cells = 2 * plan.rows
-
-    def kernel(mix_ref, back_ref, owner_ref, owner_t_ref, *outs):
-        row = lax.broadcasted_iota(jnp.int32, (plan.rows, cells), 0) % plan.xz
-        col = lax.broadcasted_iota(jnp.int32, (plan.rows, cells), 1) % plan.xz
-        same = row == col
-        for out_ref, ref in zip(outs, (mix_ref, back_ref)):
-            for h in (0, 1):
-                spread = dot(owner_ref[h * plan.rows : (h + 1) * plan.rows, :], ref[...]).astype(BF)
-                wide = dot(spread, owner_t_ref[...])
-                out_ref[h] = jnp.where(same, wide, 0.0).astype(BF)
-
-    return pl.pallas_call(
-        kernel,
-        out_shape=[pltpu.VMEM((2, plan.rows, cells), BF)] * 2,
-        compiler_params=params(),
-        cost_estimate=cost(4e7, 2e6),
-        name="mix_blocks",
-    )(mix.T, mix, owner, owner.T)
+def tile_loads(plan, tiles, source, target, sems):
+    width = plan.plane // tiles
+    groups = []
+    for k in range(tiles):
+        at = slice(k * width, (k + 1) * width)
+        rows = [slice(h * plan.rows, (h + 1) * plan.rows) for h in (0, 1)]
+        groups.append(
+            [pltpu.make_async_copy(source.at[h, :, at], target.at[rows[h], at], sems.at[h, k]) for h in (0, 1)]
+        )
+    return groups
 
 
 def gelu_slope(pre):
@@ -493,148 +571,172 @@
     return jnp.where(pre < 0.0, low, 1.0 - low)
 
 
-def fill_lhs(plan, me, lhs, own_ref, got_ref, mix_ref):
-    ms2 = 2 * plan.ms
-    for half, in_ref in ((me, own_ref), (1 - me, got_ref)):
-        lhs[half, :, :ms2] = in_ref[...]
-    for half in (0, 1):
-        lhs[half, :, ms2:] = mix_ref[half]
-
-
-def cells_forward(plan, me, own, got, plane, mixing, stack, cotangent):
-    tiles = 2
+def cells_forward(plan, me, modes, mixing, stack, cotangent, before):
+    tiles = 4
     width = plan.plane // tiles
     stripe = 32
     ms2 = 2 * plan.ms
-    deep = ms2 + 2 * plan.rows
-    items = [(t, h) for t in range(tiles) for h in (0, 1)]
-
-    def kernel(
-        me_ref, own_ref, got_ref, plane_ref, mix_ref, stack_ref, cot_ref,
-        grad_ref, send_ref, keep_ref, lhs, pre, acc, cot, sems,
-    ):
-        me = me_ref[0]
-        copies = []
-        for n, (t, h) in enumerate(items):
-            at = slice(t * width, (t + 1) * width)
-            copies.append(pltpu.make_async_copy(cot_ref.at[h, :, at], cot.at[h, :, at], sems.at[n]))
-            copies[-1].start()
-        table = pltpu.make_async_copy(plane_ref, grad_ref.at[:ms2, :], sems.at[len(items)])
-        table.start()
-        fill_lhs(plan, me, lhs, own_ref, got_ref, mix_ref)
-
-        def product(n):
-            t, h = items[n]
-            pre[n % 2] = dot(lhs[h], stack_ref[:, t * width : (t + 1) * width])
-
-        def slope(n):
-            t, h = items[n]
-            at = slice(t * width, (t + 1) * width)
-            copies[n].wait()
+    first = before is None
+
+    def kernel(me_ref, modes_ref, mix_ref, stack_ref, cot_ref, *rest):
+        if first:
+            grad, out_ref, pre, acc = rest
+            half = me_ref[0]
+        else:
+            before_ref, grad_ref, out_ref, pre, acc, grad, sems = rest
+            half = 1 - me_ref[0]
+            stores = [pltpu.make_async_copy(before_ref, grad_ref.at[1 - half], sems.at[tiles])]
+            stores[0].start()
+        lhs = jnp.concatenate([modes_ref[...], mix_ref[half]], 1)
+
+        def product(k):
+            pre[k % 2] = dot(lhs, stack_ref[:, k * width : (k + 1) * width])
+
+        def slope(k):
+            at = slice(k * width, (k + 1) * width)
             for r in range(0, plan.rows, stripe):
-                value = cot[h, r : r + stripe, at].astype(F32) * gelu_slope(pre[n % 2, r : r + stripe, :])
-                start = ms2 + h * plan.rows + r
-                grad_ref[start : start + stripe, at] = value.astype(BF)
-
-        def transform(n):
-            t, h = items[n]
-            at = slice(t * width, (t + 1) * width)
-            start = ms2 + h * plan.rows
-            value = dot_t(stack_ref[:ms2, at], grad_ref[start : start + plan.rows, at])
-            if t == 0:
-                acc[h] = value
+                rows = slice(r, r + stripe)
+                value = cot_ref[half, rows, at].astype(F32) * gelu_slope(pre[k % 2, rows, :])
+                grad[rows, at] = value.astype(BF)
+            if not first:
+                stores.append(pltpu.make_async_copy(grad.at[:, at], grad_ref.at[half, :, at], sems.at[k]))
+                stores[-1].start()
+
+        def transform(k):
+            at = slice(k * width, (k + 1) * width)
+            value = dot_t(stack_ref[:ms2, at], grad[:, at])
+            if k == 0:
+                acc[...] = value
             else:
-                acc[h] += value
+                acc[...] += value
 
         product(0)
-        for n in range(len(items)):
-            if n + 1 < len(items):
-                product(n + 1)
-            slope(n)
-            if n > 0:
-                transform(n - 1)
-        transform(len(items) - 1)
-        for half, out_ref in ((me, keep_ref), (1 - me, send_ref)):
-            pad_lanes(plan, out_ref)
-            out_ref[:, : plan.rows] = acc[half].astype(BF)
-        table.wait()
+        for k in range(tiles):
+            if k + 1 < tiles:
+                product(k + 1)
+            slope(k)
+            if k > 0:
+                transform(k - 1)
+        transform(tiles - 1)
+        pad_lanes(plan, out_ref)
+        out_ref[:, : plan.rows] = acc[...].astype(BF)
+        if not first:
+            for store in stores:
+                store.wait()
 
     out = (ms2, plan.rows_pad)
-    return pl.pallas_call(
-        kernel,
-        in_specs=[SCALAR, WHOLE, WHOLE, ANYWHERE, WHOLE, WHOLE, ANYWHERE],
-        out_specs=[WHOLE] * 3,
-        out_shape=[pltpu.VMEM((deep, plan.plane), BF), shape(out), shape(out)],
-        scratch_shapes=[
-            pltpu.VMEM((2, plan.rows, deep), BF),
-            pltpu.VMEM((2, plan.rows, width), F32),
-            pltpu.VMEM((2, ms2, plan.rows), F32),
-            pltpu.VMEM((2, plan.rows, plan.plane), BF),
-            pltpu.SemaphoreType.DMA((len(items) + 1,)),
-        ],
-        compiler_params=params(),
-        cost_estimate=cost(6e9, 1e7),
-        name="cells_forward",
-    )(me, own, got, hbm(plane), vmem(mixing), vmem(stack), hbm(cotangent.reshape(2, plan.rows, plan.plane)))
-
-
-def cells_back(plan, me, own, got, mixing, grads):
-    tiles = 2
+    cells = (2, plan.rows, plan.plane)
+    half = pltpu.VMEM((plan.rows, plan.plane), BF)
+    return pl.pallas_call(
+        kernel,
+        in_specs=[SCALAR] + [WHOLE] * (4 if first else 5),
+        out_specs=[WHOLE if first else ANYWHERE, WHOLE],
+        out_shape=[half if first else pltpu.HBM(cells, BF), shape(out)],
+        scratch_shapes=[pltpu.VMEM((2, plan.rows, width), F32), pltpu.VMEM((ms2, plan.rows), F32)]
+        + ([] if first else [half, pltpu.SemaphoreType.DMA((tiles + 1,))]),
+        compiler_params=params(),
+        cost_estimate=cost(3e9, 5e6),
+        name="cells_forward_own" if first else "cells_forward_got",
+    )(
+        me, modes, vmem(mixing), vmem(stack), vmem(cotangent.reshape(cells)),
+        *([] if first else [vmem(before)]),
+    )
+
+
+def cells_back(plan, me, modes, plane, mixing, grads, before, mix_sums):
+    tiles = 4
     width = plan.plane // tiles
-    ms2 = 2 * plan.ms
-    deep = ms2 + 2 * plan.rows
-    items = [(t, h) for t in range(tiles) for h in (0, 1)]
-
-    def kernel(me_ref, own_ref, got_ref, mix_ref, grad_ref, out_ref, lhs, held, sems):
-        fill_lhs(plan, me_ref[0], lhs, own_ref, got_ref, mix_ref)
-        copies = []
-        for n, (t, h) in enumerate(items):
-            at = slice(t * width, (t + 1) * width)
-            held[h, :, at] = dot(lhs[h], grad_ref[:, at]).astype(BF)
-            copies.append(pltpu.make_async_copy(held.at[h, :, at], out_ref.at[h, :, at], sems.at[n]))
-            copies[-1].start()
-        for copy in copies:
-            copy.wait()
-
-    cells = (2, plan.rows, plan.plane)
-    return pl.pallas_call(
-        kernel,
-        in_specs=[SCALAR, WHOLE, WHOLE, WHOLE, WHOLE],
-        out_specs=ANYWHERE,
-        out_shape=shape(cells),
-        scratch_shapes=[
-            pltpu.VMEM((2, plan.rows, deep), BF),
-            pltpu.VMEM(cells, BF),
-            pltpu.SemaphoreType.DMA((len(items),)),
-        ],
-        compiler_params=params(),
-        cost_estimate=cost(4e9, 8e6),
-        name="cells_back",
-    )(me, own, got, vmem(mixing), vmem(grads))
-
-
-def pack_tables(plan):
     per_row = plan.chans // MIX_ROWS
     lane = LANES // per_row
-    assert per_row * MIX_ROWS == plan.chans and lane >= plan.chans
-    pick = np.zeros((per_row, MIX_ROWS, plan.chans), np.float32)
-    place = np.zeros((per_row, 2 * plan.rows, LANES), np.float32)
-    for k in range(per_row):
-        for r in range(MIX_ROWS):
-            pick[k, r, r * per_row + k] = 1.0
-        for cell in range(2 * plan.rows):
-            place[k, cell, k * lane + cell // plan.xz] = 1.0
-    return pick, place.astype(ml_dtypes.bfloat16)
-
-
-def mix_partial(plan, stack, grads):
+    first = before is None
+
+    def kernel(me_ref, modes_ref, plane_in, mix_ref, grad_in, *rest):
+        if first:
+            held, grad_ref, plane_ref, sems, plane_sems = rest
+            half = me_ref[0]
+            loads = tile_loads(plan, tiles, grad_in, grad_ref, sems)
+            for k, group in enumerate(loads):
+                at = slice(k * width, (k + 1) * width)
+                group.append(pltpu.make_async_copy(plane_in.at[:, at], plane_ref.at[:, at], plane_sems.at[k]))
+                for copy in group:
+                    copy.start()
+        else:
+            before_ref, sums_ref, out_ref, mix_out, held, sums, sems = rest
+            grad_ref, plane_ref = grad_in, plane_in
+            half = 1 - me_ref[0]
+            stores = [pltpu.make_async_copy(before_ref, out_ref.at[1 - half], sems.at[tiles])]
+            stores[0].start()
+        lhs = jnp.concatenate([modes_ref[: plan.rows], mix_ref[half]], 1)
+        for k in range(tiles):
+            at = slice(k * width, (k + 1) * width)
+            if first:
+                for copy in loads[k]:
+                    copy.wait()
+            value = dot(lhs, jnp.concatenate([plane_ref[:, at], grad_ref[:, at]], 0))
+            held[:, at] = value.astype(BF)
+            if not first:
+                stores.append(pltpu.make_async_copy(held.at[:, at], out_ref.at[half, :, at], sems.at[k]))
+                stores[-1].start()
+        if not first:
+            sums[...] = modes_ref[plan.rows :, :LANES].astype(F32)
+            total = sums_ref[...] + sums[:MIX_ROWS, :] + sums[MIX_ROWS : 2 * MIX_ROWS, :]
+            for c in range(plan.chans):
+                row, start = c // per_row, (c % per_row) * lane
+                mix_out[c : c + 1, :] = total[row : row + 1, start : start + plan.chans]
+            for store in stores:
+                store.wait()
+
+    half = pltpu.VMEM((plan.rows, plan.plane), BF)
+    whole = pltpu.VMEM((2 * plan.rows, plan.plane), BF)
+    if first:
+        outs, out_specs = [half, whole, pltpu.VMEM(plane.shape, BF)], [WHOLE] * 3
+        scratch = [pltpu.SemaphoreType.DMA((2, tiles)), pltpu.SemaphoreType.DMA((tiles,))]
+    else:
+        outs = [pltpu.HBM((2, plan.rows, plan.plane), BF), shape((plan.chans, plan.chans), F32)]
+        out_specs = [ANYWHERE, WHOLE]
+        scratch = [half, pltpu.VMEM((16, LANES), F32), pltpu.SemaphoreType.DMA((tiles + 1,))]
+    return pl.pallas_call(
+        kernel,
+        in_specs=[SCALAR, WHOLE, ANYWHERE, WHOLE, ANYWHERE] if first else [SCALAR] + [WHOLE] * 6,
+        out_specs=out_specs,
+        out_shape=outs,
+        scratch_shapes=scratch,
+        compiler_params=params(),
+        cost_estimate=cost(2e9, 4e6),
+        name="cells_back_own" if first else "cells_back_got",
+    )(
+        me, modes, hbm(plane) if first else vmem(plane), vmem(mixing), hbm(grads) if first else vmem(grads),
+        *([] if first else [vmem(before), mix_sums]),
+    )
+
+
+def mix_partial(plan, mix, owner, field, grads):
+    tiles = 4
+    width = plan.plane // tiles
     cells = 2 * plan.rows
-    ms2 = 2 * plan.ms
-    pick, place = pack_tables(plan)
+    per_row = plan.chans // MIX_ROWS
+    lane = LANES // per_row
+    assert per_row * MIX_ROWS == plan.chans and lane > plan.chans
     factor = 1.0 / math.sqrt(plan.count)
 
-    def kernel(field_ref, grad_ref, pick_ref, place_ref, out_ref, acc):
-        acc[...] = dot_t(field_ref[ms2:, :], grad_ref[ms2:, :])
+    def kernel(mix_ref, owner_ref, field_in, grad_in, out_ref, mixing_ref, acc, field_ref, grad_ref, sums, matrix, sems, mix_sem):
+        loads = zip(tile_loads(plan, tiles, grad_in, grad_ref, sems.at[0]), tile_loads(plan, tiles, field_in, field_ref, sems.at[1]))
+        loads = [first + second for first, second in loads]
+        for group in loads:
+            for copy in group:
+                copy.start()
+        mix_matrix(plan, mix_ref[...], True, matrix)
+        mix_store = pltpu.make_async_copy(matrix, mixing_ref, mix_sem)
+        mix_store.start()
+        for k in range(tiles):
+            at = slice(k * width, (k + 1) * width)
+            for copy in loads[k]:
+                copy.wait()
+            value = dot_t(field_ref[:, at], grad_ref[:, at])
+            if k == 0:
+                acc[...] = value
+            else:
+                acc[...] += value
         row = lax.broadcasted_iota(jnp.int32, (plan.xz, cells), 0)
         col = lax.broadcasted_iota(jnp.int32, (plan.xz, cells), 1) % plan.xz
         same = row == col
@@ -642,28 +744,34 @@
         for c in range(plan.chans):
             part = jnp.where(same, acc[c * plan.xz : (c + 1) * plan.xz, :], 0.0)
             lines.append(jnp.sum(part, 0, keepdims=True))
-        sums = jnp.concatenate(lines, 0) * factor
-        high = sums.astype(BF)
-        low = (sums - high.astype(F32)).astype(BF)
-        total = jnp.zeros((MIX_ROWS, LANES), F32)
-        for k in range(plan.chans // MIX_ROWS):
-            spread = dot(high, place_ref[k]) + dot(low, place_ref[k])
-            total += lax.dot_general(
-                pick_ref[k], spread, (((1,), (0,)), ((), ())),
-                precision=lax.Precision.HIGHEST, preferred_element_type=F32,
-            )
-        out_ref[...] = total
-
-    return pl.pallas_call(
-        kernel,
-        in_specs=[WHOLE] * 4,
-        out_specs=WHOLE,
-        scratch_shapes=[pltpu.VMEM((cells, cells), F32)],
-        out_shape=shape((MIX_ROWS, LANES), F32),
+        line = jnp.concatenate(lines, 0) * factor
+        high = line.astype(BF)
+        low = (line - high.astype(F32)).astype(BF)
+        sums[...] = dot(high, owner_ref[...]) + dot(low, owner_ref[...])
+        out_ref[...] = jnp.zeros((MIX_ROWS, LANES), F32)
+        for c in range(plan.chans):
+            at, start = c // per_row, (c % per_row) * lane
+            out_ref[at : at + 1, start : start + plan.chans] = sums[c : c + 1, :]
+        mix_store.wait()
+
+    return pl.pallas_call(
+        kernel,
+        in_specs=[WHOLE, WHOLE, ANYWHERE, ANYWHERE],
+        out_specs=[WHOLE, ANYWHERE],
+        out_shape=[shape((MIX_ROWS, LANES), F32), pltpu.HBM((2, plan.rows, cells), BF)],
+        scratch_shapes=[
+            pltpu.VMEM((cells, cells), F32),
+            pltpu.VMEM((cells, plan.plane), BF),
+            pltpu.VMEM((cells, plan.plane), BF),
+            pltpu.VMEM((plan.chans, plan.chans), F32),
+            pltpu.VMEM((2, plan.rows, cells), BF),
+            pltpu.SemaphoreType.DMA((2, 2, tiles)),
+            pltpu.SemaphoreType.DMA,
+        ],
         compiler_params=params(),
         cost_estimate=cost(4e9, 6e6),
         name="mix_partial",
-    )(vmem(stack), vmem(grads), pick, place)
+    )(mix, owner, hbm(field.reshape(2, plan.rows, plan.plane)), hbm(grads))
 
 
 def weight_grad(plan, me, field_own, field_got, grad_own, grad_got):
@@ -736,8 +844,7 @@
         return own, swap(send), beside
 
     def product(weight, own, got, adjoint):
-        send = mode_product(plan, me, False, weight, own, got, adjoint)
-        keep = mode_product(plan, me, True, weight, own, got, adjoint)
+        send, keep = mode_product(plan, me, weight, own, got, adjoint)
         return keep, swap(send)
 
     def to_cells(keep, got, mix, beside):
@@ -746,23 +853,23 @@
         outs = z_inverse(plan, me, chunks, const["z_inverse"], mix is not None)
         return outs[1], swap(outs[0]), outs[2:], beside
 
-    stack, send = load_forward(plan, me, field, plane)
+    stack, send, mixing = load_forward(plan, me, field, plane, mix_weight)
     got = swap(send)
     keep = plane_forward(plan, me, stack)
-    mixing = mix_blocks(plan, mix_weight, const["owner"])
     weight = with_layout_constraint(spec_weight, Layout(major_to_minor=(0, 1, 2, 3, 4)))
-    field_own, field_got, (mixing, weight) = to_modes(keep, got, (mixing, weight))
+    field_own, field_got, _ = to_modes(keep, got, ())
     keep, got = product(weight, field_own, field_got, False)
     keep, got, _, _ = to_cells(keep, got, None, ())
-    grads, send, keep = cells_forward(plan, me, keep, got, plane, mixing[0], stack, cotangent)
-    partial_mix = mix_partial(plan, stack, grads)
-    grad_own, grad_got, partial_mix = to_modes(keep, swap(send), partial_mix)
-    partial_mix = partial_mix + swap(partial_mix)
+    before, keep = cells_forward(plan, me, keep, mixing, stack, cotangent, None)
+    grads, send = cells_forward(plan, me, got, mixing, stack, cotangent, before)
+    beside = mix_partial(plan, mix_weight, const["owner"], field, grads)
+    grad_own, grad_got, (partial_mix, mixing) = to_modes(keep, swap(send), beside)
     keep, got = product(weight, grad_own, grad_got, True)
     spec_grad = weight_grad(plan, me, field_own, field_got, grad_own, grad_got)
     keep, got, mix, spec_grad = to_cells(keep, got, partial_mix, spec_grad)
-    field_grad = cells_back(plan, me, keep, got, mixing[1], grads).reshape(field.shape)
-    return (field_grad, spec_grad.transpose(3, 0, 1, 2, 4), mix[0])
+    before, grads, table = cells_back(plan, me, keep, plane, mixing, grads, None, None)
+    field_grad, mix_grad = cells_back(plan, me, got, table, mixing, grads, before, mix[0])
+    return (field_grad.reshape(field.shape), spec_grad.transpose(3, 0, 1, 2, 4), mix_grad)
 
 
 def solution(mesh):

time: 117 us -> 102 us (0.87)
  local copies, waits for them, and re-layouts: 26 us -> 2.52 us
  blocking collectives: 14.4 us -> 28.2 us
  starting transfers between devices: 25.3 us -> 15.8 us
  Pallas kernels: 42 us -> 45.5 us
  waiting for transfers between devices: 7.26 us -> 8.69 us
    unnamed x48 -> x23, local copies, waits for them, and re-layouts: 26 us -> 2.52 us
    all_to_all x1 -> x2, blocking collectives: 14.4 us -> 28.2 us  [spread(): return lax.all_to_all(chunks, 'gx', split_axis=0, concat_axis=0, tiled=True)]
    all_to_all x3 -> x2, starting transfers between devices: 17.3 us -> 7.28 us  [spread(): return lax.all_to_all(chunks, 'gx', split_axis=0, concat_axis=0, tiled=True)]
    pallas_call x9 -> x10, Pallas kernels: 27.3 us -> 32.1 us  [the longest x2 8.59 us: cells_forward(): pl.pallas_call(kernel, in_specs=[SCALAR] + [WHOLE] * (4 if first else 5),...]
    all_to_all x3 -> x2, waiting for transfers between devices: 1.66 us -> 5.55 us  [spread(): return lax.all_to_all(chunks, 'gx', split_axis=0, concat_axis=0, tiled=True)]
    ppermute x9 -> x8, waiting for transfers between devices: 5.6 us -> 3.14 us  [swap(): return lax.ppermute(value, 'gz', [(0, 1), (1, 0)])]
    ppermute x9 -> x8, starting transfers between devices: 8.03 us -> 8.57 us  [swap(): return lax.ppermute(value, 'gz', [(0, 1), (1, 0)])]
  transfers between devices with their start and end apart: 12 -> 10, of which waited for: 6 -> 5; matrix products, arithmetic and copies ran while one was open for 6% -> 1% of each run, Pallas kernels for 14% -> 24%
where the time goes in v2:
time: 102 us
  Pallas kernels  45.5 us (45%)
  blocking collectives  28.2 us (28%)
  starting transfers between devices  15.8 us (15%)
  waiting for transfers between devices  8.69 us (9%)
  local copies, waits for them, and re-layouts  2.52 us (2%)
  between operations  1.11 us (1%)
    all_to_all x2, blocking collectives, spread(): return lax.all_to_all(chunks, 'gx', split_axis=0, concat_axis=0, tiled=True)  28.2 us
    pallas_call x2, Pallas kernels, cells_forward(): pl.pallas_call(kernel, in_specs=[SCALAR] + [WHOLE] * (4 if first else 5),...  8.59 us
    ppermute x8, starting transfers between devices, swap(): return lax.ppermute(value, 'gz', [(0, 1), (1, 0)])  8.57 us
    all_to_all x2, starting transfers between devices, spread(): return lax.all_to_all(chunks, 'gx', split_axis=0, concat_axis=0, tiled=True)  7.28 us
    pallas_call x1, Pallas kernels, weight_grad(): pl.pallas_call(kernel, grid_spec=pltpu.PrefetchScalarGridSpec(num_scalar_...  7.04 us
    pallas_call x2, Pallas kernels, cells_back(): pl.pallas_call(kernel, in_specs=[SCALAR, WHOLE, ANYWHERE, WHOLE, ANYWHERE...  6.51 us
    all_to_all x2, waiting for transfers between devices, spread(): return lax.all_to_all(chunks, 'gx', split_axis=0, concat_axis=0, tiled=True)  5.55 us
    pallas_call x1, Pallas kernels, mix_partial(): pl.pallas_call(kernel, in_specs=[WHOLE, WHOLE, ANYWHERE, ANYWHERE], out_s...  5.31 us
  transfers between devices with their start and end apart: 10, of which 5 were waited for; matrix products, arithmetic and copies ran while one was open for 1% of the time, Pallas kernels for 24%

profile of v2, /device:TPU:1, one launch (start us, length us, event | category | flops | bytes accessed | tf_op | source)
XLA Modules:
  0.0 101.9 jit_solution(8930247634311086521)
XLA Ops:
  0.6 4.2 %load_forward.1 = (bf16[1024,2048]{1,0:T(8,128)(2,1)S(1)}, bf16[384,384]{1,0:T(8,128)(2,1)S(1)}, bf16[2,320,640]{2,1,0:T(8,128)(2,1)S(1)}) custom-call(s32[1]{0:T(128)} %bitcast.me_ref._, bf16[2,320,2048]{2,1,0:T(8,128)(2,1)} %bitcast.7, bf16[384,2048]{1,0:T(8,128)(2,1)} %constant.16.clone.plane_ref.plane_in, bf16[20,20]{1,0:T(8,128)(2,1)} %mix_ref.3), custom_call_target="tpu_custom_call" | custom-call | flops 503316480 | bytes 5000000 | tf_op jit(solution)/shard_map/load_forward/pallas_call | solution.py:221
  6.8 16.0 %all_to_all.20.in_ref = bf16[16,64,128]{2,1,0:T(8,128)(2,1)S(1)} all-to-all(bf16[16,64,128]{2,1,0:T(8,128)(2,1)S(1)} %z_forward.2), channel_id=1, replica_groups=mesh['grp'=1,'gx'=16,'gz'=2] {'gx'}, dimensions={0} | all-to-all | bytes 524288 | tf_op jit(solution)/shard_map/all_to_all | solution.py:838
  23.4 2.5 %collective-permute-start.1 = (bf16[10,2,12,192]{3,2,1,0:T(8,128)(2,1)S(1)}, bf16[10,2,12,192]{3,2,1,0:T(8,128)(2,1)S(1)}, u32[]{:S(2)}, u32[]{:S(2)}) collective-permute-start(bf16[10,2,12,192]{3,2,1,0:T(8,128)(2,1)S(1)} %get-tuple-element.36), channel_id=1, source_target_pairs={{0,1},{1,0},{2,3},{3,2},{4,5},{5,4},{6,7},{7,6},{8,9},{9,8},{10,11... | collective-permute-start | bytes 276488 | tf_op jit(solution)/shard_map/ppermute | solution.py:835
  25.9 1.3 %copy.13.weight_ref = bf16[2,20,20,12,192]{4,3,2,1,0:T(8,128)(2,1)S(1)} copy(bf16[2,20,20,12,192]{4,0,3,2,1:T(2,128)(2,1)S(1)} %copy-done.10) | data formatting | bytes 7372800 | tf_op args[2]
  27.3 1.5 %mode_product.3 = bf16[10,2,12,192]{3,2,1,0:T(8,128)(2,1)S(1)} custom-call(s32[1]{0:T(128)} %bitcast.me_ref._, bf16[2,20,20,12,192]{4,3,2,1,0:T(8,128)(2,1)S(1)} %copy.13.weight_ref, bf16[10,2,12,192]{3,2,1,0:T(8,128)(2,1)S(1)} %get-tuple-element.35.own_ref.fo_ref, bf16[10,2,12,192]{3,2,1,0:T(8,128)(2,1)S(1)} %collective-permute-done.1.got_ref.fg_ref), custom_call_target="tpu_custom_call" | custom-call | flops 2000000000 | bytes 4000000 | tf_op jit(solution)/shard_map/mode_product/pallas_call | solution.py:400
  30.0 1.5 %mode_product.2.own_ref = bf16[10,2,12,192]{3,2,1,0:T(8,128)(2,1)S(1)} custom-call(s32[1]{0:T(128)} %bitcast.me_ref._, bf16[2,20,20,12,192]{4,3,2,1,0:T(8,128)(2,1)S(1)} %copy.13.weight_ref, bf16[10,2,12,192]{3,2,1,0:T(8,128)(2,1)S(1)} %get-tuple-element.35.own_ref.fo_ref, bf16[10,2,12,192]{3,2,1,0:T(8,128)(2,1)S(1)} %collective-permute-done.1.got_ref.fg_ref), custom_call_target="tpu_custom_call" | custom-call | flops 2000000000 | bytes 4000000 | tf_op jit(solution)/shard_map/mode_product/pallas_call | solution.py:400
  32.1 12.2 %all_to_all.21.in_ref = bf16[16,64,128]{2,1,0:T(8,128)(2,1)S(1)} all-to-all(bf16[16,64,128]{2,1,0:T(8,128)(2,1)S(1)} %x_inverse.2), channel_id=1, replica_groups=mesh['grp'=1,'gx'=16,'gz'=2] {'gx'}, dimensions={0} | all-to-all | bytes 524288 | tf_op jit(solution)/shard_map/all_to_all | solution.py:838
  44.9 1.9 %collective-permute-start.3 = (bf16[320,384]{1,0:T(8,128)(2,1)S(1)}, bf16[320,384]{1,0:T(8,128)(2,1)S(1)}, u32[]{:S(2)}, u32[]{:S(2)}) collective-permute-start(bf16[320,384]{1,0:T(8,128)(2,1)S(1)} %get-tuple-element.40), channel_id=1, source_target_pairs={{0,1},{1,0},{2,3},{3,2},{4,5},{5,4},{6,7},{7,6},{8,9},{9,8},{10,11... | collective-permute-start | bytes 737288 | tf_op jit(solution)/shard_map/ppermute | solution.py:835
  46.8 4.2 %cells_forward_own.1 = (bf16[320,2048]{1,0:T(8,128)(2,1)S(1)}, bf16[384,384]{1,0:T(8,128)(2,1)S(1)}) custom-call(s32[1]{0:T(128)} %bitcast.me_ref._, bf16[320,384]{1,0:T(8,128)(2,1)S(1)} %get-tuple-element.37.modes_ref, bf16[2,320,640]{2,1,0:T(8,128)(2,1)S(1)} %get-tuple-element.38.mix_ref, bf16[1024,2048]{1,0:T(8,128)(2,1)S(1)} %get-tuple-element.33.stack_ref, ...), custom_call_target="tpu_custom_call" | custom-call | flops 3000000000 | bytes 5000000 | tf_op jit(solution)/shard_map/cells_forward_own/pallas_call | solution.py:630
  51.0 4.4 %cells_forward_got.1 = (bf16[2,320,2048]{2,1,0:T(8,128)(2,1)}, bf16[384,384]{1,0:T(8,128)(2,1)S(1)}) custom-call(s32[1]{0:T(128)} %bitcast.me_ref._, bf16[320,384]{1,0:T(8,128)(2,1)S(1)} %collective-permute-done.3.modes_ref, bf16[2,320,640]{2,1,0:T(8,128)(2,1)S(1)} %get-tuple-element.38.mix_ref, bf16[1024,2048]{1,0:T(8,128)(2,1)S(1)} %get-tuple-element.33.stack_ref, ...), custom_call_target="tpu_custom_call" | custom-call | flops 3000000000 | bytes 5000000 | tf_op jit(solution)/shard_map/cells_forward_got/pallas_call | solution.py:630
  55.5 1.6 %collective-permute-done.4.got_ref = bf16[384,384]{1,0:T(8,128)(2,1)S(1)} collective-permute-done((bf16[384,384]{1,0:T(8,128)(2,1)S(1)}, bf16[384,384]{1,0:T(8,128)(2,1)S(1)}, u32[]{:S(2)}, u32[]{:S(2)}) %collective-permute-start.4) | collective-permute-done | bytes 294944 | tf_op jit(solution)/shard_map/ppermute | solution.py:835
  58.1 3.8 %all-to-all-start.2 = ((bf16[16,64,128]{2,1,0:T(8,128)(2,1)}), bf16[16,64,128]{2,1,0:T(8,128)(2,1)S(1)}, u32[]{:S(2)}, u32[]{:S(2)}) async-start(bf16[16,64,128]{2,1,0:T(8,128)(2,1)} %z_forward.3), calls=%async_computation.2 | async-start | bytes 524288 | tf_op jit(solution)/shard_map/all_to_all | solution.py:838
  61.9 5.3 %mix_partial.1 = (f32[4,128]{1,0:T(4,128)S(1)}, bf16[2,320,640]{2,1,0:T(8,128)(2,1)}) custom-call(bf16[20,20]{1,0:T(8,128)(2,1)S(1)} %copy-done.5, bf16[640,20]{1,0:T(8,128)(2,1)S(1)} %copy-done.8, bf16[2,320,2048]{2,1,0:T(8,128)(2,1)} %bitcast.8, bf16[2,320,2048]{2,1,0:T(8,128)(2,1)} %get-tuple-element.43.grad_in), custom_call_target="tpu_custom_call" | custom-call | flops 4000000000 | bytes 6000000 | tf_op jit(solution)/shard_map/mix_partial/pallas_call | solution.py:757
  67.2 3.5 %all-to-all-done.2.in_ref = bf16[16,64,128]{2,1,0:T(8,128)(2,1)S(1)} async-done(((bf16[16,64,128]{2,1,0:T(8,128)(2,1)}), bf16[16,64,128]{2,1,0:T(8,128)(2,1)S(1)}, u32[]{:S(2)}, u32[]{:S(2)}) %all-to-all-start.2) | async-done | bytes 262176 | tf_op jit(solution)/shard_map/all_to_all | solution.py:838
  71.3 1.7 %collective-permute-start.5 = (bf16[10,2,12,192]{3,2,1,0:T(8,128)(2,1)S(1)}, bf16[10,2,12,192]{3,2,1,0:T(8,128)(2,1)S(1)}, u32[]{:S(2)}, u32[]{:S(2)}) collective-permute-start(bf16[10,2,12,192]{3,2,1,0:T(8,128)(2,1)S(1)} %get-tuple-element.48), channel_id=1, source_target_pairs={{0,1},{1,0},{2,3},{3,2},{4,5},{5,4},{6,7},{7,6},{8,9},{9,8},{10,11... | collective-permute-start | bytes 276488 | tf_op jit(solution)/shard_map/ppermute | solution.py:835
  74.1 3.0 %mode_product_send.1 = (bf16[10,2,12,192]{3,2,1,0:T(8,128)(2,1)S(1)}, bf16[2,10,20,12,192]{4,3,2,1,0:T(8,128)(2,1)S(1)}) custom-call(s32[1]{0:T(128)} %bitcast.me_ref._, bf16[2,20,20,12,192]{4,3,2,1,0:T(8,128)(2,1)} %copy-done.1, bf16[10,2,12,192]{3,2,1,0:T(8,128)(2,1)S(1)} %get-tuple-element.47.own_ref.go_ref, ...), custom_call_target="tpu_custom_call" | custom-call | flops 2000000000 | bytes 6000000 | tf_op jit(solution)/shard_map/mode_product_send/pallas_call | solution.py:413
  77.5 1.4 %mode_product_keep.1.own_ref = bf16[10,2,12,192]{3,2,1,0:T(8,128)(2,1)S(1)} custom-call(s32[1]{0:T(128)} %bitcast.me_ref._, bf16[2,10,20,12,192]{4,3,2,1,0:T(8,128)(2,1)S(1)} %get-tuple-element.49.weight_ref, bf16[10,2,12,192]{3,2,1,0:T(8,128)(2,1)S(1)} %get-tuple-element.47.own_ref.go_ref, bf16[10,2,12,192]{3,2,1,0:T(8,128)(2,1)S(1)} %collective-permute-done.5.got_ref.gg_ref), custom_call_target="tpu_custom_call" | custom-call | flops 2000000000 | bytes 4000000 | tf_op jit(solution)/shard_map/mode_product_keep/pallas_call | solution.py:423
  79.0 1.3 %x_inverse.3 = bf16[16,64,128]{2,1,0:T(8,128)(2,1)} custom-call(s32[1]{0:T(128)} %bitcast.me_ref._, bf16[10,2,12,192]{3,2,1,0:T(8,128)(2,1)S(1)} %mode_product_keep.1.own_ref, bf16[10,2,12,192]{3,2,1,0:T(8,128)(2,1)S(1)} %collective-permute-done.6.got_ref, bf16[2,2,192,1024]{3,2,1,0:T(8,128)(2,1)S(1)} %copy-done.3, f32[4,128]{1,0:T(4,128)S(1)} %get-tuple-element.51.rest_0_), custom_call_target="tpu_custom_call" | custom-call | flops 300000000 | bytes 3000000 | tf_op jit(solution)/shard_map/x_inverse/pallas_call | solution.py:471
  80.3 3.5 %all-to-all-start.3 = ((bf16[16,64,128]{2,1,0:T(8,128)(2,1)}), bf16[16,64,128]{2,1,0:T(8,128)(2,1)S(1)}, u32[]{:S(2)}, u32[]{:S(2)}) async-start(bf16[16,64,128]{2,1,0:T(8,128)(2,1)} %x_inverse.3), calls=%async_computation.3 | async-start | bytes 524288 | tf_op jit(solution)/shard_map/all_to_all | solution.py:838
  83.8 7.0 %weight_grad.1 = f32[20,20,12,2,192]{4,3,2,1,0:T(2,128)} custom-call(s32[1]{0:T(128)} %bitcast.me_ref._, bf16[10,2,12,192]{3,2,1,0:T(8,128)(2,1)S(1)} %get-tuple-element.35.own_ref.fo_ref, bf16[10,2,12,192]{3,2,1,0:T(8,128)(2,1)S(1)} %collective-permute-done.1.got_ref.fg_ref, bf16[10,2,12,192]{3,2,1,0:T(8,128)(2,1)S(1)} %get-tuple-element.47.own_ref.go_ref, ...), custom_call_target="tpu_custom_call" | custom-call | flops 8000000000 | bytes 13000000 | tf_op jit(solution)/shard_map/weight_grad/pallas_call | solution.py:811
  90.9 2.0 %all-to-all-done.3.in_ref = bf16[16,64,128]{2,1,0:T(8,128)(2,1)S(1)} async-done(((bf16[16,64,128]{2,1,0:T(8,128)(2,1)}), bf16[16,64,128]{2,1,0:T(8,128)(2,1)S(1)}, u32[]{:S(2)}, u32[]{:S(2)}) %all-to-all-start.3) | async-done | bytes 262176 | tf_op jit(solution)/shard_map/all_to_all | solution.py:838
  93.4 1.8 %collective-permute-start.7 = (bf16[336,384]{1,0:T(8,128)(2,1)S(1)}, bf16[336,384]{1,0:T(8,128)(2,1)S(1)}, u32[]{:S(2)}, u32[]{:S(2)}) collective-permute-start(bf16[336,384]{1,0:T(8,128)(2,1)S(1)} %get-tuple-element.53), channel_id=1, source_target_pairs={{0,1},{1,0},{2,3},{3,2},{4,5},{5,4},{6,7},{7,6},{8,9},{9,8},{10,11... | collective-permute-start | bytes 774152 | tf_op jit(solution)/shard_map/ppermute | solution.py:835
  95.2 3.6 %cells_back_own.1 = (bf16[320,2048]{1,0:T(8,128)(2,1)S(1)}, bf16[640,2048]{1,0:T(8,128)(2,1)S(1)}, bf16[384,2048]{1,0:T(8,128)(2,1)S(1)}) custom-call(s32[1]{0:T(128)} %bitcast.me_ref._, bf16[320,384]{1,0:T(8,128)(2,1)S(1)} %get-tuple-element.54.modes_ref, bf16[384,2048]{1,0:T(8,128)(2,1)} %constant.16.clone.plane_ref.plane_in, ...), custom_call_target="tpu_custom_call" | custom-call | flops 2000000000 | bytes 4000000 | tf_op jit(solution)/shard_map/cells_back_own/pallas_call | solution.py:698
  98.8 3.0 %cells_back_got.1 = (bf16[2,320,2048]{2,1,0:T(8,128)(2,1)}, f32[20,20]{1,0:T(8,128)}) custom-call(s32[1]{0:T(128)} %bitcast.me_ref._, bf16[336,384]{1,0:T(8,128)(2,1)S(1)} %collective-permute-done.7.modes_ref, bf16[384,2048]{1,0:T(8,128)(2,1)S(1)} %get-tuple-element.56.plane_in, bf16[2,320,640]{2,1,0:T(8,128)(2,1)S(1)} %copy-done.9, ...), custom_call_target="tpu_custom_call" | custom-call | flops 2000000000 | bytes 4000000 | tf_op jit(solution)/shard_map/cells_back_got/pallas_call | solution.py:698
  (41 shorter events, 8.5 us)
Async XLA Ops:
  4.8 1.7 %copy-start.4 = (bf16[2,512,256]{2,1,0:T(8,128)(2,1)S(1)}, bf16[2,512,256]{2,1,0:T(8,128)(2,1)}, u32[]{:S(2)}) copy-start(bf16[2,512,256]{2,1,0:T(8,128)(2,1)} %constant.17.clone.table_ref) | copy-start | bytes 1572868
  4.8 1.6 %collective-permute-start = (bf16[384,384]{1,0:T(8,128)(2,1)S(1)}, bf16[384,384]{1,0:T(8,128)(2,1)S(1)}, u32[]{:S(2)}, u32[]{:S(2)}) collective-permute-start(bf16[384,384]{1,0:T(8,128)(2,1)S(1)} %get-tuple-element.34), channel_id=1, source_target_pairs={{0,1},{1,0},{2,3},{3,2},{4,5},{5,4},{6,7},{7,6},{8,9},{9,8},{10,11... | collective-permute-start | bytes 884744 | tf_op jit(solution)/shard_map/ppermute | solution.py:835
  4.9 18.0 %copy-start = (bf16[2,2,1024,192]{3,2,1,0:T(8,128)(2,1)S(1)}, bf16[2,2,1024,192]{3,2,1,0:T(8,128)(2,1)}, u32[]{:S(2)}) copy-start(bf16[2,2,1024,192]{3,2,1,0:T(8,128)(2,1)} %constant.19.clone.table_ref) | copy-start | bytes 4718596
  4.9 21.0 %copy-start.10 = (bf16[2,20,20,12,192]{4,0,3,2,1:T(2,128)(2,1)S(1)}, bf16[2,20,20,12,192]{4,0,3,2,1:T(2,128)(2,1)}, u32[]{:S(2)}) copy-start(bf16[2,20,20,12,192]{4,0,3,2,1:T(2,128)(2,1)} %param.12) | copy-start | bytes 11059204
  23.4 3.9 %collective-permute-start.1 = (bf16[10,2,12,192]{3,2,1,0:T(8,128)(2,1)S(1)}, bf16[10,2,12,192]{3,2,1,0:T(8,128)(2,1)S(1)}, u32[]{:S(2)}, u32[]{:S(2)}) collective-permute-start(bf16[10,2,12,192]{3,2,1,0:T(8,128)(2,1)S(1)} %get-tuple-element.36), channel_id=1, source_target_pairs={{0,1},{1,0},{2,3},{3,2},{4,5},{5,4},{6,7},{7,6},{8,9},{9,8},{10,11... | collective-permute-start | bytes 276488 | tf_op jit(solution)/shard_map/ppermute | solution.py:835
  27.2 2.8 %copy-start.1 = (bf16[2,20,20,12,192]{4,3,2,1,0:T(8,128)(2,1)}, bf16[2,20,20,12,192]{4,3,2,1,0:T(8,128)(2,1)S(1)}, u32[]{:S(2)}) copy-start(bf16[2,20,20,12,192]{4,3,2,1,0:T(8,128)(2,1)S(1)} %copy.13.weight_ref) | copy-start | bytes 11059204
  28.8 2.8 %copy-start.2 = (bf16[2,2,192,1024]{3,2,1,0:T(8,128)(2,1)S(1)}, bf16[2,2,192,1024]{3,2,1,0:T(8,128)(2,1)}, u32[]{:S(2)}) copy-start(bf16[2,2,192,1024]{3,2,1,0:T(8,128)(2,1)} %constant.20.clone.table_ref) | copy-start | bytes 4718596
  28.8 2.8 %collective-permute-start.2 = (bf16[10,2,12,192]{3,2,1,0:T(8,128)(2,1)S(1)}, bf16[10,2,12,192]{3,2,1,0:T(8,128)(2,1)S(1)}, u32[]{:S(2)}, u32[]{:S(2)}) collective-permute-start(bf16[10,2,12,192]{3,2,1,0:T(8,128)(2,1)S(1)} %mode_product.3), channel_id=1, source_target_pairs={{0,1},{1,0},{2,3},{3,2},{4,5},{5,4},{6,7},{7,6},{8,9},{9,8},{10,11... | collective-permute-start | bytes 276488 | tf_op jit(solution)/shard_map/ppermute | solution.py:835
  30.0 14.3 %copy-start.7 = (bf16[2,512,256]{2,1,0:T(8,128)(2,1)S(1)}, bf16[2,512,256]{2,1,0:T(8,128)(2,1)}, u32[]{:S(2)}) copy-start(bf16[2,512,256]{2,1,0:T(8,128)(2,1)} %constant.18.clone.table_ref) | copy-start | bytes 1572868
  31.6 15.2 %copy-start.6 = (bf16[20,2,16,2048]{3,2,1,0:T(8,128)(2,1)S(1)}, bf16[20,2,16,2048]{3,2,1,0:T(8,128)(2,1)}, u32[]{:S(2)}) copy-start(bf16[20,2,16,2048]{3,2,1,0:T(8,128)(2,1)} %param.11) | copy-start | bytes 7864324
  44.9 6.1 %collective-permute-start.3 = (bf16[320,384]{1,0:T(8,128)(2,1)S(1)}, bf16[320,384]{1,0:T(8,128)(2,1)S(1)}, u32[]{:S(2)}, u32[]{:S(2)}) collective-permute-start(bf16[320,384]{1,0:T(8,128)(2,1)S(1)} %get-tuple-element.40), channel_id=1, source_target_pairs={{0,1},{1,0},{2,3},{3,2},{4,5},{5,4},{6,7},{7,6},{8,9},{9,8},{10,11... | collective-permute-start | bytes 737288 | tf_op jit(solution)/shard_map/ppermute | solution.py:835
  51.0 10.9 %copy-start.5 = (bf16[20,20]{1,0:T(8,128)(2,1)S(1)}, bf16[20,20]{1,0:T(8,128)(2,1)}, u32[]{:S(2)}) copy-start(bf16[20,20]{1,0:T(8,128)(2,1)} %mix_ref.3) | copy-start | bytes 2404
  51.0 10.9 %copy-start.8 = (bf16[640,20]{1,0:T(8,128)(2,1)S(1)}, bf16[640,20]{1,0:T(8,128)(2,1)}, u32[]{:S(2)}) copy-start(bf16[640,20]{1,0:T(8,128)(2,1)} %constant.21.clone.owner_ref) | copy-start | bytes 76804
  55.4 1.6 %collective-permute-start.4 = (bf16[384,384]{1,0:T(8,128)(2,1)S(1)}, bf16[384,384]{1,0:T(8,128)(2,1)S(1)}, u32[]{:S(2)}, u32[]{:S(2)}) collective-permute-start(bf16[384,384]{1,0:T(8,128)(2,1)S(1)} %get-tuple-element.42), channel_id=1, source_target_pairs={{0,1},{1,0},{2,3},{3,2},{4,5},{5,4},{6,7},{7,6},{8,9},{9,8},{10,11... | collective-permute-start | bytes 884744 | tf_op jit(solution)/shard_map/ppermute | solution.py:835
  58.1 12.6 %all-to-all-start.2 = ((bf16[16,64,128]{2,1,0:T(8,128)(2,1)}), bf16[16,64,128]{2,1,0:T(8,128)(2,1)S(1)}, u32[]{:S(2)}, u32[]{:S(2)}) async-start(bf16[16,64,128]{2,1,0:T(8,128)(2,1)} %z_forward.3), calls=%async_computation.2 | async-start | bytes 524288 | tf_op jit(solution)/shard_map/all_to_all | solution.py:838
  71.3 2.8 %collective-permute-start.5 = (bf16[10,2,12,192]{3,2,1,0:T(8,128)(2,1)S(1)}, bf16[10,2,12,192]{3,2,1,0:T(8,128)(2,1)S(1)}, u32[]{:S(2)}, u32[]{:S(2)}) collective-permute-start(bf16[10,2,12,192]{3,2,1,0:T(8,128)(2,1)S(1)} %get-tuple-element.48), channel_id=1, source_target_pairs={{0,1},{1,0},{2,3},{3,2},{4,5},{5,4},{6,7},{7,6},{8,9},{9,8},{10,11... | collective-permute-start | bytes 276488 | tf_op jit(solution)/shard_map/ppermute | solution.py:835
  77.1 1.8 %collective-permute-start.6 = (bf16[10,2,12,192]{3,2,1,0:T(8,128)(2,1)S(1)}, bf16[10,2,12,192]{3,2,1,0:T(8,128)(2,1)S(1)}, u32[]{:S(2)}, u32[]{:S(2)}) collective-permute-start(bf16[10,2,12,192]{3,2,1,0:T(8,128)(2,1)S(1)} %get-tuple-element.50), channel_id=1, source_target_pairs={{0,1},{1,0},{2,3},{3,2},{4,5},{5,4},{6,7},{7,6},{8,9},{9,8},{10,11... | collective-permute-start | bytes 276488 | tf_op jit(solution)/shard_map/ppermute | solution.py:835
  77.5 1.4 %copy-start.3 = (bf16[2,2,192,1024]{3,2,1,0:T(8,128)(2,1)S(1)}, bf16[2,2,192,1024]{3,2,1,0:T(8,128)(2,1)}, u32[]{:S(2)}) copy-start(bf16[2,2,192,1024]{3,2,1,0:T(8,128)(2,1)} %constant.20.clone.table_ref) | copy-start | bytes 4718596
  80.3 12.6 %all-to-all-start.3 = ((bf16[16,64,128]{2,1,0:T(8,128)(2,1)}), bf16[16,64,128]{2,1,0:T(8,128)(2,1)S(1)}, u32[]{:S(2)}, u32[]{:S(2)}) async-start(bf16[16,64,128]{2,1,0:T(8,128)(2,1)} %x_inverse.3), calls=%async_computation.3 | async-start | bytes 524288 | tf_op jit(solution)/shard_map/all_to_all | solution.py:838
  83.8 11.4 %copy-start.9 = (bf16[2,320,640]{2,1,0:T(8,128)(2,1)S(1)}, bf16[2,320,640]{2,1,0:T(8,128)(2,1)}, u32[]{:S(2)}) copy-start(bf16[2,320,640]{2,1,0:T(8,128)(2,1)} %get-tuple-element.55.mix_ref) | copy-start | bytes 2457604
  93.4 5.3 %collective-permute-start.7 = (bf16[336,384]{1,0:T(8,128)(2,1)S(1)}, bf16[336,384]{1,0:T(8,128)(2,1)S(1)}, u32[]{:S(2)}, u32[]{:S(2)}) collective-permute-start(bf16[336,384]{1,0:T(8,128)(2,1)S(1)} %get-tuple-element.53), channel_id=1, source_target_pairs={{0,1},{1,0},{2,3},{3,2},{4,5},{5,4},{6,7},{7,6},{8,9},{9,8},{10,11... | collective-permute-start | bytes 774152 | tf_op jit(solution)/shard_map/ppermute | solution.py:835

commit v3 on v2

--- a/solution.py
+++ b/solution.py
@@ -157,17 +157,29 @@
     return pl.ds(pl.multiple_of(2 * plan.ms + half * plan.rows, math.gcd(2 * plan.ms, plan.rows)), plan.rows)
 
 
-def mix_matrix(plan, mix, back, out_ref):
+def mix_masks(plan, owned_ref, mask_ref, wide_ref):
     cells = 2 * plan.rows
+    shift = plan.xz.bit_length() - 1
+    assert 1 << shift == plan.xz
     iota = lambda dims, axis: lax.broadcasted_iota(jnp.int32, dims, axis)
-    one_hot = lambda hit: hit.astype(F32).astype(BF)
-    owner = one_hot(iota((cells, plan.chans), 0) // plan.xz == iota((cells, plan.chans), 1))
-    owned = one_hot(iota((plan.chans, cells), 1) // plan.xz == iota((plan.chans, cells), 0))
-    spread = (dot if back else dot_t)(owner, mix).astype(BF)
-    same = iota((plan.rows, cells), 0) % plan.xz == iota((plan.rows, cells), 1) % plan.xz
-    for h in (0, 1):
-        wide = dot(spread[h * plan.rows : (h + 1) * plan.rows], owned)
-        out_ref[h] = jnp.where(same, wide, 0.0).astype(BF)
+    mine = (iota((plan.chans, cells), 1) >> shift) == iota((plan.chans, cells), 0)
+    owned_ref[...] = jnp.where(mine, 1.0, 0.0).astype(BF)
+    apart = (iota((plan.xz, cells), 0) - iota((plan.xz, cells), 1)) & (plan.xz - 1)
+    mask_ref[...] = jnp.where(apart == 0, 1.0, 0.0).astype(F32)
+
+
+def mix_matrix(plan, mix, back, owned_ref, mask_ref, wide_ref, out_ref):
+    sides = (((1,), (0,)), ((), ())) if back else (((0,), (0,)), ((), ()))
+    wide_ref[...] = lax.dot_general(mix, owned_ref[...], sides, preferred_element_type=F32)
+    for c in range(plan.chans):
+        half, start = c // plan.half, (c % plan.half) * plan.xz
+        line = wide_ref[c : c + 1, :] * mask_ref[...]
+        out_ref[half, start : start + plan.xz, :] = line.astype(BF)
+
+
+def mix_scratch(plan):
+    cells = 2 * plan.rows
+    return [pltpu.VMEM((plan.chans, cells), BF), pltpu.VMEM((plan.xz, cells), F32), pltpu.VMEM((plan.chans, cells), F32)]
 
 
 def load_forward(plan, me, field, plane, mix):
@@ -177,7 +189,8 @@
     cells = 2 * plan.rows
 
     def kernel(
-        me_ref, field_ref, plane_ref, mix_ref, stack_ref, out_ref, mixing_ref, acc, small, sems, mix_sem,
+        me_ref, field_ref, plane_ref, mix_ref, stack_ref, out_ref, mixing_ref,
+        acc, small, sems, mix_sem, *masks,
     ):
         me = me_ref[0]
         copies = []
@@ -201,8 +214,7 @@
             group[1].start()
         for group in copies:
             group[2].start()
-        mix_load.wait()
-        mix_matrix(plan, small[...], False, mixing_ref)
+        mix_masks(plan, *masks)
         for k, group in enumerate(copies):
             at = slice(k * width, (k + 1) * width)
             group[0].wait()
@@ -214,6 +226,8 @@
                 acc[...] += value
         pad_lanes(plan, out_ref)
         out_ref[:, : plan.rows] = acc[...].astype(BF)
+        mix_load.wait()
+        mix_matrix(plan, small[...], False, *masks, mixing_ref)
         for group in copies:
             group[2].wait()
 
@@ -228,30 +242,43 @@
             pltpu.VMEM((plan.chans, plan.chans), BF),
             pltpu.SemaphoreType.DMA((3, tiles)),
             pltpu.SemaphoreType.DMA,
-        ],
+        ]
+        + mix_scratch(plan),
         compiler_params=params(),
         cost_estimate=cost(4 * plan.ms * plan.rows * plan.plane, 5e6),
         name="load_forward",
     )(me, hbm(field.reshape(2, plan.rows, plan.plane)), hbm(plane), hbm(mix))
 
 
-def plane_forward(plan, me, stack):
+def plane_forward(plan, me, stack, spec_weight):
     ms2 = 2 * plan.ms
-
-    def kernel(me_ref, stack_ref, out_ref):
+    tiles = 4
+    native = spec_weight.transpose(1, 2, 3, 0, 4)
+    step = plan.chans // tiles
+
+    def kernel(me_ref, stack_ref, weight_in, out_ref, weight_ref, sems):
+        loads = []
+        for k in range(tiles):
+            at = slice(k * step, (k + 1) * step)
+            loads.append(pltpu.make_async_copy(weight_in.at[at], weight_ref.at[at], sems.at[k]))
+            loads[-1].start()
         value = dot_t(stack_ref[:ms2, :], stack_ref[half_rows(plan, me_ref[0]), :])
         pad_lanes(plan, out_ref)
         out_ref[:, : plan.rows] = value.astype(BF)
-
-    return pl.pallas_call(
-        kernel,
-        in_specs=[SCALAR, WHOLE],
-        out_specs=WHOLE,
-        out_shape=shape((ms2, plan.rows_pad)),
+        for load in loads:
+            load.wait()
+
+    keep, native = pl.pallas_call(
+        kernel,
+        in_specs=[SCALAR, WHOLE, ANYWHERE],
+        out_specs=[WHOLE, WHOLE],
+        out_shape=[shape((ms2, plan.rows_pad)), pltpu.VMEM(native.shape, BF)],
+        scratch_shapes=[pltpu.SemaphoreType.DMA((tiles,))],
         compiler_params=params(),
         cost_estimate=cost(4 * plan.ms * plan.rows * plan.plane, 3e6),
         name="plane_forward",
-    )(me, vmem(stack))
+    )(me, vmem(stack), hbm(native))
+    return keep, native.transpose(3, 0, 1, 2, 4)
 
 
 def z_forward(plan, me, own, got, table):
@@ -331,106 +358,45 @@
     )(me, chunks, table)
 
 
-def mode_sums(plan, weight_ref, held, out_ref, adjoint, arrive, start=0):
-    def one(k, carry):
-        arrive(k)
-        real = jnp.zeros((plan.s, plan.modes), F32)
-        imag = jnp.zeros((plan.s, plan.modes), F32)
-        for c in range(plan.chans):
-            pos = (start + k, c) if adjoint else (c, start + k)
-            wr = weight_ref[0, pos[0], pos[1]].astype(F32)
-            wi = weight_ref[1, pos[0], pos[1]].astype(F32)
-            mr = held[c // plan.half, c % plan.half, 0]
-            mi = held[c // plan.half, c % plan.half, 1]
-            if adjoint:
-                real += wr * mr + wi * mi
-                imag += wr * mi - wi * mr
-            else:
-                real += wr * mr - wi * mi
-                imag += wr * mi + wi * mr
-        out_ref[k, 0] = real.astype(BF)
-        out_ref[k, 1] = imag.astype(BF)
-        return carry
-
-    lax.fori_loop(0, plan.half, one, 0)
-
-
-def mode_product(plan, me, weight, own, got, adjoint):
-    side = (plan.half, 2, plan.s, plan.modes)
-    if adjoint:
-        part = (2, plan.half, plan.chans, plan.s, plan.modes)
-    else:
-        part = (2, plan.chans, plan.half, plan.s, plan.modes)
-    held = pltpu.VMEM((2,) + side, F32)
-
-    def hold(me, held, own_ref, got_ref):
+def mode_product(plan, me, mine, weight, own, got, adjoint):
+    def kernel(me_ref, weight_ref, own_ref, got_ref, out_ref, held):
+        me = me_ref[0]
         held[me] = own_ref[...].astype(F32)
         held[1 - me] = got_ref[...].astype(F32)
-
-    def first(me_ref, weight_ref, own_ref, got_ref, out_ref, rest_ref, held, part_ref, sems):
-        me = me_ref[0]
-
-        def copy(k, half, to, sem):
-            if adjoint:
-                return pltpu.make_async_copy(weight_ref.at[:, half * plan.half + k], to.at[:, k], sem)
-            return pltpu.make_async_copy(weight_ref.at[:, :, half * plan.half + k], to.at[:, :, k], sem)
-
-        for k in range(plan.half):
-            copy(k, 1 - me, part_ref, sems.at[0, k]).start()
-        for k in range(plan.half):
-            copy(k, me, rest_ref, sems.at[1, k]).start()
-        hold(me, held, own_ref, got_ref)
-        arrive = lambda k: copy(k, 1 - me, part_ref, sems.at[0, k]).wait()
-        mode_sums(plan, part_ref, held, out_ref, adjoint, arrive)
-        for k in range(plan.half):
-            copy(k, me, rest_ref, sems.at[1, k]).wait()
-
-    def second(me_ref, weight_ref, own_ref, got_ref, out_ref, held):
-        hold(me_ref[0], held, own_ref, got_ref)
-        mode_sums(plan, weight_ref, held, out_ref, adjoint, lambda k: None)
-
-    def resident(mine, me_ref, weight_ref, own_ref, got_ref, out_ref, held):
-        me = me_ref[0]
-        hold(me, held, own_ref, got_ref)
         start = (me if mine else 1 - me) * plan.half
-        mode_sums(plan, weight_ref, held, out_ref, adjoint, lambda k: None, start)
-
-    if not adjoint:
-        return [
-            pl.pallas_call(
-                functools.partial(resident, mine),
-                in_specs=[SCALAR, WHOLE, WHOLE, WHOLE],
-                out_specs=WHOLE,
-                out_shape=shape(side),
-                scratch_shapes=[held],
-                compiler_params=params(),
-                cost_estimate=cost(2e9, 4e6),
-                name="mode_product",
-            )(me, vmem(weight), own, got)
-            for mine in (False, True)
-        ]
-
-    send, rest = pl.pallas_call(
-        first,
-        in_specs=[SCALAR, ANYWHERE, WHOLE, WHOLE],
-        out_specs=[WHOLE, WHOLE],
-        out_shape=[shape(side), pltpu.VMEM(part, BF)],
-        scratch_shapes=[held, pltpu.VMEM(part, BF), pltpu.SemaphoreType.DMA((2, plan.half))],
-        compiler_params=params(),
-        cost_estimate=cost(2e9, 6e6),
-        name="mode_product_send",
-    )(me, hbm(weight), own, got)
-    keep = pl.pallas_call(
-        second,
+
+        def one(k, carry):
+            real = jnp.zeros((plan.s, plan.modes), F32)
+            imag = jnp.zeros((plan.s, plan.modes), F32)
+            for c in range(plan.chans):
+                pos = (start + k, c) if adjoint else (c, start + k)
+                wr = weight_ref[0, pos[0], pos[1]].astype(F32)
+                wi = weight_ref[1, pos[0], pos[1]].astype(F32)
+                mr = held[c // plan.half, c % plan.half, 0]
+                mi = held[c // plan.half, c % plan.half, 1]
+                if adjoint:
+                    real += wr * mr + wi * mi
+                    imag += wr * mi - wi * mr
+                else:
+                    real += wr * mr - wi * mi
+                    imag += wr * mi + wi * mr
+            out_ref[k, 0] = real.astype(BF)
+            out_ref[k, 1] = imag.astype(BF)
+            return carry
+
+        lax.fori_loop(0, plan.half, one, 0)
+
+    side = (plan.half, 2, plan.s, plan.modes)
+    return pl.pallas_call(
+        kernel,
         in_specs=[SCALAR, WHOLE, WHOLE, WHOLE],
         out_specs=WHOLE,
         out_shape=shape(side),
-        scratch_shapes=[held],
+        scratch_shapes=[pltpu.VMEM((2,) + side, F32)],
         compiler_params=params(),
         cost_estimate=cost(2e9, 4e6),
-        name="mode_product_keep",
-    )(me, vmem(rest), own, got)
-    return send, keep
+        name="mode_product",
+    )(me, vmem(weight), own, got)
 
 
 def x_inverse(plan, me, own, got, table, mix):
@@ -583,7 +549,7 @@
             grad, out_ref, pre, acc = rest
             half = me_ref[0]
         else:
-            before_ref, grad_ref, out_ref, pre, acc, grad, sems = rest
+            before_ref, grad_ref, out_ref, grad, pre, acc, sems = rest
             half = 1 - me_ref[0]
             stores = [pltpu.make_async_copy(before_ref, grad_ref.at[1 - half], sems.at[tiles])]
             stores[0].start()
@@ -630,10 +596,10 @@
     return pl.pallas_call(
         kernel,
         in_specs=[SCALAR] + [WHOLE] * (4 if first else 5),
-        out_specs=[WHOLE if first else ANYWHERE, WHOLE],
-        out_shape=[half if first else pltpu.HBM(cells, BF), shape(out)],
+        out_specs=[WHOLE, WHOLE] if first else [ANYWHERE, WHOLE, WHOLE],
+        out_shape=[half, shape(out)] if first else [pltpu.HBM(cells, BF), shape(out), half],
         scratch_shapes=[pltpu.VMEM((2, plan.rows, width), F32), pltpu.VMEM((ms2, plan.rows), F32)]
-        + ([] if first else [half, pltpu.SemaphoreType.DMA((tiles + 1,))]),
+        + ([] if first else [pltpu.SemaphoreType.DMA((tiles + 1,))]),
         compiler_params=params(),
         cost_estimate=cost(3e9, 5e6),
         name="cells_forward_own" if first else "cells_forward_got",
@@ -652,7 +618,7 @@
 
     def kernel(me_ref, modes_ref, plane_in, mix_ref, grad_in, *rest):
         if first:
-            held, grad_ref, plane_ref, sems, plane_sems = rest
+            held, grad_ref, plane_ref, matrix, sems, plane_sems, *masks = rest
             half = me_ref[0]
             loads = tile_loads(plan, tiles, grad_in, grad_ref, sems)
             for k, group in enumerate(loads):
@@ -660,13 +626,16 @@
                 group.append(pltpu.make_async_copy(plane_in.at[:, at], plane_ref.at[:, at], plane_sems.at[k]))
                 for copy in group:
                     copy.start()
+            mix_masks(plan, *masks)
+            mix_matrix(plan, mix_ref[...], True, *masks, matrix)
         else:
             before_ref, sums_ref, out_ref, mix_out, held, sums, sems = rest
+            matrix = mix_ref
             grad_ref, plane_ref = grad_in, plane_in
             half = 1 - me_ref[0]
             stores = [pltpu.make_async_copy(before_ref, out_ref.at[1 - half], sems.at[tiles])]
             stores[0].start()
-        lhs = jnp.concatenate([modes_ref[: plan.rows], mix_ref[half]], 1)
+        lhs = jnp.concatenate([modes_ref[: plan.rows], matrix[half]], 1)
         for k in range(tiles):
             at = slice(k * width, (k + 1) * width)
             if first:
@@ -689,8 +658,9 @@
     half = pltpu.VMEM((plan.rows, plan.plane), BF)
     whole = pltpu.VMEM((2 * plan.rows, plan.plane), BF)
     if first:
-        outs, out_specs = [half, whole, pltpu.VMEM(plane.shape, BF)], [WHOLE] * 3
-        scratch = [pltpu.SemaphoreType.DMA((2, tiles)), pltpu.SemaphoreType.DMA((tiles,))]
+        outs = [half, whole, pltpu.VMEM(plane.shape, BF), pltpu.VMEM((2, plan.rows, 2 * plan.rows), BF)]
+        out_specs = [WHOLE] * 4
+        scratch = [pltpu.SemaphoreType.DMA((2, tiles)), pltpu.SemaphoreType.DMA((tiles,))] + mix_scratch(plan)
     else:
         outs = [pltpu.HBM((2, plan.rows, plan.plane), BF), shape((plan.chans, plan.chans), F32)]
         out_specs = [ANYWHERE, WHOLE]
@@ -705,73 +675,57 @@
         cost_estimate=cost(2e9, 4e6),
         name="cells_back_own" if first else "cells_back_got",
     )(
-        me, modes, hbm(plane) if first else vmem(plane), vmem(mixing), hbm(grads) if first else vmem(grads),
+        me, modes, hbm(plane) if first else vmem(plane), mixing if first else vmem(mixing), hbm(grads) if first else vmem(grads),
         *([] if first else [vmem(before), mix_sums]),
     )
 
 
-def mix_partial(plan, mix, owner, field, grads):
-    tiles = 4
-    width = plan.plane // tiles
+def mix_partial(plan, me, owner, stack, grad, before):
     cells = 2 * plan.rows
+    ms2 = 2 * plan.ms
     per_row = plan.chans // MIX_ROWS
     lane = LANES // per_row
     assert per_row * MIX_ROWS == plan.chans and lane > plan.chans
     factor = 1.0 / math.sqrt(plan.count)
-
-    def kernel(mix_ref, owner_ref, field_in, grad_in, out_ref, mixing_ref, acc, field_ref, grad_ref, sums, matrix, sems, mix_sem):
-        loads = zip(tile_loads(plan, tiles, grad_in, grad_ref, sems.at[0]), tile_loads(plan, tiles, field_in, field_ref, sems.at[1]))
-        loads = [first + second for first, second in loads]
-        for group in loads:
-            for copy in group:
-                copy.start()
-        mix_matrix(plan, mix_ref[...], True, matrix)
-        mix_store = pltpu.make_async_copy(matrix, mixing_ref, mix_sem)
-        mix_store.start()
-        for k in range(tiles):
-            at = slice(k * width, (k + 1) * width)
-            for copy in loads[k]:
-                copy.wait()
-            value = dot_t(field_ref[:, at], grad_ref[:, at])
-            if k == 0:
-                acc[...] = value
-            else:
-                acc[...] += value
-        row = lax.broadcasted_iota(jnp.int32, (plan.xz, cells), 0)
-        col = lax.broadcasted_iota(jnp.int32, (plan.xz, cells), 1) % plan.xz
-        same = row == col
+    first = before is None
+
+    def kernel(me_ref, owner_ref, stack_ref, grad_ref, *rest):
+        acc = rest[-1] if first else rest[-2]
+        acc[...] = dot_t(stack_ref[ms2:, :], grad_ref[...])
+        iota = lambda axis: lax.broadcasted_iota(jnp.int32, (plan.xz, plan.rows), axis)
+        apart = (iota(0) - iota(1)) & (plan.xz - 1)
         lines = []
         for c in range(plan.chans):
-            part = jnp.where(same, acc[c * plan.xz : (c + 1) * plan.xz, :], 0.0)
+            part = jnp.where(apart == 0, acc[c * plan.xz : (c + 1) * plan.xz, :], 0.0)
             lines.append(jnp.sum(part, 0, keepdims=True))
         line = jnp.concatenate(lines, 0) * factor
         high = line.astype(BF)
         low = (line - high.astype(F32)).astype(BF)
-        sums[...] = dot(high, owner_ref[...]) + dot(low, owner_ref[...])
+        owned = owner_ref[: plan.rows, : plan.half]
+        value = dot(high, owned) + dot(low, owned)
+        if first:
+            rest[0][...] = value
+            return
+        before_ref, out_ref, _, sums = rest
+        swapped = me_ref[0] == 0
+        sums[:, : plan.half] = jnp.where(swapped, before_ref[...], value)
+        sums[:, plan.half :] = jnp.where(swapped, value, before_ref[...])
         out_ref[...] = jnp.zeros((MIX_ROWS, LANES), F32)
         for c in range(plan.chans):
             at, start = c // per_row, (c % per_row) * lane
             out_ref[at : at + 1, start : start + plan.chans] = sums[c : c + 1, :]
-        mix_store.wait()
-
-    return pl.pallas_call(
-        kernel,
-        in_specs=[WHOLE, WHOLE, ANYWHERE, ANYWHERE],
-        out_specs=[WHOLE, ANYWHERE],
-        out_shape=[shape((MIX_ROWS, LANES), F32), pltpu.HBM((2, plan.rows, cells), BF)],
-        scratch_shapes=[
-            pltpu.VMEM((cells, cells), F32),
-            pltpu.VMEM((cells, plan.plane), BF),
-            pltpu.VMEM((cells, plan.plane), BF),
-            pltpu.VMEM((plan.chans, plan.chans), F32),
-            pltpu.VMEM((2, plan.rows, cells), BF),
-            pltpu.SemaphoreType.DMA((2, 2, tiles)),
-            pltpu.SemaphoreType.DMA,
-        ],
-        compiler_params=params(),
-        cost_estimate=cost(4e9, 6e6),
-        name="mix_partial",
-    )(mix, owner, hbm(field.reshape(2, plan.rows, plan.plane)), hbm(grads))
+
+    return pl.pallas_call(
+        kernel,
+        in_specs=[SCALAR] + [WHOLE] * (3 if first else 4),
+        out_specs=WHOLE,
+        out_shape=shape((plan.chans, plan.half) if first else (MIX_ROWS, LANES), F32),
+        scratch_shapes=[pltpu.VMEM((cells, plan.rows), F32)]
+        + ([] if first else [pltpu.VMEM((plan.chans, plan.chans), F32)]),
+        compiler_params=params(),
+        cost_estimate=cost(2e9, 4e6),
+        name="mix_partial_own" if first else "mix_partial_got",
+    )(me, owner, vmem(stack), vmem(grad), *([] if first else [before]))
 
 
 def weight_grad(plan, me, field_own, field_got, grad_own, grad_got):
@@ -831,20 +785,21 @@
     me = core.reshape(1)
     plane = const["plane"]
 
+
     def swap(value):
         return lax.ppermute(value, "gz", [(0, 1), (1, 0)])
 
     def spread(chunks):
         return lax.all_to_all(chunks, "gx", split_axis=0, concat_axis=0, tiled=True)
 
-    def to_modes(keep, got, beside):
+    def to_modes(keep, got):
         chunks = spread(z_forward(plan, me, keep, got, const["z_forward"]))
-        chunks, beside = lax.optimization_barrier((chunks, beside))
         send, own = x_forward(plan, me, chunks, const["x_forward"])
-        return own, swap(send), beside
-
-    def product(weight, own, got, adjoint):
-        send, keep = mode_product(plan, me, weight, own, got, adjoint)
+        return own, swap(send)
+
+    def product(own, got, adjoint):
+        send = mode_product(plan, me, False, weight, own, got, adjoint)
+        keep = mode_product(plan, me, True, weight, own, got, adjoint)
         return keep, swap(send)
 
     def to_cells(keep, got, mix, beside):
@@ -855,19 +810,23 @@
 
     stack, send, mixing = load_forward(plan, me, field, plane, mix_weight)
     got = swap(send)
-    keep = plane_forward(plan, me, stack)
-    weight = with_layout_constraint(spec_weight, Layout(major_to_minor=(0, 1, 2, 3, 4)))
-    field_own, field_got, _ = to_modes(keep, got, ())
-    keep, got = product(weight, field_own, field_got, False)
+    keep, weight = plane_forward(plan, me, stack, spec_weight)
+    field_own, field_got = to_modes(keep, got)
+    keep, got = product(field_own, field_got, False)
     keep, got, _, _ = to_cells(keep, got, None, ())
-    before, keep = cells_forward(plan, me, keep, mixing, stack, cotangent, None)
-    grads, send = cells_forward(plan, me, got, mixing, stack, cotangent, before)
-    beside = mix_partial(plan, mix_weight, const["owner"], field, grads)
-    grad_own, grad_got, (partial_mix, mixing) = to_modes(keep, swap(send), beside)
-    keep, got = product(weight, grad_own, grad_got, True)
+    grad_own, keep = cells_forward(plan, me, keep, mixing, stack, cotangent, None)
+    grads, send, grad_got = cells_forward(plan, me, got, mixing, stack, cotangent, grad_own)
+    got = swap(send)
+    partial_mix = mix_partial(plan, me, const["owner"], stack, grad_own, None)
+    got, partial_mix = lax.optimization_barrier((got, partial_mix))
+    grad_own, got = to_modes(keep, got)
+    partial_mix = mix_partial(plan, me, const["owner"], stack, grad_got, partial_mix)
+    got, partial_mix = lax.optimization_barrier((got, partial_mix))
+    grad_got = got
+    keep, got = product(grad_own, grad_got, True)
     spec_grad = weight_grad(plan, me, field_own, field_got, grad_own, grad_got)
     keep, got, mix, spec_grad = to_cells(keep, got, partial_mix, spec_grad)
-    before, grads, table = cells_back(plan, me, keep, plane, mixing, grads, None, None)
+    before, grads, table, mixing = cells_back(plan, me, keep, plane, mix_weight, grads, None, None)
     field_grad, mix_grad = cells_back(plan, me, got, table, mixing, grads, before, mix[0])
     return (field_grad.reshape(field.shape), spec_grad.transpose(3, 0, 1, 2, 4), mix_grad)
 

time: 102 us -> 99.5 us (0.975)
  blocking collectives: 28.2 us -> 39.4 us
  waiting for transfers between devices: 8.69 us -> 1.67 us
  Pallas kernels: 45.5 us -> 42 us
  starting transfers between devices: 15.8 us -> 13.6 us
  local copies, waits for them, and re-layouts: 2.52 us -> 1.38 us
    all_to_all x2 -> x3, blocking collectives: 28.2 us -> 39.4 us  [spread(): return lax.all_to_all(chunks, 'gx', split_axis=0, concat_axis=0, tiled=True)]
    all_to_all x2 -> x1, waiting for transfers between devices: 5.55 us -> 1.64 us  [spread(): return lax.all_to_all(chunks, 'gx', split_axis=0, concat_axis=0, tiled=True)]
    all_to_all x2 -> x1, starting transfers between devices: 7.28 us -> 3.75 us  [spread(): return lax.all_to_all(chunks, 'gx', split_axis=0, concat_axis=0, tiled=True)]
    ppermute x8, waiting for transfers between devices: 3.14 us -> 0.03 us  [swap(): return lax.ppermute(value, 'gz', [(0, 1), (1, 0)])]
    unnamed x23 -> x14, local copies, waits for them, and re-layouts: 2.52 us -> 0.04 us
    pallas_call x6 -> x7, Pallas kernels: 13.8 us -> 12.3 us  [the longest x4 6.13 us: mode_product(): pl.pallas_call(kernel, in_specs=[SCALAR, WHOLE, WHOLE, WHOLE], out_specs=...]
    pallas_call x0 -> x1, local copies, waits for them, and re-layouts: none -> 1.34 us  [plane_forward(): pl.pallas_call(kernel, in_specs=[SCALAR, WHOLE, ANYWHERE], out_specs=[WHO...]
    ppermute x8, starting transfers between devices: 8.57 us -> 9.88 us  [swap(): return lax.ppermute(value, 'gz', [(0, 1), (1, 0)])]
  transfers between devices with their start and end apart: 10 -> 9, of which waited for: 5 -> 1; matrix products, arithmetic and copies ran while one was open for 1% -> 1% of each run, Pallas kernels for 24% -> 24%
where the time goes in v3:
time: 99.5 us; the launch traced here: 99.2 us
  Pallas kernels  42 us (42%)
  blocking collectives  39.4 us (40%)
  starting transfers between devices  13.6 us (14%)
  waiting for transfers between devices  1.67 us (2%)
  local copies, waits for them, and re-layouts  1.38 us (1%)
  between operations  1.07 us (1%)
    all_to_all x3, blocking collectives, spread(): return lax.all_to_all(chunks, 'gx', split_axis=0, concat_axis=0, tiled=True)  39.4 us
    ppermute x8, starting transfers between devices, swap(): return lax.ppermute(value, 'gz', [(0, 1), (1, 0)])  9.88 us
    pallas_call x2, Pallas kernels, cells_forward(): pl.pallas_call(kernel, in_specs=[SCALAR] + [WHOLE] * (4 if first else 5),...  8.62 us
    pallas_call x1, Pallas kernels, weight_grad(): pl.pallas_call(kernel, grid_spec=pltpu.PrefetchScalarGridSpec(num_scalar_...  7.04 us
    pallas_call x2, Pallas kernels, cells_back(): pl.pallas_call(kernel, in_specs=[SCALAR, WHOLE, ANYWHERE, WHOLE, ANYWHERE...  6.29 us
    pallas_call x4, Pallas kernels, mode_product(): pl.pallas_call(kernel, in_specs=[SCALAR, WHOLE, WHOLE, WHOLE], out_specs=...  6.13 us
    all_to_all x1, starting transfers between devices, spread(): return lax.all_to_all(chunks, 'gx', split_axis=0, concat_axis=0, tiled=True)  3.75 us
    pallas_call x2, Pallas kernels, mix_partial(): pl.pallas_call(kernel, in_specs=[SCALAR] + [WHOLE] * (3 if first else 4),...  3.53 us
  transfers between devices with their start and end apart: 9, of which 1 were waited for; matrix products, arithmetic and copies ran while one was open for 1% of the time, Pallas kernels for 24%

profile of v3, /device:TPU:1, one launch (start us, length us, event | category | flops | bytes accessed | tf_op | source)
XLA Modules:
  0.0 99.2 jit_solution(6843569673664800128)
XLA Ops:
  0.6 3.1 %load_forward.1 = (bf16[1024,2048]{1,0:T(8,128)(2,1)S(1)}, bf16[384,384]{1,0:T(8,128)(2,1)S(1)}, bf16[2,320,640]{2,1,0:T(8,128)(2,1)S(1)}) custom-call(s32[1]{0:T(128)} %bitcast.me_ref._, bf16[2,320,2048]{2,1,0:T(8,128)(2,1)} %bitcast.16, bf16[384,2048]{1,0:T(8,128)(2,1)} %constant.16.clone.plane_ref.plane_in, bf16[20,20]{1,0:T(8,128)(2,1)} %mix_ref.3), custom_call_target="tpu_custom_call" | custom-call | flops 503316480 | bytes 5000000 | tf_op jit(solution)/shard_map/load_forward/pallas_call | solution.py:235
  3.9 2.6 %plane_forward.1 = (bf16[384,384]{1,0:T(8,128)(2,1)S(1)}, bf16[20,20,12,2,192]{4,3,2,1,0:T(2,128)(2,1)S(1)}) custom-call(s32[1]{0:T(128)} %bitcast.me_ref._, bf16[1024,2048]{1,0:T(8,128)(2,1)S(1)} %get-tuple-element.34.stack_ref, bf16[20,20,12,2,192]{4,3,2,1,0:T(2,128)(2,1)} %bitcast.15), custom_call_target="tpu_custom_call" | custom-call | flops 503316480 | bytes 3000000 | tf_op jit(solution)/shard_map/plane_forward/pallas_call | solution.py:271
  6.9 16.8 %all_to_all.20.in_ref = bf16[16,64,128]{2,1,0:T(8,128)(2,1)S(1)} all-to-all(bf16[16,64,128]{2,1,0:T(8,128)(2,1)S(1)} %z_forward.2), channel_id=1, replica_groups=mesh['grp'=1,'gx'=16,'gz'=2] {'gx'}, dimensions={0} | all-to-all | bytes 524288 | tf_op jit(solution)/shard_map/all_to_all | solution.py:793
  24.3 1.9 %collective-permute-start.1 = (bf16[10,2,12,192]{3,2,1,0:T(8,128)(2,1)S(1)}, bf16[10,2,12,192]{3,2,1,0:T(8,128)(2,1)S(1)}, u32[]{:S(2)}, u32[]{:S(2)}) collective-permute-start(bf16[10,2,12,192]{3,2,1,0:T(8,128)(2,1)S(1)} %get-tuple-element.39), channel_id=1, source_target_pairs={{0,1},{1,0},{2,3},{3,2},{4,5},{5,4},{6,7},{7,6},{8,9},{9,8},{10,11... | collective-permute-start | bytes 276488 | tf_op jit(solution)/shard_map/ppermute | solution.py:790
  26.2 1.3 %copy.15 = bf16[20,20,12,2,192]{4,2,1,0,3:T(8,128)(2,1)S(1)} copy(bf16[20,20,12,2,192]{4,3,2,1,0:T(2,128)(2,1)S(1)} %get-tuple-element.35) | data formatting | bytes 7372800 | tf_op jit(solution)/shard_map/plane_forward/pallas_call | solution.py:271
  27.5 1.5 %mode_product.5 = bf16[10,2,12,192]{3,2,1,0:T(8,128)(2,1)S(1)} custom-call(s32[1]{0:T(128)} %bitcast.me_ref._, bf16[2,20,20,12,192]{4,3,2,1,0:T(8,128)(2,1)S(1)} %bitcast.9, bf16[10,2,12,192]{3,2,1,0:T(8,128)(2,1)S(1)} %get-tuple-element.38.own_ref.fo_ref, bf16[10,2,12,192]{3,2,1,0:T(8,128)(2,1)S(1)} %collective-permute-done.1.got_ref.fg_ref), custom_call_target="tpu_custom_call" | custom-call | flops 2000000000 | bytes 4000000 | tf_op jit(solution)/shard_map/mode_product/pallas_call | solution.py:390
  29.2 1.5 %mode_product.4.own_ref = bf16[10,2,12,192]{3,2,1,0:T(8,128)(2,1)S(1)} custom-call(s32[1]{0:T(128)} %bitcast.me_ref._, bf16[2,20,20,12,192]{4,3,2,1,0:T(8,128)(2,1)S(1)} %bitcast.10, bf16[10,2,12,192]{3,2,1,0:T(8,128)(2,1)S(1)} %get-tuple-element.38.own_ref.fo_ref, bf16[10,2,12,192]{3,2,1,0:T(8,128)(2,1)S(1)} %collective-permute-done.1.got_ref.fg_ref), custom_call_target="tpu_custom_call" | custom-call | flops 2000000000 | bytes 4000000 | tf_op jit(solution)/shard_map/mode_product/pallas_call | solution.py:390
  31.3 11.4 %all_to_all.21.in_ref = bf16[16,64,128]{2,1,0:T(8,128)(2,1)S(1)} all-to-all(bf16[16,64,128]{2,1,0:T(8,128)(2,1)S(1)} %x_inverse.2), channel_id=1, replica_groups=mesh['grp'=1,'gx'=16,'gz'=2] {'gx'}, dimensions={0} | all-to-all | bytes 524288 | tf_op jit(solution)/shard_map/all_to_all | solution.py:793
  43.2 2.7 %collective-permute-start.3 = (bf16[320,384]{1,0:T(8,128)(2,1)S(1)}, bf16[320,384]{1,0:T(8,128)(2,1)S(1)}, u32[]{:S(2)}, u32[]{:S(2)}) collective-permute-start(bf16[320,384]{1,0:T(8,128)(2,1)S(1)} %get-tuple-element.43), channel_id=1, source_target_pairs={{0,1},{1,0},{2,3},{3,2},{4,5},{5,4},{6,7},{7,6},{8,9},{9,8},{10,11... | collective-permute-start | bytes 737288 | tf_op jit(solution)/shard_map/ppermute | solution.py:790
  45.9 4.2 %cells_forward_own.1 = (bf16[320,2048]{1,0:T(8,128)(2,1)S(1)}, bf16[384,384]{1,0:T(8,128)(2,1)S(1)}) custom-call(s32[1]{0:T(128)} %bitcast.me_ref._, bf16[320,384]{1,0:T(8,128)(2,1)S(1)} %get-tuple-element.40.modes_ref, bf16[2,320,640]{2,1,0:T(8,128)(2,1)S(1)} %get-tuple-element.41.mix_ref, bf16[1024,2048]{1,0:T(8,128)(2,1)S(1)} %get-tuple-element.34.stack_ref, ...), custom_call_target="tpu_custom_call" | custom-call | flops 3000000000 | bytes 5000000 | tf_op jit(solution)/shard_map/cells_forward_own/pallas_call | solution.py:596
  50.2 4.4 %cells_forward_got.1 = (bf16[2,320,2048]{2,1,0:T(8,128)(2,1)}, bf16[384,384]{1,0:T(8,128)(2,1)S(1)}, bf16[320,2048]{1,0:T(8,128)(2,1)S(1)}) custom-call(s32[1]{0:T(128)} %bitcast.me_ref._, bf16[320,384]{1,0:T(8,128)(2,1)S(1)} %collective-permute-done.3.modes_ref, bf16[2,320,640]{2,1,0:T(8,128)(2,1)S(1)} %get-tuple-element.41.mix_ref, ...), custom_call_target="tpu_custom_call" | custom-call | flops 3000000000 | bytes 5000000 | tf_op jit(solution)/shard_map/cells_forward_got/pallas_call | solution.py:596
  54.7 1.7 %mix_partial_own.1.rest_0_ = f32[20,10]{1,0:T(8,128)S(1)} custom-call(s32[1]{0:T(128)} %bitcast.me_ref._, bf16[640,20]{1,0:T(8,128)(2,1)S(1)} %copy-done.6, bf16[1024,2048]{1,0:T(8,128)(2,1)S(1)} %get-tuple-element.34.stack_ref, bf16[320,2048]{1,0:T(8,128)(2,1)S(1)} %get-tuple-element.44.rest_0_.grad_ref), custom_call_target="tpu_custom_call" | custom-call | flops 2000000000 | bytes 4000000 | tf_op jit(solution)/shard_map/mix_partial_own/pallas_call | solution.py:718
  56.8 11.3 %all_to_all.22.in_ref = bf16[16,64,128]{2,1,0:T(8,128)(2,1)S(1)} all-to-all(bf16[16,64,128]{2,1,0:T(8,128)(2,1)S(1)} %z_forward.3), channel_id=1, replica_groups=mesh['grp'=1,'gx'=16,'gz'=2] {'gx'}, dimensions={0} | all-to-all | bytes 524288 | tf_op jit(solution)/shard_map/all_to_all | solution.py:793
  68.5 2.7 %collective-permute-start.5 = (bf16[10,2,12,192]{3,2,1,0:T(8,128)(2,1)S(1)}, bf16[10,2,12,192]{3,2,1,0:T(8,128)(2,1)S(1)}, u32[]{:S(2)}, u32[]{:S(2)}) collective-permute-start(bf16[10,2,12,192]{3,2,1,0:T(8,128)(2,1)S(1)} %get-tuple-element.48), channel_id=1, source_target_pairs={{0,1},{1,0},{2,3},{3,2},{4,5},{5,4},{6,7},{7,6},{8,9},{9,8},{10,11... | collective-permute-start | bytes 276488 | tf_op jit(solution)/shard_map/ppermute | solution.py:790
  71.3 1.9 %mix_partial_got.1.rest_0_ = f32[4,128]{1,0:T(4,128)S(1)} custom-call(s32[1]{0:T(128)} %bitcast.me_ref._, bf16[640,20]{1,0:T(8,128)(2,1)S(1)} %copy-done.6, bf16[1024,2048]{1,0:T(8,128)(2,1)S(1)} %get-tuple-element.34.stack_ref, bf16[320,2048]{1,0:T(8,128)(2,1)S(1)} %get-tuple-element.49.grad_ref, f32[20,10]{1,0:T(8,128)S(1)} %mix_partial_own.1.rest_0_), custom_call_target="tpu_custom_call" | custom-call | flops 2000000000 | bytes 4000000 | tf_op jit(solution)/shard_map/mix_partial_got/pallas_call | solution.py:718
  73.1 1.5 %mode_product.7 = bf16[10,2,12,192]{3,2,1,0:T(8,128)(2,1)S(1)} custom-call(s32[1]{0:T(128)} %bitcast.me_ref._, bf16[2,20,20,12,192]{4,3,2,1,0:T(8,128)(2,1)S(1)} %bitcast.11, bf16[10,2,12,192]{3,2,1,0:T(8,128)(2,1)S(1)} %get-tuple-element.47.own_ref.go_ref, bf16[10,2,12,192]{3,2,1,0:T(8,128)(2,1)S(1)} %collective-permute-done.5.got_ref.gg_ref), custom_call_target="tpu_custom_call" | custom-call | flops 2000000000 | bytes 4000000 | tf_op jit(solution)/shard_map/mode_product/pallas_call | solution.py:390
  74.7 1.5 %mode_product.6.own_ref = bf16[10,2,12,192]{3,2,1,0:T(8,128)(2,1)S(1)} custom-call(s32[1]{0:T(128)} %bitcast.me_ref._, bf16[2,20,20,12,192]{4,3,2,1,0:T(8,128)(2,1)S(1)} %bitcast.12, bf16[10,2,12,192]{3,2,1,0:T(8,128)(2,1)S(1)} %get-tuple-element.47.own_ref.go_ref, bf16[10,2,12,192]{3,2,1,0:T(8,128)(2,1)S(1)} %collective-permute-done.5.got_ref.gg_ref), custom_call_target="tpu_custom_call" | custom-call | flops 2000000000 | bytes 4000000 | tf_op jit(solution)/shard_map/mode_product/pallas_call | solution.py:390
  76.3 1.3 %x_inverse.3 = bf16[16,64,128]{2,1,0:T(8,128)(2,1)} custom-call(s32[1]{0:T(128)} %bitcast.me_ref._, bf16[10,2,12,192]{3,2,1,0:T(8,128)(2,1)S(1)} %mode_product.6.own_ref, bf16[10,2,12,192]{3,2,1,0:T(8,128)(2,1)S(1)} %collective-permute-done.6.got_ref, bf16[2,2,192,1024]{3,2,1,0:T(8,128)(2,1)S(1)} %copy-done.1, f32[4,128]{1,0:T(4,128)S(1)} %mix_partial_got.1.rest_0_), custom_call_target="tpu_custom_call" | custom-call | flops 300000000 | bytes 3000000 | tf_op jit(solution)/shard_map/x_inverse/pallas_call | solution.py:437
  77.6 3.8 %all-to-all-start.3 = ((bf16[16,64,128]{2,1,0:T(8,128)(2,1)}), bf16[16,64,128]{2,1,0:T(8,128)(2,1)S(1)}, u32[]{:S(2)}, u32[]{:S(2)}) async-start(bf16[16,64,128]{2,1,0:T(8,128)(2,1)} %x_inverse.3), calls=%async_computation.3 | async-start | bytes 524288 | tf_op jit(solution)/shard_map/all_to_all | solution.py:793
  81.3 7.0 %weight_grad.1 = f32[20,20,12,2,192]{4,3,2,1,0:T(2,128)} custom-call(s32[1]{0:T(128)} %bitcast.me_ref._, bf16[10,2,12,192]{3,2,1,0:T(8,128)(2,1)S(1)} %get-tuple-element.38.own_ref.fo_ref, bf16[10,2,12,192]{3,2,1,0:T(8,128)(2,1)S(1)} %collective-permute-done.1.got_ref.fg_ref, bf16[10,2,12,192]{3,2,1,0:T(8,128)(2,1)S(1)} %get-tuple-element.47.own_ref.go_ref, ...), custom_call_target="tpu_custom_call" | custom-call | flops 8000000000 | bytes 13000000 | tf_op jit(solution)/shard_map/weight_grad/pallas_call | solution.py:765
  88.4 1.6 %all-to-all-done.3.in_ref = bf16[16,64,128]{2,1,0:T(8,128)(2,1)S(1)} async-done(((bf16[16,64,128]{2,1,0:T(8,128)(2,1)}), bf16[16,64,128]{2,1,0:T(8,128)(2,1)S(1)}, u32[]{:S(2)}, u32[]{:S(2)}) %all-to-all-start.3) | async-done | bytes 262176 | tf_op jit(solution)/shard_map/all_to_all | solution.py:793
  90.6 2.1 %collective-permute-start.7 = (bf16[336,384]{1,0:T(8,128)(2,1)S(1)}, bf16[336,384]{1,0:T(8,128)(2,1)S(1)}, u32[]{:S(2)}, u32[]{:S(2)}) collective-permute-start(bf16[336,384]{1,0:T(8,128)(2,1)S(1)} %get-tuple-element.54), channel_id=1, source_target_pairs={{0,1},{1,0},{2,3},{3,2},{4,5},{5,4},{6,7},{7,6},{8,9},{9,8},{10,11... | collective-permute-start | bytes 774152 | tf_op jit(solution)/shard_map/ppermute | solution.py:790
  92.7 3.4 %cells_back_own.1 = (bf16[320,2048]{1,0:T(8,128)(2,1)S(1)}, bf16[640,2048]{1,0:T(8,128)(2,1)S(1)}, bf16[384,2048]{1,0:T(8,128)(2,1)S(1)}, bf16[2,320,640]{2,1,0:T(8,128)(2,1)S(1)}) custom-call(s32[1]{0:T(128)} %bitcast.me_ref._, bf16[320,384]{1,0:T(8,128)(2,1)S(1)} %get-tuple-element.55.modes_ref, bf16[384,2048]{1,0:T(8,128)(2,1)} %constant.16.clone.plane_ref.plane_in, ...), custom_call_target="tpu_custom_call" | custom-call | flops 2000000000 | bytes 4000000 | tf_op jit(solution)/shard_map/cells_back_own/pallas_call | solution.py:668
  96.1 2.9 %cells_back_got.1 = (bf16[2,320,2048]{2,1,0:T(8,128)(2,1)}, f32[20,20]{1,0:T(8,128)}) custom-call(s32[1]{0:T(128)} %bitcast.me_ref._, bf16[336,384]{1,0:T(8,128)(2,1)S(1)} %collective-permute-done.7.modes_ref, bf16[384,2048]{1,0:T(8,128)(2,1)S(1)} %get-tuple-element.57.plane_in, bf16[2,320,640]{2,1,0:T(8,128)(2,1)S(1)} %get-tuple-element.58.mix_ref, ...), custom_call_target="tpu_custom_call" | custom-call | flops 2000000000 | bytes 4000000 | tf_op jit(solution)/shard_map/cells_back_got/pallas_call | solution.py:668
  (33 shorter events, 3.8 us)
Async XLA Ops:
  3.8 2.7 %collective-permute-start = (bf16[384,384]{1,0:T(8,128)(2,1)S(1)}, bf16[384,384]{1,0:T(8,128)(2,1)S(1)}, u32[]{:S(2)}, u32[]{:S(2)}) collective-permute-start(bf16[384,384]{1,0:T(8,128)(2,1)S(1)} %get-tuple-element.37), channel_id=1, source_target_pairs={{0,1},{1,0},{2,3},{3,2},{4,5},{5,4},{6,7},{7,6},{8,9},{9,8},{10,11... | collective-permute-start | bytes 884744 | tf_op jit(solution)/shard_map/ppermute | solution.py:790
  3.9 2.6 %copy-start.2 = (bf16[2,512,256]{2,1,0:T(8,128)(2,1)S(1)}, bf16[2,512,256]{2,1,0:T(8,128)(2,1)}, u32[]{:S(2)}) copy-start(bf16[2,512,256]{2,1,0:T(8,128)(2,1)} %constant.17.clone.table_ref) | copy-start | bytes 1572868
  3.9 19.8 %copy-start = (bf16[2,2,1024,192]{3,2,1,0:T(8,128)(2,1)S(1)}, bf16[2,2,1024,192]{3,2,1,0:T(8,128)(2,1)}, u32[]{:S(2)}) copy-start(bf16[2,2,1024,192]{3,2,1,0:T(8,128)(2,1)} %constant.19.clone.table_ref) | copy-start | bytes 4718596
  24.3 3.3 %collective-permute-start.1 = (bf16[10,2,12,192]{3,2,1,0:T(8,128)(2,1)S(1)}, bf16[10,2,12,192]{3,2,1,0:T(8,128)(2,1)S(1)}, u32[]{:S(2)}, u32[]{:S(2)}) collective-permute-start(bf16[10,2,12,192]{3,2,1,0:T(8,128)(2,1)S(1)} %get-tuple-element.39), channel_id=1, source_target_pairs={{0,1},{1,0},{2,3},{3,2},{4,5},{5,4},{6,7},{7,6},{8,9},{9,8},{10,11... | collective-permute-start | bytes 276488 | tf_op jit(solution)/shard_map/ppermute | solution.py:790
  29.1 1.7 %copy-start.1 = (bf16[2,2,192,1024]{3,2,1,0:T(8,128)(2,1)S(1)}, bf16[2,2,192,1024]{3,2,1,0:T(8,128)(2,1)}, u32[]{:S(2)}) copy-start(bf16[2,2,192,1024]{3,2,1,0:T(8,128)(2,1)} %constant.20.clone.table_ref) | copy-start | bytes 4718596
  29.1 1.7 %collective-permute-start.2 = (bf16[10,2,12,192]{3,2,1,0:T(8,128)(2,1)S(1)}, bf16[10,2,12,192]{3,2,1,0:T(8,128)(2,1)S(1)}, u32[]{:S(2)}, u32[]{:S(2)}) collective-permute-start(bf16[10,2,12,192]{3,2,1,0:T(8,128)(2,1)S(1)} %mode_product.5), channel_id=1, source_target_pairs={{0,1},{1,0},{2,3},{3,2},{4,5},{5,4},{6,7},{7,6},{8,9},{9,8},{10,11... | collective-permute-start | bytes 276488 | tf_op jit(solution)/shard_map/ppermute | solution.py:790
  29.2 13.5 %copy-start.5 = (bf16[2,512,256]{2,1,0:T(8,128)(2,1)S(1)}, bf16[2,512,256]{2,1,0:T(8,128)(2,1)}, u32[]{:S(2)}) copy-start(bf16[2,512,256]{2,1,0:T(8,128)(2,1)} %constant.18.clone.table_ref) | copy-start | bytes 1572868
  30.7 15.2 %copy-start.4 = (bf16[20,2,16,2048]{3,2,1,0:T(8,128)(2,1)S(1)}, bf16[20,2,16,2048]{3,2,1,0:T(8,128)(2,1)}, u32[]{:S(2)}) copy-start(bf16[20,2,16,2048]{3,2,1,0:T(8,128)(2,1)} %param.11) | copy-start | bytes 7864324
  43.2 7.0 %collective-permute-start.3 = (bf16[320,384]{1,0:T(8,128)(2,1)S(1)}, bf16[320,384]{1,0:T(8,128)(2,1)S(1)}, u32[]{:S(2)}, u32[]{:S(2)}) collective-permute-start(bf16[320,384]{1,0:T(8,128)(2,1)S(1)} %get-tuple-element.43), channel_id=1, source_target_pairs={{0,1},{1,0},{2,3},{3,2},{4,5},{5,4},{6,7},{7,6},{8,9},{9,8},{10,11... | collective-permute-start | bytes 737288 | tf_op jit(solution)/shard_map/ppermute | solution.py:790
  50.2 4.5 %copy-start.6 = (bf16[640,20]{1,0:T(8,128)(2,1)S(1)}, bf16[640,20]{1,0:T(8,128)(2,1)}, u32[]{:S(2)}) copy-start(bf16[640,20]{1,0:T(8,128)(2,1)} %constant.21.clone.owner_ref) | copy-start | bytes 76804
  54.6 1.8 %collective-permute-start.4 = (bf16[384,384]{1,0:T(8,128)(2,1)S(1)}, bf16[384,384]{1,0:T(8,128)(2,1)S(1)}, u32[]{:S(2)}, u32[]{:S(2)}) collective-permute-start(bf16[384,384]{1,0:T(8,128)(2,1)S(1)} %get-tuple-element.45), channel_id=1, source_target_pairs={{0,1},{1,0},{2,3},{3,2},{4,5},{5,4},{6,7},{7,6},{8,9},{9,8},{10,11... | collective-permute-start | bytes 884744 | tf_op jit(solution)/shard_map/ppermute | solution.py:790
  68.5 4.6 %collective-permute-start.5 = (bf16[10,2,12,192]{3,2,1,0:T(8,128)(2,1)S(1)}, bf16[10,2,12,192]{3,2,1,0:T(8,128)(2,1)S(1)}, u32[]{:S(2)}, u32[]{:S(2)}) collective-permute-start(bf16[10,2,12,192]{3,2,1,0:T(8,128)(2,1)S(1)} %get-tuple-element.48), channel_id=1, source_target_pairs={{0,1},{1,0},{2,3},{3,2},{4,5},{5,4},{6,7},{7,6},{8,9},{9,8},{10,11... | collective-permute-start | bytes 276488 | tf_op jit(solution)/shard_map/ppermute | solution.py:790
  74.7 1.6 %collective-permute-start.6 = (bf16[10,2,12,192]{3,2,1,0:T(8,128)(2,1)S(1)}, bf16[10,2,12,192]{3,2,1,0:T(8,128)(2,1)S(1)}, u32[]{:S(2)}, u32[]{:S(2)}) collective-permute-start(bf16[10,2,12,192]{3,2,1,0:T(8,128)(2,1)S(1)} %mode_product.7), channel_id=1, source_target_pairs={{0,1},{1,0},{2,3},{3,2},{4,5},{5,4},{6,7},{7,6},{8,9},{9,8},{10,11... | collective-permute-start | bytes 276488 | tf_op jit(solution)/shard_map/ppermute | solution.py:790
  77.6 12.5 %all-to-all-start.3 = ((bf16[16,64,128]{2,1,0:T(8,128)(2,1)}), bf16[16,64,128]{2,1,0:T(8,128)(2,1)S(1)}, u32[]{:S(2)}, u32[]{:S(2)}) async-start(bf16[16,64,128]{2,1,0:T(8,128)(2,1)} %x_inverse.3), calls=%async_computation.3 | async-start | bytes 524288 | tf_op jit(solution)/shard_map/all_to_all | solution.py:793
  81.3 11.4 %copy-start.3 = (bf16[20,20]{1,0:T(8,128)(2,1)S(1)}, bf16[20,20]{1,0:T(8,128)(2,1)}, u32[]{:S(2)}) copy-start(bf16[20,20]{1,0:T(8,128)(2,1)} %mix_ref.3) | copy-start | bytes 2404
  90.6 5.5 %collective-permute-start.7 = (bf16[336,384]{1,0:T(8,128)(2,1)S(1)}, bf16[336,384]{1,0:T(8,128)(2,1)S(1)}, u32[]{:S(2)}, u32[]{:S(2)}) collective-permute-start(bf16[336,384]{1,0:T(8,128)(2,1)S(1)} %get-tuple-element.54), channel_id=1, source_target_pairs={{0,1},{1,0},{2,3},{3,2},{4,5},{5,4},{6,7},{7,6},{8,9},{9,8},{10,11... | collective-permute-start | bytes 774152 | tf_op jit(solution)/shard_map/ppermute | solution.py:790

commit v4 on v3

--- a/solution.py
+++ b/solution.py
@@ -183,7 +183,7 @@
 
 
 def load_forward(plan, me, field, plane, mix):
-    tiles = 4
+    tiles = 2
     width = plan.plane // tiles
     ms2 = 2 * plan.ms
     cells = 2 * plan.rows
@@ -538,7 +538,7 @@
 
 
 def cells_forward(plan, me, modes, mixing, stack, cotangent, before):
-    tiles = 4
+    tiles = 2
     width = plan.plane // tiles
     stripe = 32
     ms2 = 2 * plan.ms

time: 99.5 us -> 99.2 us (level)
  no operation moved by 1% of the time
where the time goes in v4:
time: 99.2 us; the launch traced here: 98.9 us
  Pallas kernels  41.7 us (42%)
  blocking collectives  39.5 us (40%)
  starting transfers between devices  13.5 us (14%)
  waiting for transfers between devices  1.73 us (2%)
  local copies, waits for them, and re-layouts  1.38 us (1%)
  between operations  1.07 us (1%)
    all_to_all x3, blocking collectives, spread(): return lax.all_to_all(chunks, 'gx', split_axis=0, concat_axis=0, tiled=True)  39.5 us
    ppermute x8, starting transfers between devices, swap(): return lax.ppermute(value, 'gz', [(0, 1), (1, 0)])  9.78 us
    pallas_call x2, Pallas kernels, cells_forward(): pl.pallas_call(kernel, in_specs=[SCALAR] + [WHOLE] * (4 if first else 5),...  8.51 us
    pallas_call x1, Pallas kernels, weight_grad(): pl.pallas_call(kernel, grid_spec=pltpu.PrefetchScalarGridSpec(num_scalar_...  7.04 us
    pallas_call x2, Pallas kernels, cells_back(): pl.pallas_call(kernel, in_specs=[SCALAR, WHOLE, ANYWHERE, WHOLE, ANYWHERE...  6.29 us
    pallas_call x4, Pallas kernels, mode_product(): pl.pallas_call(kernel, in_specs=[SCALAR, WHOLE, WHOLE, WHOLE], out_specs=...  6.13 us
    all_to_all x1, starting transfers between devices, spread(): return lax.all_to_all(chunks, 'gx', split_axis=0, concat_axis=0, tiled=True)  3.75 us
    pallas_call x2, Pallas kernels, mix_partial(): pl.pallas_call(kernel, in_specs=[SCALAR] + [WHOLE] * (3 if first else 4),...  3.54 us
  transfers between devices with their start and end apart: 9, of which 1 were waited for; matrix products, arithmetic and copies ran while one was open for 1% of the time, Pallas kernels for 24%

profile of v4, /device:TPU:1, one launch (start us, length us, event | category | flops | bytes accessed | tf_op | source)
XLA Modules:
  0.0 98.9 jit_solution(15002710197887118197)
XLA Ops:
  0.6 2.9 %load_forward.1 = (bf16[1024,2048]{1,0:T(8,128)(2,1)S(1)}, bf16[384,384]{1,0:T(8,128)(2,1)S(1)}, bf16[2,320,640]{2,1,0:T(8,128)(2,1)S(1)}) custom-call(s32[1]{0:T(128)} %bitcast.me_ref._, bf16[2,320,2048]{2,1,0:T(8,128)(2,1)} %bitcast.16, bf16[384,2048]{1,0:T(8,128)(2,1)} %constant.16.clone.plane_ref.plane_in, bf16[20,20]{1,0:T(8,128)(2,1)} %mix_ref.3), custom_call_target="tpu_custom_call" | custom-call | flops 503316480 | bytes 5000000 | tf_op jit(solution)/shard_map/load_forward/pallas_call | solution.py:235
  3.7 2.6 %plane_forward.1 = (bf16[384,384]{1,0:T(8,128)(2,1)S(1)}, bf16[20,20,12,2,192]{4,3,2,1,0:T(2,128)(2,1)S(1)}) custom-call(s32[1]{0:T(128)} %bitcast.me_ref._, bf16[1024,2048]{1,0:T(8,128)(2,1)S(1)} %get-tuple-element.34.stack_ref, bf16[20,20,12,2,192]{4,3,2,1,0:T(2,128)(2,1)} %bitcast.15), custom_call_target="tpu_custom_call" | custom-call | flops 503316480 | bytes 3000000 | tf_op jit(solution)/shard_map/plane_forward/pallas_call | solution.py:271
  6.7 16.8 %all_to_all.20.in_ref = bf16[16,64,128]{2,1,0:T(8,128)(2,1)S(1)} all-to-all(bf16[16,64,128]{2,1,0:T(8,128)(2,1)S(1)} %z_forward.2), channel_id=1, replica_groups=mesh['grp'=1,'gx'=16,'gz'=2] {'gx'}, dimensions={0} | all-to-all | bytes 524288 | tf_op jit(solution)/shard_map/all_to_all | solution.py:793
  24.1 1.9 %collective-permute-start.1 = (bf16[10,2,12,192]{3,2,1,0:T(8,128)(2,1)S(1)}, bf16[10,2,12,192]{3,2,1,0:T(8,128)(2,1)S(1)}, u32[]{:S(2)}, u32[]{:S(2)}) collective-permute-start(bf16[10,2,12,192]{3,2,1,0:T(8,128)(2,1)S(1)} %get-tuple-element.39), channel_id=1, source_target_pairs={{0,1},{1,0},{2,3},{3,2},{4,5},{5,4},{6,7},{7,6},{8,9},{9,8},{10,11... | collective-permute-start | bytes 276488 | tf_op jit(solution)/shard_map/ppermute | solution.py:790
  26.0 1.3 %copy.15 = bf16[20,20,12,2,192]{4,2,1,0,3:T(8,128)(2,1)S(1)} copy(bf16[20,20,12,2,192]{4,3,2,1,0:T(2,128)(2,1)S(1)} %get-tuple-element.35) | data formatting | bytes 7372800 | tf_op jit(solution)/shard_map/plane_forward/pallas_call | solution.py:271
  27.3 1.5 %mode_product.5 = bf16[10,2,12,192]{3,2,1,0:T(8,128)(2,1)S(1)} custom-call(s32[1]{0:T(128)} %bitcast.me_ref._, bf16[2,20,20,12,192]{4,3,2,1,0:T(8,128)(2,1)S(1)} %bitcast.9, bf16[10,2,12,192]{3,2,1,0:T(8,128)(2,1)S(1)} %get-tuple-element.38.own_ref.fo_ref, bf16[10,2,12,192]{3,2,1,0:T(8,128)(2,1)S(1)} %collective-permute-done.1.got_ref.fg_ref), custom_call_target="tpu_custom_call" | custom-call | flops 2000000000 | bytes 4000000 | tf_op jit(solution)/shard_map/mode_product/pallas_call | solution.py:390
  29.0 1.5 %mode_product.4.own_ref = bf16[10,2,12,192]{3,2,1,0:T(8,128)(2,1)S(1)} custom-call(s32[1]{0:T(128)} %bitcast.me_ref._, bf16[2,20,20,12,192]{4,3,2,1,0:T(8,128)(2,1)S(1)} %bitcast.10, bf16[10,2,12,192]{3,2,1,0:T(8,128)(2,1)S(1)} %get-tuple-element.38.own_ref.fo_ref, bf16[10,2,12,192]{3,2,1,0:T(8,128)(2,1)S(1)} %collective-permute-done.1.got_ref.fg_ref), custom_call_target="tpu_custom_call" | custom-call | flops 2000000000 | bytes 4000000 | tf_op jit(solution)/shard_map/mode_product/pallas_call | solution.py:390
  31.1 11.4 %all_to_all.21.in_ref = bf16[16,64,128]{2,1,0:T(8,128)(2,1)S(1)} all-to-all(bf16[16,64,128]{2,1,0:T(8,128)(2,1)S(1)} %x_inverse.2), channel_id=1, replica_groups=mesh['grp'=1,'gx'=16,'gz'=2] {'gx'}, dimensions={0} | all-to-all | bytes 524288 | tf_op jit(solution)/shard_map/all_to_all | solution.py:793
  43.0 2.7 %collective-permute-start.3 = (bf16[320,384]{1,0:T(8,128)(2,1)S(1)}, bf16[320,384]{1,0:T(8,128)(2,1)S(1)}, u32[]{:S(2)}, u32[]{:S(2)}) collective-permute-start(bf16[320,384]{1,0:T(8,128)(2,1)S(1)} %get-tuple-element.43), channel_id=1, source_target_pairs={{0,1},{1,0},{2,3},{3,2},{4,5},{5,4},{6,7},{7,6},{8,9},{9,8},{10,11... | collective-permute-start | bytes 737288 | tf_op jit(solution)/shard_map/ppermute | solution.py:790
  45.7 4.2 %cells_forward_own.1 = (bf16[320,2048]{1,0:T(8,128)(2,1)S(1)}, bf16[384,384]{1,0:T(8,128)(2,1)S(1)}) custom-call(s32[1]{0:T(128)} %bitcast.me_ref._, bf16[320,384]{1,0:T(8,128)(2,1)S(1)} %get-tuple-element.40.modes_ref, bf16[2,320,640]{2,1,0:T(8,128)(2,1)S(1)} %get-tuple-element.41.mix_ref, bf16[1024,2048]{1,0:T(8,128)(2,1)S(1)} %get-tuple-element.34.stack_ref, ...), custom_call_target="tpu_custom_call" | custom-call | flops 3000000000 | bytes 5000000 | tf_op jit(solution)/shard_map/cells_forward_own/pallas_call | solution.py:596
  50.0 4.3 %cells_forward_got.1 = (bf16[2,320,2048]{2,1,0:T(8,128)(2,1)}, bf16[384,384]{1,0:T(8,128)(2,1)S(1)}, bf16[320,2048]{1,0:T(8,128)(2,1)S(1)}) custom-call(s32[1]{0:T(128)} %bitcast.me_ref._, bf16[320,384]{1,0:T(8,128)(2,1)S(1)} %collective-permute-done.3.modes_ref, bf16[2,320,640]{2,1,0:T(8,128)(2,1)S(1)} %get-tuple-element.41.mix_ref, ...), custom_call_target="tpu_custom_call" | custom-call | flops 3000000000 | bytes 5000000 | tf_op jit(solution)/shard_map/cells_forward_got/pallas_call | solution.py:596
  54.4 1.7 %mix_partial_own.1.rest_0_ = f32[20,10]{1,0:T(8,128)S(1)} custom-call(s32[1]{0:T(128)} %bitcast.me_ref._, bf16[640,20]{1,0:T(8,128)(2,1)S(1)} %copy-done.6, bf16[1024,2048]{1,0:T(8,128)(2,1)S(1)} %get-tuple-element.34.stack_ref, bf16[320,2048]{1,0:T(8,128)(2,1)S(1)} %get-tuple-element.44.rest_0_.grad_ref), custom_call_target="tpu_custom_call" | custom-call | flops 2000000000 | bytes 4000000 | tf_op jit(solution)/shard_map/mix_partial_own/pallas_call | solution.py:718
  56.4 11.3 %all_to_all.22.in_ref = bf16[16,64,128]{2,1,0:T(8,128)(2,1)S(1)} all-to-all(bf16[16,64,128]{2,1,0:T(8,128)(2,1)S(1)} %z_forward.3), channel_id=1, replica_groups=mesh['grp'=1,'gx'=16,'gz'=2] {'gx'}, dimensions={0} | all-to-all | bytes 524288 | tf_op jit(solution)/shard_map/all_to_all | solution.py:793
  68.3 2.7 %collective-permute-start.5 = (bf16[10,2,12,192]{3,2,1,0:T(8,128)(2,1)S(1)}, bf16[10,2,12,192]{3,2,1,0:T(8,128)(2,1)S(1)}, u32[]{:S(2)}, u32[]{:S(2)}) collective-permute-start(bf16[10,2,12,192]{3,2,1,0:T(8,128)(2,1)S(1)} %get-tuple-element.48), channel_id=1, source_target_pairs={{0,1},{1,0},{2,3},{3,2},{4,5},{5,4},{6,7},{7,6},{8,9},{9,8},{10,11... | collective-permute-start | bytes 276488 | tf_op jit(solution)/shard_map/ppermute | solution.py:790
  71.0 1.9 %mix_partial_got.1.rest_0_ = f32[4,128]{1,0:T(4,128)S(1)} custom-call(s32[1]{0:T(128)} %bitcast.me_ref._, bf16[640,20]{1,0:T(8,128)(2,1)S(1)} %copy-done.6, bf16[1024,2048]{1,0:T(8,128)(2,1)S(1)} %get-tuple-element.34.stack_ref, bf16[320,2048]{1,0:T(8,128)(2,1)S(1)} %get-tuple-element.49.grad_ref, f32[20,10]{1,0:T(8,128)S(1)} %mix_partial_own.1.rest_0_), custom_call_target="tpu_custom_call" | custom-call | flops 2000000000 | bytes 4000000 | tf_op jit(solution)/shard_map/mix_partial_got/pallas_call | solution.py:718
  72.8 1.5 %mode_product.7 = bf16[10,2,12,192]{3,2,1,0:T(8,128)(2,1)S(1)} custom-call(s32[1]{0:T(128)} %bitcast.me_ref._, bf16[2,20,20,12,192]{4,3,2,1,0:T(8,128)(2,1)S(1)} %bitcast.11, bf16[10,2,12,192]{3,2,1,0:T(8,128)(2,1)S(1)} %get-tuple-element.47.own_ref.go_ref, bf16[10,2,12,192]{3,2,1,0:T(8,128)(2,1)S(1)} %collective-permute-done.5.got_ref.gg_ref), custom_call_target="tpu_custom_call" | custom-call | flops 2000000000 | bytes 4000000 | tf_op jit(solution)/shard_map/mode_product/pallas_call | solution.py:390
  74.4 1.5 %mode_product.6.own_ref = bf16[10,2,12,192]{3,2,1,0:T(8,128)(2,1)S(1)} custom-call(s32[1]{0:T(128)} %bitcast.me_ref._, bf16[2,20,20,12,192]{4,3,2,1,0:T(8,128)(2,1)S(1)} %bitcast.12, bf16[10,2,12,192]{3,2,1,0:T(8,128)(2,1)S(1)} %get-tuple-element.47.own_ref.go_ref, bf16[10,2,12,192]{3,2,1,0:T(8,128)(2,1)S(1)} %collective-permute-done.5.got_ref.gg_ref), custom_call_target="tpu_custom_call" | custom-call | flops 2000000000 | bytes 4000000 | tf_op jit(solution)/shard_map/mode_product/pallas_call | solution.py:390
  76.0 1.3 %x_inverse.3 = bf16[16,64,128]{2,1,0:T(8,128)(2,1)} custom-call(s32[1]{0:T(128)} %bitcast.me_ref._, bf16[10,2,12,192]{3,2,1,0:T(8,128)(2,1)S(1)} %mode_product.6.own_ref, bf16[10,2,12,192]{3,2,1,0:T(8,128)(2,1)S(1)} %collective-permute-done.6.got_ref, bf16[2,2,192,1024]{3,2,1,0:T(8,128)(2,1)S(1)} %copy-done.1, f32[4,128]{1,0:T(4,128)S(1)} %mix_partial_got.1.rest_0_), custom_call_target="tpu_custom_call" | custom-call | flops 300000000 | bytes 3000000 | tf_op jit(solution)/shard_map/x_inverse/pallas_call | solution.py:437
  77.3 3.8 %all-to-all-start.3 = ((bf16[16,64,128]{2,1,0:T(8,128)(2,1)}), bf16[16,64,128]{2,1,0:T(8,128)(2,1)S(1)}, u32[]{:S(2)}, u32[]{:S(2)}) async-start(bf16[16,64,128]{2,1,0:T(8,128)(2,1)} %x_inverse.3), calls=%async_computation.3 | async-start | bytes 524288 | tf_op jit(solution)/shard_map/all_to_all | solution.py:793
  81.0 7.0 %weight_grad.1 = f32[20,20,12,2,192]{4,3,2,1,0:T(2,128)} custom-call(s32[1]{0:T(128)} %bitcast.me_ref._, bf16[10,2,12,192]{3,2,1,0:T(8,128)(2,1)S(1)} %get-tuple-element.38.own_ref.fo_ref, bf16[10,2,12,192]{3,2,1,0:T(8,128)(2,1)S(1)} %collective-permute-done.1.got_ref.fg_ref, bf16[10,2,12,192]{3,2,1,0:T(8,128)(2,1)S(1)} %get-tuple-element.47.own_ref.go_ref, ...), custom_call_target="tpu_custom_call" | custom-call | flops 8000000000 | bytes 13000000 | tf_op jit(solution)/shard_map/weight_grad/pallas_call | solution.py:765
  88.1 1.7 %all-to-all-done.3.in_ref = bf16[16,64,128]{2,1,0:T(8,128)(2,1)S(1)} async-done(((bf16[16,64,128]{2,1,0:T(8,128)(2,1)}), bf16[16,64,128]{2,1,0:T(8,128)(2,1)S(1)}, u32[]{:S(2)}, u32[]{:S(2)}) %all-to-all-start.3) | async-done | bytes 262176 | tf_op jit(solution)/shard_map/all_to_all | solution.py:793
  90.3 2.1 %collective-permute-start.7 = (bf16[336,384]{1,0:T(8,128)(2,1)S(1)}, bf16[336,384]{1,0:T(8,128)(2,1)S(1)}, u32[]{:S(2)}, u32[]{:S(2)}) collective-permute-start(bf16[336,384]{1,0:T(8,128)(2,1)S(1)} %get-tuple-element.54), channel_id=1, source_target_pairs={{0,1},{1,0},{2,3},{3,2},{4,5},{5,4},{6,7},{7,6},{8,9},{9,8},{10,11... | collective-permute-start | bytes 774152 | tf_op jit(solution)/shard_map/ppermute | solution.py:790
  92.4 3.4 %cells_back_own.1 = (bf16[320,2048]{1,0:T(8,128)(2,1)S(1)}, bf16[640,2048]{1,0:T(8,128)(2,1)S(1)}, bf16[384,2048]{1,0:T(8,128)(2,1)S(1)}, bf16[2,320,640]{2,1,0:T(8,128)(2,1)S(1)}) custom-call(s32[1]{0:T(128)} %bitcast.me_ref._, bf16[320,384]{1,0:T(8,128)(2,1)S(1)} %get-tuple-element.55.modes_ref, bf16[384,2048]{1,0:T(8,128)(2,1)} %constant.16.clone.plane_ref.plane_in, ...), custom_call_target="tpu_custom_call" | custom-call | flops 2000000000 | bytes 4000000 | tf_op jit(solution)/shard_map/cells_back_own/pallas_call | solution.py:668
  95.8 2.9 %cells_back_got.1 = (bf16[2,320,2048]{2,1,0:T(8,128)(2,1)}, f32[20,20]{1,0:T(8,128)}) custom-call(s32[1]{0:T(128)} %bitcast.me_ref._, bf16[336,384]{1,0:T(8,128)(2,1)S(1)} %collective-permute-done.7.modes_ref, bf16[384,2048]{1,0:T(8,128)(2,1)S(1)} %get-tuple-element.57.plane_in, bf16[2,320,640]{2,1,0:T(8,128)(2,1)S(1)} %get-tuple-element.58.mix_ref, ...), custom_call_target="tpu_custom_call" | custom-call | flops 2000000000 | bytes 4000000 | tf_op jit(solution)/shard_map/cells_back_got/pallas_call | solution.py:668
  (33 shorter events, 3.8 us)
Async XLA Ops:
  3.6 2.7 %collective-permute-start = (bf16[384,384]{1,0:T(8,128)(2,1)S(1)}, bf16[384,384]{1,0:T(8,128)(2,1)S(1)}, u32[]{:S(2)}, u32[]{:S(2)}) collective-permute-start(bf16[384,384]{1,0:T(8,128)(2,1)S(1)} %get-tuple-element.37), channel_id=1, source_target_pairs={{0,1},{1,0},{2,3},{3,2},{4,5},{5,4},{6,7},{7,6},{8,9},{9,8},{10,11... | collective-permute-start | bytes 884744 | tf_op jit(solution)/shard_map/ppermute | solution.py:790
  3.7 2.6 %copy-start.2 = (bf16[2,512,256]{2,1,0:T(8,128)(2,1)S(1)}, bf16[2,512,256]{2,1,0:T(8,128)(2,1)}, u32[]{:S(2)}) copy-start(bf16[2,512,256]{2,1,0:T(8,128)(2,1)} %constant.17.clone.table_ref) | copy-start | bytes 1572868
  3.7 19.8 %copy-start = (bf16[2,2,1024,192]{3,2,1,0:T(8,128)(2,1)S(1)}, bf16[2,2,1024,192]{3,2,1,0:T(8,128)(2,1)}, u32[]{:S(2)}) copy-start(bf16[2,2,1024,192]{3,2,1,0:T(8,128)(2,1)} %constant.19.clone.table_ref) | copy-start | bytes 4718596
  24.1 3.3 %collective-permute-start.1 = (bf16[10,2,12,192]{3,2,1,0:T(8,128)(2,1)S(1)}, bf16[10,2,12,192]{3,2,1,0:T(8,128)(2,1)S(1)}, u32[]{:S(2)}, u32[]{:S(2)}) collective-permute-start(bf16[10,2,12,192]{3,2,1,0:T(8,128)(2,1)S(1)} %get-tuple-element.39), channel_id=1, source_target_pairs={{0,1},{1,0},{2,3},{3,2},{4,5},{5,4},{6,7},{7,6},{8,9},{9,8},{10,11... | collective-permute-start | bytes 276488 | tf_op jit(solution)/shard_map/ppermute | solution.py:790
  28.9 1.7 %copy-start.1 = (bf16[2,2,192,1024]{3,2,1,0:T(8,128)(2,1)S(1)}, bf16[2,2,192,1024]{3,2,1,0:T(8,128)(2,1)}, u32[]{:S(2)}) copy-start(bf16[2,2,192,1024]{3,2,1,0:T(8,128)(2,1)} %constant.20.clone.table_ref) | copy-start | bytes 4718596
  28.9 1.7 %collective-permute-start.2 = (bf16[10,2,12,192]{3,2,1,0:T(8,128)(2,1)S(1)}, bf16[10,2,12,192]{3,2,1,0:T(8,128)(2,1)S(1)}, u32[]{:S(2)}, u32[]{:S(2)}) collective-permute-start(bf16[10,2,12,192]{3,2,1,0:T(8,128)(2,1)S(1)} %mode_product.5), channel_id=1, source_target_pairs={{0,1},{1,0},{2,3},{3,2},{4,5},{5,4},{6,7},{7,6},{8,9},{9,8},{10,11... | collective-permute-start | bytes 276488 | tf_op jit(solution)/shard_map/ppermute | solution.py:790
  29.0 13.5 %copy-start.5 = (bf16[2,512,256]{2,1,0:T(8,128)(2,1)S(1)}, bf16[2,512,256]{2,1,0:T(8,128)(2,1)}, u32[]{:S(2)}) copy-start(bf16[2,512,256]{2,1,0:T(8,128)(2,1)} %constant.18.clone.table_ref) | copy-start | bytes 1572868
  30.5 15.2 %copy-start.4 = (bf16[20,2,16,2048]{3,2,1,0:T(8,128)(2,1)S(1)}, bf16[20,2,16,2048]{3,2,1,0:T(8,128)(2,1)}, u32[]{:S(2)}) copy-start(bf16[20,2,16,2048]{3,2,1,0:T(8,128)(2,1)} %param.11) | copy-start | bytes 7864324
  43.0 6.9 %collective-permute-start.3 = (bf16[320,384]{1,0:T(8,128)(2,1)S(1)}, bf16[320,384]{1,0:T(8,128)(2,1)S(1)}, u32[]{:S(2)}, u32[]{:S(2)}) collective-permute-start(bf16[320,384]{1,0:T(8,128)(2,1)S(1)} %get-tuple-element.43), channel_id=1, source_target_pairs={{0,1},{1,0},{2,3},{3,2},{4,5},{5,4},{6,7},{7,6},{8,9},{9,8},{10,11... | collective-permute-start | bytes 737288 | tf_op jit(solution)/shard_map/ppermute | solution.py:790
  50.0 4.4 %copy-start.6 = (bf16[640,20]{1,0:T(8,128)(2,1)S(1)}, bf16[640,20]{1,0:T(8,128)(2,1)}, u32[]{:S(2)}) copy-start(bf16[640,20]{1,0:T(8,128)(2,1)} %constant.21.clone.owner_ref) | copy-start | bytes 76804
  54.3 1.8 %collective-permute-start.4 = (bf16[384,384]{1,0:T(8,128)(2,1)S(1)}, bf16[384,384]{1,0:T(8,128)(2,1)S(1)}, u32[]{:S(2)}, u32[]{:S(2)}) collective-permute-start(bf16[384,384]{1,0:T(8,128)(2,1)S(1)} %get-tuple-element.45), channel_id=1, source_target_pairs={{0,1},{1,0},{2,3},{3,2},{4,5},{5,4},{6,7},{7,6},{8,9},{9,8},{10,11... | collective-permute-start | bytes 884744 | tf_op jit(solution)/shard_map/ppermute | solution.py:790
  68.3 4.6 %collective-permute-start.5 = (bf16[10,2,12,192]{3,2,1,0:T(8,128)(2,1)S(1)}, bf16[10,2,12,192]{3,2,1,0:T(8,128)(2,1)S(1)}, u32[]{:S(2)}, u32[]{:S(2)}) collective-permute-start(bf16[10,2,12,192]{3,2,1,0:T(8,128)(2,1)S(1)} %get-tuple-element.48), channel_id=1, source_target_pairs={{0,1},{1,0},{2,3},{3,2},{4,5},{5,4},{6,7},{7,6},{8,9},{9,8},{10,11... | collective-permute-start | bytes 276488 | tf_op jit(solution)/shard_map/ppermute | solution.py:790
  74.4 1.6 %collective-permute-start.6 = (bf16[10,2,12,192]{3,2,1,0:T(8,128)(2,1)S(1)}, bf16[10,2,12,192]{3,2,1,0:T(8,128)(2,1)S(1)}, u32[]{:S(2)}, u32[]{:S(2)}) collective-permute-start(bf16[10,2,12,192]{3,2,1,0:T(8,128)(2,1)S(1)} %mode_product.7), channel_id=1, source_target_pairs={{0,1},{1,0},{2,3},{3,2},{4,5},{5,4},{6,7},{7,6},{8,9},{9,8},{10,11... | collective-permute-start | bytes 276488 | tf_op jit(solution)/shard_map/ppermute | solution.py:790
  77.3 12.5 %all-to-all-start.3 = ((bf16[16,64,128]{2,1,0:T(8,128)(2,1)}), bf16[16,64,128]{2,1,0:T(8,128)(2,1)S(1)}, u32[]{:S(2)}, u32[]{:S(2)}) async-start(bf16[16,64,128]{2,1,0:T(8,128)(2,1)} %x_inverse.3), calls=%async_computation.3 | async-start | bytes 524288 | tf_op jit(solution)/shard_map/all_to_all | solution.py:793
  81.0 11.4 %copy-start.3 = (bf16[20,20]{1,0:T(8,128)(2,1)S(1)}, bf16[20,20]{1,0:T(8,128)(2,1)}, u32[]{:S(2)}) copy-start(bf16[20,20]{1,0:T(8,128)(2,1)} %mix_ref.3) | copy-start | bytes 2404
  90.3 5.5 %collective-permute-start.7 = (bf16[336,384]{1,0:T(8,128)(2,1)S(1)}, bf16[336,384]{1,0:T(8,128)(2,1)S(1)}, u32[]{:S(2)}, u32[]{:S(2)}) collective-permute-start(bf16[336,384]{1,0:T(8,128)(2,1)S(1)} %get-tuple-element.54), channel_id=1, source_target_pairs={{0,1},{1,0},{2,3},{3,2},{4,5},{5,4},{6,7},{7,6},{8,9},{9,8},{10,11... | collective-permute-start | bytes 774152 | tf_op jit(solution)/shard_map/ppermute | solution.py:790
